TPU v7x, 512 devices: a whole 4x4x16 slice. The times are simulated.
512 devices in a mesh: dp: 8 (over x, core), ctx: 64 (over y, z).
Axes of the slice: x: 4, y: 4, z: 16, core: 2. Of those that a mesh axis runs over, the one named last changes fastest.
Arguments:
- queries: bfloat16 [131072, 2048], P(('dp', 'ctx')), may hold values from -5 to 5
- keys: bfloat16 [131072, 512], P(('dp', 'ctx')), may hold values from -5 to 5
- values: bfloat16 [131072, 512], P(('dp', 'ctx')), may hold values from -5 to 5
- grad_out: bfloat16 [131072, 2048], P(('dp', 'ctx')), may hold values from -5 to 5
- doc_lengths: int32 [341], replicated, may hold values from 1 to 768, 131072 in all
Outputs:
- grad_queries: bfloat16 [131072, 2048], P(('dp', 'ctx'))
- grad_keys: bfloat16 [131072, 512], P(('dp', 'ctx'))
- grad_values: bfloat16 [131072, 512], P(('dp', 'ctx'))
Inputs may be any that keep to these rules, and one draw needn't show every extreme that they name: `doc_lengths`: they sum to 131072; the longest is exactly 768.
All inputs are finite; a program needn't handle non-finite values.
Results may differ from a plain program's by a relative error of at most 0.024.
Values may be sent and summed in bfloat16 or wider, within the bound.
No kernel may reach another device: no remote copies, remote signals or barrier semaphores. Data moves between devices by JAX's collectives and lax.ppermute only.
A program may use at most 64 MiB of HBM per device.

v0:
```python
import jax
import jax.numpy as jnp
from jax import lax
from jax.sharding import PartitionSpec as P

HEADS = 16
KV_HEADS = 4
HEAD_DIM = 128
REACH = 3


def passed_along(block, axis, distance):
    devices = range(lax.axis_size(axis))
    route = [(i - distance, i) for i in devices if i - distance in devices]
    return lax.ppermute(block, axis, route)


def doc_mask(ends, q_pos, k_pos):
    q_doc = jnp.sum((ends[None, :] <= q_pos[:, None]).astype(jnp.int32), axis=1)
    k_doc = jnp.sum((ends[None, :] <= k_pos[:, None]).astype(jnp.int32), axis=1)
    return (
        (q_doc[:, None] == k_doc[None, :])
        & (k_pos[None, :] <= q_pos[:, None])
        & (k_pos[None, :] >= 0)
    )


def group_terms(q_group, k_group, v_group, g_group, allowed, scale):
    scores = jnp.einsum("tgd,kd->gtk", q_group, k_group, preferred_element_type=jnp.float32) * scale
    masked = jnp.where(allowed[None], scores, -1e30)
    top = jnp.max(masked, axis=2, keepdims=True)
    expo = jnp.where(allowed[None], jnp.exp(masked - top), 0.0)
    probs = expo / jnp.sum(expo, axis=2, keepdims=True)
    probs_b = probs.astype(jnp.bfloat16)
    attn = jnp.einsum("gtk,kd->tgd", probs_b, v_group, preferred_element_type=jnp.float32).astype(
        jnp.bfloat16
    )
    delta = jnp.einsum("tgd,tgd->gt", g_group, attn, preferred_element_type=jnp.float32)
    dprobs = jnp.einsum("tgd,kd->gtk", g_group, v_group, preferred_element_type=jnp.float32)
    dscores = (probs * (dprobs - delta[:, :, None])).astype(jnp.bfloat16)
    grad_q = (
        jnp.einsum("gtk,kd->tgd", dscores, k_group, preferred_element_type=jnp.float32) * scale
    ).astype(jnp.bfloat16)
    grad_k = jnp.einsum("gtk,tgd->kd", dscores, q_group, preferred_element_type=jnp.float32) * scale
    grad_v = jnp.einsum("gtk,tgd->kd", probs_b, g_group, preferred_element_type=jnp.float32)
    return (grad_q, grad_k, grad_v)


def block_terms(q_block, window, g_block, allowed):
    tok = q_block.shape[0]
    width = window.shape[0]
    groups = HEADS // KV_HEADS
    kv_width = KV_HEADS * HEAD_DIM
    scale = HEAD_DIM ** (-0.5)
    q_split = q_block.reshape(tok, KV_HEADS, groups, HEAD_DIM).transpose(1, 0, 2, 3)
    g_split = g_block.reshape(tok, KV_HEADS, groups, HEAD_DIM).transpose(1, 0, 2, 3)
    k_split = window[:, :kv_width].reshape(width, KV_HEADS, HEAD_DIM).transpose(1, 0, 2)
    v_split = window[:, kv_width:].reshape(width, KV_HEADS, HEAD_DIM).transpose(1, 0, 2)
    grad_q, grad_k, grad_v = lax.map(
        lambda xs: group_terms(xs[0], xs[1], xs[2], xs[3], allowed, scale),
        (q_split, k_split, v_split, g_split),
    )
    grad_q = grad_q.transpose(1, 0, 2, 3).reshape(tok, HEADS * HEAD_DIM)
    grad_k = grad_k.transpose(1, 0, 2).reshape(width, kv_width)
    grad_v = grad_v.transpose(1, 0, 2).reshape(width, kv_width)
    return (grad_q, jnp.concatenate([grad_k, grad_v], axis=1))


def on_device(queries, keys, values, grad_out, doc_lengths):
    tok = queries.shape[0]
    kv_width = KV_HEADS * HEAD_DIM
    width = (REACH + 1) * tok
    block = lax.axis_index(("dp", "ctx"))
    start = block * tok
    packed = jnp.concatenate([keys, values], axis=1)
    pieces = [passed_along(packed, ("dp", "ctx"), distance) for distance in range(REACH, 0, -1)]
    window = jnp.concatenate(pieces + [packed], axis=0)
    ends = jnp.cumsum(doc_lengths)
    q_pos = start + jnp.arange(tok, dtype=jnp.int32)
    k_pos = start - REACH * tok + jnp.arange(width, dtype=jnp.int32)
    allowed = doc_mask(ends, q_pos, k_pos)
    grad_queries, partial_value = block_terms(queries, window, grad_out, allowed)
    total = partial_value[REACH * tok :]
    for distance in range(1, REACH + 1):
        piece = partial_value[(REACH - distance) * tok : (REACH - distance + 1) * tok]
        total = total + passed_along(piece, ("dp", "ctx"), -distance)
    grad_keys = total[:, :kv_width].astype(jnp.bfloat16)
    grad_values = total[:, kv_width:].astype(jnp.bfloat16)
    return (grad_queries, grad_keys, grad_values)


def solution(mesh):
    return jax.shard_map(
        on_device,
        mesh=mesh,
        in_specs=(
            P(("dp", "ctx"), None),
            P(("dp", "ctx"), None),
            P(("dp", "ctx"), None),
            P(("dp", "ctx"), None),
            P(),
        ),
        out_specs=(P(("dp", "ctx"), None), P(("dp", "ctx"), None), P(("dp", "ctx"), None)),
        check_vma=False,
    )
```

profile of v0, /device:TPU:6, one launch (start us, length us, event | category | flops | bytes accessed | tf_op | source)
XLA Modules:
  0.0 319.9 jit_solution(16077295724140404511)
XLA Ops:
  3.0 6.5 %collective-permute-start = (bf16[256,1024]{0,1:T(8,128)(2,1)S(1)}, bf16[256,1024]{0,1:T(8,128)(2,1)}, u32[]{:S(2)}, u32[]{:S(2)}) collective-permute-start(bf16[256,1024]{0,1:T(8,128)(2,1)S(1)} %pad_maximum_fusion), channel_id=1, source_target_pairs={{0,3},{1,4},{2,5},{3,6},{4,7},{5,8},{6,9},{7,10},{8,11},{9,12},{10... | collective-permute-start | bytes 1572872 | tf_op jit(solution)/shard_map/ppermute | solution.py:15
  9.6 6.4 %collective-permute-start.1 = (bf16[256,1024]{0,1:T(8,128)(2,1)S(1)}, bf16[256,1024]{0,1:T(8,128)(2,1)}, u32[]{:S(2)}, u32[]{:S(2)}) collective-permute-start(bf16[256,1024]{0,1:T(8,128)(2,1)S(1)} %pad_maximum_fusion), channel_id=1, source_target_pairs={{0,2},{1,3},{2,4},{3,5},{4,6},{5,7},{6,8},{7,9},{8,10},{9,11},{10,... | collective-permute-start | bytes 1572872 | tf_op jit(solution)/shard_map/ppermute | solution.py:15
  16.0 3.8 %collective-permute-start.2 = (bf16[256,1024]{0,1:T(8,128)(2,1)S(1)}, bf16[256,1024]{0,1:T(8,128)(2,1)}, u32[]{:S(2)}, u32[]{:S(2)}) collective-permute-start(bf16[256,1024]{0,1:T(8,128)(2,1)S(1)} %pad_maximum_fusion), channel_id=1, source_target_pairs={{0,1},{1,2},{2,3},{3,4},{4,5},{5,6},{6,7},{7,8},{8,9},{9,10},{10,1... | collective-permute-start | bytes 1572872 | tf_op jit(solution)/shard_map/ppermute | solution.py:15
  23.6 25.0 %collective-permute-done = bf16[256,1024]{0,1:T(8,128)(2,1)} collective-permute-done((bf16[256,1024]{0,1:T(8,128)(2,1)S(1)}, bf16[256,1024]{0,1:T(8,128)(2,1)}, u32[]{:S(2)}, u32[]{:S(2)}) %collective-permute-start) | collective-permute-done | bytes 524320 | tf_op jit(solution)/shard_map/ppermute | solution.py:15
  48.5 18.4 %collective-permute-done.1 = bf16[256,1024]{0,1:T(8,128)(2,1)} collective-permute-done((bf16[256,1024]{0,1:T(8,128)(2,1)S(1)}, bf16[256,1024]{0,1:T(8,128)(2,1)}, u32[]{:S(2)}, u32[]{:S(2)}) %collective-permute-start.1) | collective-permute-done | bytes 524320 | tf_op jit(solution)/shard_map/ppermute | solution.py:15
  67.0 18.1 %collective-permute-done.2 = bf16[256,1024]{0,1:T(8,128)(2,1)} collective-permute-done((bf16[256,1024]{0,1:T(8,128)(2,1)S(1)}, bf16[256,1024]{0,1:T(8,128)(2,1)}, u32[]{:S(2)}, u32[]{:S(2)}) %collective-permute-start.2) | collective-permute-done | bytes 524320 | tf_op jit(solution)/shard_map/ppermute | solution.py:15
  85.0 7.8 %maximum_maximum_fusion = bf16[1024,1024]{0,1:T(8,128)(2,1)S(1)} fusion(bf16[256,512]{0,1:T(8,128)(2,1)S(1)} %copy.31, bf16[256,512]{0,1:T(8,128)(2,1)S(1)} %copy.30, bf16[256,1024]{0,1:T(8,128)(2,1)} %collective-permute-done.2, bf16[256,1024]{0,1:T(8,128)(2,1)} %collective-permute-done.1, bf16[256,1024]{0,1:T(8,128)(2,1)} %collective-permute-done), kind=kLoop, calls=%fused_computation.61 | loop fusion | flops 10485760 | bytes 4194304 | tf_op jit(solution)/shard_map/concatenate | solution.py:77
  92.8 1.5 fusion.75
  94.2 81.5 %while.15 = (s32[]{:T(128)}, bf16[4,256,4,128]{1,3,2,0:T(8,128)(2,1)}, f32[4,1024,128]{2,1,0:T(8,128)}, f32[4,1024,128]{2,1,0:T(8,128)}, bf16[4,1024,128]{1,2,0:...) while((s32[]{:T(128)}, ...), condition=%wide.region_7.8_spmd.clone, body=%wide.region_4.7_spmd.clone.sunk | while | flops 1624244224 | bytes 36999844 | solution.py:59
  95.1 4.9 %fusion.114 = (f32[4,256]{1,0:T(4,128)S(1)}, f32[4,256,1024]{1,2,0:T(8,128)}) fusion(pred[256,1024]{0,1:T(8,128)(4,1)S(1)} %and_and_fusion.2, bf16[4,256,4,128]{1,3,2,0:T(8,128)(2,1)} %get-tuple-element.265, s32[]{:T(128)} %get-tuple-element.246, bf16[4,1024,128]{1,2,0:T(8,128)(2,1)} %get-tuple-element.264), kind=kOutput, calls=%fused_computation.75.clone.1 | convolution fusion | flops 273679360 | bytes 5248000 | tf_op jit(solution)/shard_map/while/body/eval_jaxpr/sub | solution.py:32
  100.0 2.5 fusion.115
  104.0 1.5 fusion.116
  105.5 3.0 fusion.117
  108.5 2.5 fusion.119
  111.0 2.1 fusion.118
  113.1 1.5 fusion.120
  115.5 4.9 %fusion.114 = (f32[4,256]{1,0:T(4,128)S(1)}, f32[4,256,1024]{1,2,0:T(8,128)}) fusion(pred[256,1024]{0,1:T(8,128)(4,1)S(1)} %and_and_fusion.2, bf16[4,256,4,128]{1,3,2,0:T(8,128)(2,1)} %get-tuple-element.265, s32[]{:T(128)} %get-tuple-element.246, bf16[4,1024,128]{1,2,0:T(8,128)(2,1)} %get-tuple-element.264), kind=kOutput, calls=%fused_computation.75.clone.1 | convolution fusion | flops 273679360 | bytes 5248000 | tf_op jit(solution)/shard_map/while/body/eval_jaxpr/sub | solution.py:32
  120.4 2.5 fusion.115
  124.3 1.5 fusion.116
  125.8 3.0 fusion.117
  128.9 2.5 fusion.119
  131.4 2.1 fusion.118
  133.5 1.5 fusion.120
  135.9 4.9 %fusion.114 = (f32[4,256]{1,0:T(4,128)S(1)}, f32[4,256,1024]{1,2,0:T(8,128)}) fusion(pred[256,1024]{0,1:T(8,128)(4,1)S(1)} %and_and_fusion.2, bf16[4,256,4,128]{1,3,2,0:T(8,128)(2,1)} %get-tuple-element.265, s32[]{:T(128)} %get-tuple-element.246, bf16[4,1024,128]{1,2,0:T(8,128)(2,1)} %get-tuple-element.264), kind=kOutput, calls=%fused_computation.75.clone.1 | convolution fusion | flops 273679360 | bytes 5248000 | tf_op jit(solution)/shard_map/while/body/eval_jaxpr/sub | solution.py:32
  140.8 2.5 fusion.115
  144.7 1.5 fusion.116
  146.2 3.0 fusion.117
  149.3 2.5 fusion.119
  151.7 2.1 fusion.118
  153.8 1.5 fusion.120
  156.2 4.9 %fusion.114 = (f32[4,256]{1,0:T(4,128)S(1)}, f32[4,256,1024]{1,2,0:T(8,128)}) fusion(pred[256,1024]{0,1:T(8,128)(4,1)S(1)} %and_and_fusion.2, bf16[4,256,4,128]{1,3,2,0:T(8,128)(2,1)} %get-tuple-element.265, s32[]{:T(128)} %get-tuple-element.246, bf16[4,1024,128]{1,2,0:T(8,128)(2,1)} %get-tuple-element.264), kind=kOutput, calls=%fused_computation.75.clone.1 | convolution fusion | flops 273679360 | bytes 5248000 | tf_op jit(solution)/shard_map/while/body/eval_jaxpr/sub | solution.py:32
  161.1 2.5 fusion.115
  165.1 1.5 fusion.116
  166.6 3.0 fusion.117
  169.6 2.5 fusion.119
  172.1 2.1 fusion.118
  174.2 1.5 fusion.120
  175.7 1.9 bitcast_dynamic-update-slice_fusion.1
  177.6 1.9 bitcast_dynamic-update-slice_fusion
  179.5 1.5 fusion.74
  182.0 2.8 collective-permute-start.3
  184.8 4.3 %collective-permute-start.4 = (f32[256,1024]{1,0:T(8,128)}, f32[256,1024]{1,0:T(8,128)}, u32[]{:S(2)}, u32[]{:S(2)}) collective-permute-start(f32[256,1024]{1,0:T(8,128)} %get-tuple-element.144), channel_id=1, source_target_pairs={{2,0},{3,1},{4,2},{5,3},{6,4},{7,5},{8,6},{9,7},{10,8},{11,9},{12,... | collective-permute-start | bytes 3145736 | tf_op jit(solution)/shard_map/ppermute | solution.py:15
  189.2 5.1 %collective-permute-start.5 = (f32[256,1024]{1,0:T(8,128)S(1)}, f32[256,1024]{1,0:T(8,128)}, u32[]{:S(2)}, u32[]{:S(2)}) collective-permute-start(f32[256,1024]{1,0:T(8,128)S(1)} %get-tuple-element.143), channel_id=1, source_target_pairs={{3,0},{4,1},{5,2},{6,3},{7,4},{8,5},{9,6},{10,7},{11,8},{12,9},{13... | collective-permute-start | bytes 3145736 | tf_op jit(solution)/shard_map/ppermute | solution.py:15
  194.3 1.4 copy.51
  195.7 20.7 %collective-permute-done.3 = f32[256,1024]{1,0:T(8,128)S(1)} collective-permute-done((f32[256,1024]{1,0:T(8,128)}, f32[256,1024]{1,0:T(8,128)S(1)}, u32[]{:S(2)}, u32[]{:S(2)}) %collective-permute-start.3) | collective-permute-done | bytes 1048608 | tf_op jit(solution)/shard_map/ppermute | solution.py:15
  216.4 43.1 %collective-permute-done.4 = f32[256,1024]{1,0:T(8,128)} collective-permute-done((f32[256,1024]{1,0:T(8,128)}, f32[256,1024]{1,0:T(8,128)}, u32[]{:S(2)}, u32[]{:S(2)}) %collective-permute-start.4) | collective-permute-done | bytes 1048608 | tf_op jit(solution)/shard_map/ppermute | solution.py:15
  259.6 57.3 %collective-permute-done.5 = f32[256,1024]{1,0:T(8,128)} collective-permute-done((f32[256,1024]{1,0:T(8,128)S(1)}, f32[256,1024]{1,0:T(8,128)}, u32[]{:S(2)}, u32[]{:S(2)}) %collective-permute-start.5) | collective-permute-done | bytes 1048608 | tf_op jit(solution)/shard_map/ppermute | solution.py:15
  316.9 2.2 fusion.64
  (58 shorter events, 16.9 us)
Async XLA Ops:
  0.6 19.2 %copy-start.5 = (s32[341]{0:T(512)S(1)}, s32[341]{0:T(512)}, u32[]{:S(2)}) copy-start(s32[341]{0:T(512)} %param.11) | copy-start | bytes 4096
  0.6 19.8 %copy-start.2 = (bf16[256,2048]{1,0:T(8,128)(2,1)S(1)}, bf16[256,2048]{1,0:T(8,128)(2,1)}, u32[]{:S(2)}) copy-start(bf16[256,2048]{1,0:T(8,128)(2,1)} %param.7) | copy-start | bytes 3145732
  0.7 21.2 %copy-start.3 = (bf16[256,2048]{1,0:T(8,128)(2,1)S(1)}, bf16[256,2048]{1,0:T(8,128)(2,1)}, u32[]{:S(2)}) copy-start(bf16[256,2048]{1,0:T(8,128)(2,1)} %param.10) | copy-start | bytes 3145732
  3.0 45.5 %collective-permute-start = (bf16[256,1024]{0,1:T(8,128)(2,1)S(1)}, bf16[256,1024]{0,1:T(8,128)(2,1)}, u32[]{:S(2)}, u32[]{:S(2)}) collective-permute-start(bf16[256,1024]{0,1:T(8,128)(2,1)S(1)} %pad_maximum_fusion), channel_id=1, source_target_pairs={{0,3},{1,4},{2,5},{3,6},{4,7},{5,8},{6,9},{7,10},{8,11},{9,12},{10... | collective-permute-start | bytes 1572872 | tf_op jit(solution)/shard_map/ppermute | solution.py:15
  9.6 57.4 %collective-permute-start.1 = (bf16[256,1024]{0,1:T(8,128)(2,1)S(1)}, bf16[256,1024]{0,1:T(8,128)(2,1)}, u32[]{:S(2)}, u32[]{:S(2)}) collective-permute-start(bf16[256,1024]{0,1:T(8,128)(2,1)S(1)} %pad_maximum_fusion), channel_id=1, source_target_pairs={{0,2},{1,3},{2,4},{3,5},{4,6},{5,7},{6,8},{7,9},{8,10},{9,11},{10,... | collective-permute-start | bytes 1572872 | tf_op jit(solution)/shard_map/ppermute | solution.py:15
  16.0 69.0 %collective-permute-start.2 = (bf16[256,1024]{0,1:T(8,128)(2,1)S(1)}, bf16[256,1024]{0,1:T(8,128)(2,1)}, u32[]{:S(2)}, u32[]{:S(2)}) collective-permute-start(bf16[256,1024]{0,1:T(8,128)(2,1)S(1)} %pad_maximum_fusion), channel_id=1, source_target_pairs={{0,1},{1,2},{2,3},{3,4},{4,5},{5,6},{6,7},{7,8},{8,9},{9,10},{10,1... | collective-permute-start | bytes 1572872 | tf_op jit(solution)/shard_map/ppermute | solution.py:15
  104.0 1.5 copy-start
  124.3 1.5 copy-start
  144.7 1.5 copy-start
  165.0 1.5 copy-start
  179.5 2.6 copy-start.1
  179.5 14.8 %copy-start.4 = (bf16[4,256,4,128]{1,3,2,0:T(8,128)(2,1)S(1)}, bf16[4,256,4,128]{1,3,2,0:T(8,128)(2,1)}, u32[]{:S(2)}) copy-start(bf16[4,256,4,128]{1,3,2,0:T(8,128)(2,1)} %get-tuple-element.52) | copy-start | bytes 3145732
  182.0 34.4 %collective-permute-start.3 = (f32[256,1024]{1,0:T(8,128)}, f32[256,1024]{1,0:T(8,128)S(1)}, u32[]{:S(2)}, u32[]{:S(2)}) collective-permute-start(f32[256,1024]{1,0:T(8,128)} %get-tuple-element.142), channel_id=1, source_target_pairs={{1,0},{2,1},{3,2},{4,3},{5,4},{6,5},{7,6},{8,7},{9,8},{10,9},{11,1... | collective-permute-start | bytes 3145736 | tf_op jit(solution)/shard_map/ppermute | solution.py:15
  184.8 74.8 %collective-permute-start.4 = (f32[256,1024]{1,0:T(8,128)}, f32[256,1024]{1,0:T(8,128)}, u32[]{:S(2)}, u32[]{:S(2)}) collective-permute-start(f32[256,1024]{1,0:T(8,128)} %get-tuple-element.144), channel_id=1, source_target_pairs={{2,0},{3,1},{4,2},{5,3},{6,4},{7,5},{8,6},{9,7},{10,8},{11,9},{12,... | collective-permute-start | bytes 3145736 | tf_op jit(solution)/shard_map/ppermute | solution.py:15
  189.2 127.8 %collective-permute-start.5 = (f32[256,1024]{1,0:T(8,128)S(1)}, f32[256,1024]{1,0:T(8,128)}, u32[]{:S(2)}, u32[]{:S(2)}) collective-permute-start(f32[256,1024]{1,0:T(8,128)S(1)} %get-tuple-element.143), channel_id=1, source_target_pairs={{3,0},{4,1},{5,2},{6,3},{7,4},{8,5},{9,6},{10,7},{11,8},{12,9},{13... | collective-permute-start | bytes 3145736 | tf_op jit(solution)/shard_map/ppermute | solution.py:15
where the time goes:
time: 323 us; the launch traced here: 320 us
  waiting for transfers between devices  183 us (57%)
  matrix products  62 us (19%)
  starting transfers between devices  28.9 us (9%)
  other arithmetic  24.6 us (8%)
  local copies, waits for them, and re-layouts  20.6 us (6%)
    ppermute x6, waiting for transfers between devices, passed_along(): return lax.ppermute(block, axis, route)  183 us
    ppermute x6, starting transfers between devices, passed_along(): return lax.ppermute(block, axis, route)  28.9 us
    sub x4, matrix products, group_terms(): expo = jnp.where(allowed[None], jnp.exp(masked - top), 0.0)  19.5 us
    dot_general x4, matrix products, group_terms(): jnp.einsum('tgd,kd->gtk', g_group, v_group, preferred_element_type=jnp.fl...  12.1 us
    convert_element_type x4, other arithmetic, group_terms(): probs_b = probs.astype(jnp.bfloat16)  10.1 us
    dot_general x4, matrix products, group_terms(): jnp.einsum('gtk,tgd->kd', dscores, q_group, preferred_element_type=jnp.fl...  9.89 us
    dot_general x4, matrix products, group_terms(): jnp.einsum('gtk,kd->tgd', dscores, k_group, preferred_element_type=jnp.fl...  8.45 us
    unnamed x15, local copies, waits for them, and re-layouts  7.91 us
  transfers between devices with their start and end apart: 6, of which 6 were waited for; matrix products, arithmetic and copies ran while one was open for 2% of the time, Pallas kernels for 0%

commit v1 on v0

v1 whole, which is shorter than its diff:
```python
import functools
import jax, jax.numpy as jnp
from jax import lax
from jax.sharding import PartitionSpec as P
from jax.experimental import pallas as pl
from jax.experimental.pallas import tpu as pltpu
HEAD_DIM=128; REACH=3; TOK=256; HALF=128; GROUP=4
LANES=GROUP*HALF
SCALE=HEAD_DIM**-0.5
LOG2E=1.4426950408889634
NEG=-1e30
F32=jnp.float32; BF=jnp.bfloat16
def nt(a,b): return lax.dot_general(a,b,(((1,),(1,)),((),())),preferred_element_type=F32)
def nn(a,b): return lax.dot_general(a,b,(((1,),(0,)),((),())),preferred_element_type=F32)
def fold(x,op):
    r=x[:8]
    for i in range(1,x.shape[0]//8): r=op(r,x[i*8:(i+1)*8])
    return r
def rows_of(d,hf):
    if d==0 and hf==0: return 0,128
    if d==3 and hf==1: return 128,256
    return 0,256
def kernel(before_ref,start_ref,q_ref,g_ref,kv0,kv1,kv2,kv3,gq_ref,o0,o1,o2,o3,q4,g4,s_ref,dp_ref,m_ref,l_ref,e_ref,acc_ref):
    kv=(kv0,kv1,kv2,kv3); outs=(o0,o1,o2,o3)
    before=before_ref[0]
    for hf in range(2):
        for h in range(GROUP):
            r=slice(hf*LANES+h*HALF,hf*LANES+(h+1)*HALF)
            q4[r,:]=q_ref[hf*HALF:(hf+1)*HALF,h*128:(h+1)*128]
            g4[r,:]=g_ref[hf*HALF:(hf+1)*HALF,h*128:(h+1)*128]
    def lanes(hf): return slice(hf*LANES,(hf+1)*LANES)
    def gate(d,f):
        if d==0: f()
        else: pl.when(before>(d-1)*TOK)(f)
    def pass1(d):
        for hf in range(2):
            a,b=rows_of(d,hf); ln=lanes(hf)
            s=nt(kv[d][a:b,:128],q4[ln,:])
            st=start_ref[:,hf*HALF:(hf+1)*HALF]
            kpos=lax.broadcasted_iota(jnp.int32,(b-a,HALF),0)+(a-d*TOK)
            ok=kpos>=st
            if d==0: ok=ok&(kpos<=lax.broadcasted_iota(jnp.int32,(b-a,HALF),1)+hf*HALF)
            s=jnp.concatenate([jnp.where(ok,s[:,h*HALF:(h+1)*HALF],NEG) for h in range(GROUP)],axis=1)
            s_ref[d,a:b,ln]=s
            mx=fold(s,jnp.maximum)
            m_ref[:,ln]=mx if d==0 else jnp.maximum(m_ref[:,ln],mx)
    for d in range(4): gate(d,functools.partial(pass1,d))
    m_ref[...]=jnp.broadcast_to(jnp.max(m_ref[...],axis=0,keepdims=True),m_ref.shape)
    def pass2(d):
        for hf in range(2):
            a,b=rows_of(d,hf); ln=lanes(hf)
            p=jnp.exp2((s_ref[d,a:b,ln]-m_ref[:1,ln])*(SCALE*LOG2E))
            dp=nt(kv[d][a:b,128:],g4[ln,:])
            s_ref[d,a:b,ln]=p
            dp_ref[d,a:b,ln]=dp
            ls=fold(p,jnp.add); es=fold(p*dp,jnp.add)
            l_ref[:,ln]=ls if d==0 else l_ref[:,ln]+ls
            e_ref[:,ln]=es if d==0 else e_ref[:,ln]+es
    for d in range(4): gate(d,functools.partial(pass2,d))
    il=1.0/jnp.sum(l_ref[...],axis=0,keepdims=True)
    l_ref[...]=jnp.broadcast_to(il,l_ref.shape)
    e_ref[...]=jnp.broadcast_to(jnp.sum(e_ref[...],axis=0,keepdims=True)*il,e_ref.shape)
    def pass3(d):
        dk=[];dv=[]
        for hf in range(2):
            a,b=rows_of(d,hf); ln=lanes(hf)
            pr=s_ref[d,a:b,ln]*l_ref[:1,ln]
            ds=(pr*(dp_ref[d,a:b,ln]-e_ref[:1,ln])).astype(BF)
            pb=pr.astype(BF)
            x=nn(ds,q4[ln,:])*SCALE; y=nn(pb,g4[ln,:])
            z=jnp.zeros((128,128),F32)
            if a: x=jnp.concatenate([z,x],0); y=jnp.concatenate([z,y],0)
            if b<256: x=jnp.concatenate([x,z],0); y=jnp.concatenate([y,z],0)
            dk.append(x); dv.append(y)
            kt=kv[d][a:b,:128].astype(F32).T.astype(BF)
            t=nn(kt,ds)
            if d==0: acc_ref[:,ln]=t
            else: acc_ref[:,ln]+=t
        outs[d][:,:128]=(dk[0]+dk[1]).astype(outs[d].dtype)
        outs[d][:,128:]=(dv[0]+dv[1]).astype(outs[d].dtype)
    for d in range(4):
        gate(d,functools.partial(pass3,d))
        if d:
            @pl.when(before<=(d-1)*TOK)
            def _(): outs[d][...]=jnp.zeros_like(outs[d])
    for hf in range(2):
        for h in range(GROUP):
            c=slice(hf*LANES+h*HALF,hf*LANES+(h+1)*HALF)
            gq_ref[hf*HALF:(hf+1)*HALF,h*128:(h+1)*128]=(acc_ref[:,c]*SCALE).T.astype(BF)
def call(before,start,q,g,kvs,ng,g0,interpret=False):
    col=lambda w:pl.BlockSpec((TOK,w),lambda i:(0,i))
    qcol=pl.BlockSpec((TOK,512),lambda i:(0,i+g0))
    return pl.pallas_call(kernel,grid=(ng,),
        in_specs=[pl.BlockSpec(memory_space=pltpu.SMEM),pl.BlockSpec((1,TOK),lambda i:(0,0)),qcol,qcol]+[col(256)]*4,
        out_specs=[col(512)]+[col(256)]*4,
        out_shape=[jax.ShapeDtypeStruct((TOK,512*ng),BF),jax.ShapeDtypeStruct((TOK,256*ng),F32)]+[jax.ShapeDtypeStruct((TOK,256*ng),BF)]*3,
        scratch_shapes=[pltpu.VMEM((1024,128),BF)]*2+[pltpu.VMEM((4,256,1024),F32)]*2+[pltpu.VMEM((8,1024),F32)]*3+[pltpu.VMEM((128,1024),F32)],
        compiler_params=pltpu.CompilerParams(vmem_limit_bytes=48*2**20),interpret=interpret)(before,start,q,g,*kvs)
CHUNKS = ((0, 2), (2, 2))


def pack_kernel(chunks, keys_ref, values_ref, *outs):
    for (first, count), out in zip(chunks, outs):
        for i in range(count):
            src = slice((first + i) * 128, (first + i + 1) * 128)
            out[:, i * 256 : i * 256 + 128] = keys_ref[:, src]
            out[:, i * 256 + 128 : i * 256 + 256] = values_ref[:, src]


def pack(keys, values, chunks):
    return pl.pallas_call(
        functools.partial(pack_kernel, chunks),
        out_shape=[jax.ShapeDtypeStruct((TOK, 256 * n), BF) for _, n in chunks],
    )(keys, values)


def final_kernel(chunks, *refs):
    own, got = refs[: len(chunks)], refs[len(chunks) : 2 * len(chunks)]
    gk, gv = refs[2 * len(chunks) :]
    for (first, count), a, b in zip(chunks, own, got):
        for i in range(count):
            dst = slice((first + i) * 128, (first + i + 1) * 128)
            k = slice(i * 256, i * 256 + 128)
            v = slice(i * 256 + 128, i * 256 + 256)
            gk[:, dst] = (a[:, k] + b[:, k].astype(F32)).astype(BF)
            gv[:, dst] = (a[:, v] + b[:, v].astype(F32)).astype(BF)


def final(own, got, chunks):
    return pl.pallas_call(
        functools.partial(final_kernel, chunks),
        out_shape=[jax.ShapeDtypeStruct((TOK, 512), BF)] * 2,
    )(*own, *got)


def shift(x, distance):
    devices = range(lax.axis_size(("dp", "ctx")))
    route = [(i - distance, i) for i in devices if i - distance in devices]
    return lax.ppermute(x, ("dp", "ctx"), route)


def add(a, b):
    return (a.astype(F32) + b.astype(F32)).astype(BF)


def on_device(queries, keys, values, grad_out, doc_lengths):
    first = lax.axis_index(("dp", "ctx")) * TOK
    ends = jnp.cumsum(doc_lengths)
    pos = first + jnp.arange(TOK, dtype=jnp.int32)
    starts = jnp.max(jnp.where(ends[:, None] <= pos[None, :], ends[:, None], 0), axis=0) - first
    before = jnp.maximum(-starts[:1], 0)
    windows = [[kv] for kv in pack(keys, values, CHUNKS)]
    for _ in range(REACH):
        for w in windows:
            w.append(shift(w[-1], 1))
    grads = [
        call(before, starts[None], queries, grad_out, w, n, f) for (f, n), w in zip(CHUNKS, windows)
    ]
    own = [g[1] for g in grads]
    got = [shift(g[4], -1) for g in grads]
    got = [shift(add(x, g[3]), -1) for x, g in zip(got, grads)]
    got = [shift(add(x, g[2]), -1) for x, g in zip(got, grads)]
    gk, gv = final(own, got, CHUNKS)
    gq = jnp.concatenate([g[0] for g in grads], axis=1)
    return gq, gk, gv


def solution(mesh):
    spec = P(("dp", "ctx"), None)
    return jax.shard_map(
        on_device,
        mesh=mesh,
        in_specs=(spec, spec, spec, spec, P()),
        out_specs=(spec, spec, spec),
        check_vma=False,
    )
```

time: 323 us -> 117 us (0.36)
  waiting for transfers between devices: 183 us -> 46.9 us
  matrix products: 62 us -> 0 us
  other arithmetic: 24.6 us -> 1.86 us
  Pallas kernels: 0 us -> 18.8 us
  local copies, waits for them, and re-layouts: 20.6 us -> 6.31 us
  starting transfers between devices: 28.9 us -> 39.7 us
    ppermute x6 -> x12, waiting for transfers between devices: 183 us -> 46.9 us  [shift(): return lax.ppermute(x, ('dp', 'ctx'), route)]
    dot_general x20 -> x0, matrix products: 42.5 us -> none  [the longest x4 12.1 us: group_terms(): jnp.einsum('tgd,kd->gtk', g_group, v_group, preferred_element_type=jnp.fl...]
    sub x4 -> x0, matrix products: 19.5 us -> none  [group_terms(): expo = jnp.where(allowed[None], jnp.exp(masked - top), 0.0)]
    pallas_call x0 -> x4, Pallas kernels: none -> 18.8 us  [the longest x2 14.7 us: call(): pl.pallas_call(kernel, grid=(ng,), in_specs=[pl.BlockSpec(memory_space=pl...]
    ppermute x6 -> x12, starting transfers between devices: 28.9 us -> 39.7 us  [shift(): return lax.ppermute(x, ('dp', 'ctx'), route)]
    convert_element_type x4, other arithmetic: 10.1 us -> 0.27 us  [add(): return (a.astype(F32) + b.astype(F32)).astype(BF)]
    concatenate x2 -> x1, other arithmetic: 7.79 us -> 1.04 us  [on_device(): gq = jnp.concatenate([g[0] for g in grads], axis=1)]
    dynamic_slice x8 -> x0, local copies, waits for them, and re-layouts: 4.57 us -> none  [block_terms(): lax.map(lambda xs: group_terms(xs[0], xs[1], xs[2], xs[3], allowed, scale...]
  transfers between devices with their start and end apart: 6 -> 12, of which waited for: 6 -> 8; matrix products, arithmetic and copies ran while one was open for 2% -> 3% of each run, Pallas kernels for 0% -> 13%
where the time goes in v1:
time: 117 us; the launch traced here: 115 us
  waiting for transfers between devices  46.9 us (40%)
  starting transfers between devices  39.7 us (34%)
  Pallas kernels  18.8 us (16%)
  local copies, waits for them, and re-layouts  6.31 us (5%)
  other arithmetic  1.86 us (2%)
  between operations  1.49 us (1%)
    ppermute x12, waiting for transfers between devices, shift(): return lax.ppermute(x, ('dp', 'ctx'), route)  46.9 us
    ppermute x12, starting transfers between devices, shift(): return lax.ppermute(x, ('dp', 'ctx'), route)  39.7 us
    pallas_call x2, Pallas kernels, call(): pl.pallas_call(kernel, grid=(ng,), in_specs=[pl.BlockSpec(memory_space=pl...  14.7 us
    unnamed x16, local copies, waits for them, and re-layouts  4.92 us
  transfers between devices with their start and end apart: 12, of which 8 were waited for; matrix products, arithmetic and copies ran while one was open for 3% of the time, Pallas kernels for 13%

profile of v1, /device:TPU:6, one launch (start us, length us, event | category | flops | bytes accessed | tf_op | source)
XLA Modules:
  0.0 115.1 jit_solution(3652832975368978263)
XLA Ops:
  0.6 1.9 %shard_map.76 = (bf16[256,512]{1,0:T(8,128)(2,1)}, bf16[256,512]{1,0:T(8,128)(2,1)}) custom-call(bf16[256,512]{1,0:T(8,128)(2,1)} %keys_ref.1, bf16[256,512]{1,0:T(8,128)(2,1)} %values_ref.1), custom_call_target="tpu_custom_call" | custom-call | tf_op jit(solution)/shard_map/pallas_call | solution.py:111
  2.5 3.8 %collective-permute-start = (bf16[256,512]{1,0:T(8,128)(2,1)}, bf16[256,512]{1,0:T(8,128)(2,1)S(1)}, u32[]{:S(2)}, u32[]{:S(2)}) collective-permute-start(bf16[256,512]{1,0:T(8,128)(2,1)} %get-tuple-element.17.kv0), channel_id=1, source_target_pairs={{0,1},{1,2},{2,3},{3,4},{4,5},{5,6},{6,7},{7,8},{8,9},{9,10},{10,1... | collective-permute-start | bytes 786440 | tf_op jit(solution)/shard_map/ppermute | solution.py:139
  6.4 3.8 %collective-permute-start.3 = (bf16[256,512]{1,0:T(8,128)(2,1)}, bf16[256,512]{1,0:T(8,128)(2,1)S(1)}, u32[]{:S(2)}, u32[]{:S(2)}) collective-permute-start(bf16[256,512]{1,0:T(8,128)(2,1)} %get-tuple-element.19.kv0), channel_id=1, source_target_pairs={{0,1},{1,2},{2,3},{3,4},{4,5},{5,6},{6,7},{7,8},{8,9},{9,10},{10,1... | collective-permute-start | bytes 786440 | tf_op jit(solution)/shard_map/ppermute | solution.py:139
  10.2 0.7 pad_bitcast_fusion
  10.9 0.3 reduce-window.9
  11.2 0.1 slice.13
  11.3 0.1 slice_reduce_fusion
  11.4 12.5 %collective-permute-done.kv1 = bf16[256,512]{1,0:T(8,128)(2,1)S(1)} collective-permute-done((bf16[256,512]{1,0:T(8,128)(2,1)}, bf16[256,512]{1,0:T(8,128)(2,1)S(1)}, u32[]{:S(2)}, u32[]{:S(2)}) %collective-permute-start) | collective-permute-done | bytes 262176 | tf_op jit(solution)/shard_map/ppermute | solution.py:139
  23.9 1.9 %collective-permute-start.1 = (bf16[256,512]{1,0:T(8,128)(2,1)S(1)}, bf16[256,512]{1,0:T(8,128)(2,1)S(1)}, u32[]{:S(2)}, u32[]{:S(2)}) collective-permute-start(bf16[256,512]{1,0:T(8,128)(2,1)S(1)} %collective-permute-done.kv1), channel_id=1, source_target_pairs={{0,1},{1,2},{2,3},{3,4},{4,5},{5,6},{6,7},{7,8},{8,9},{9,10},{10,1... | collective-permute-start | bytes 786440 | tf_op jit(solution)/shard_map/ppermute | solution.py:139
  25.8 3.0 %collective-permute-done.3.kv1 = bf16[256,512]{1,0:T(8,128)(2,1)S(1)} collective-permute-done((bf16[256,512]{1,0:T(8,128)(2,1)}, bf16[256,512]{1,0:T(8,128)(2,1)S(1)}, u32[]{:S(2)}, u32[]{:S(2)}) %collective-permute-start.3) | collective-permute-done | bytes 262176 | tf_op jit(solution)/shard_map/ppermute | solution.py:139
  28.8 1.9 %collective-permute-start.4 = (bf16[256,512]{1,0:T(8,128)(2,1)S(1)}, bf16[256,512]{1,0:T(8,128)(2,1)S(1)}, u32[]{:S(2)}, u32[]{:S(2)}) collective-permute-start(bf16[256,512]{1,0:T(8,128)(2,1)S(1)} %collective-permute-done.3.kv1), channel_id=1, source_target_pairs={{0,1},{1,2},{2,3},{3,4},{4,5},{5,6},{6,7},{7,8},{8,9},{9,10},{10,1... | collective-permute-start | bytes 786440 | tf_op jit(solution)/shard_map/ppermute | solution.py:139
  30.7 0.1 add_bitcast_fusion
  30.8 12.9 %collective-permute-done.4.kv2 = bf16[256,512]{1,0:T(8,128)(2,1)S(1)} collective-permute-done((bf16[256,512]{1,0:T(8,128)(2,1)S(1)}, bf16[256,512]{1,0:T(8,128)(2,1)S(1)}, u32[]{:S(2)}, u32[]{:S(2)}) %collective-permute-start.4) | collective-permute-done | bytes 262176 | tf_op jit(solution)/shard_map/ppermute | solution.py:139
  43.7 1.9 %collective-permute-start.5 = (bf16[256,512]{1,0:T(8,128)(2,1)S(1)}, bf16[256,512]{1,0:T(8,128)(2,1)S(1)}, u32[]{:S(2)}, u32[]{:S(2)}) collective-permute-start(bf16[256,512]{1,0:T(8,128)(2,1)S(1)} %collective-permute-done.4.kv2), channel_id=1, source_target_pairs={{0,1},{1,2},{2,3},{3,4},{4,5},{5,6},{6,7},{7,8},{8,9},{9,10},{10,1... | collective-permute-start | bytes 786440 | tf_op jit(solution)/shard_map/ppermute | solution.py:139
  45.6 0.1 select_reduce_fusion
  45.7 0.0 collective-permute-done.1.kv2
  45.8 1.9 %collective-permute-start.2 = (bf16[256,512]{1,0:T(8,128)(2,1)S(1)}, bf16[256,512]{1,0:T(8,128)(2,1)S(1)}, u32[]{:S(2)}, u32[]{:S(2)}) collective-permute-start(bf16[256,512]{1,0:T(8,128)(2,1)S(1)} %collective-permute-done.1.kv2), channel_id=1, source_target_pairs={{0,1},{1,2},{2,3},{3,4},{4,5},{5,6},{6,7},{7,8},{8,9},{9,10},{10,1... | collective-permute-start | bytes 786440 | tf_op jit(solution)/shard_map/ppermute | solution.py:139
  47.7 0.5 slice.16
  48.9 9.6 %collective-permute-done.5.kv3 = bf16[256,512]{1,0:T(8,128)(2,1)S(1)} collective-permute-done((bf16[256,512]{1,0:T(8,128)(2,1)S(1)}, bf16[256,512]{1,0:T(8,128)(2,1)S(1)}, u32[]{:S(2)}, u32[]{:S(2)}) %collective-permute-start.5) | collective-permute-done | bytes 262176 | tf_op jit(solution)/shard_map/ppermute | solution.py:139
  58.5 1.2 %copy-done = bf16[256,2048]{1,0:T(8,128)(2,1)S(1)} copy-done((bf16[256,2048]{1,0:T(8,128)(2,1)S(1)}, bf16[256,2048]{1,0:T(8,128)(2,1)}, u32[]{:S(2)}) %copy-start) | copy-done | bytes 1048600
  59.7 1.2 %copy-done.1 = bf16[256,2048]{1,0:T(8,128)(2,1)S(1)} copy-done((bf16[256,2048]{1,0:T(8,128)(2,1)S(1)}, bf16[256,2048]{1,0:T(8,128)(2,1)}, u32[]{:S(2)}) %copy-start.1) | copy-done | bytes 1048600
  60.9 0.9 copy-done.5
  61.9 7.3 %shard_map.78 = (bf16[256,1024]{1,0:T(8,128)(2,1)S(1)}, f32[256,512]{1,0:T(8,128)S(1)}, bf16[256,512]{1,0:T(8,128)(2,1)S(1)}, bf16[256,512]{1,0:T(8,128)(2,1)S(1)}, bf16[256,512]{1,0:T(8,128)(2,1)S(1)}) custom-call(s32[1]{0:T(128)S(6)} %max.3.before_ref, s32[1,256]{1,0:T(1,128)S(1)} %bitcast.6, bf16[256,2048]{1,0:T(8,128)(2,1)S(1)} %copy-done, ...), custom_call_target="tpu_custom_call" | custom-call | tf_op jit(solution)/shard_map/pallas_call | solution.py:93
  69.2 0.0 copy-start.2
  69.2 0.8 copy-done.2
  70.0 1.9 %collective-permute-start.9 = (bf16[256,512]{1,0:T(8,128)(2,1)S(1)}, bf16[256,512]{1,0:T(8,128)(2,1)S(1)}, u32[]{:S(2)}, u32[]{:S(2)}) collective-permute-start(bf16[256,512]{1,0:T(8,128)(2,1)S(1)} %get-tuple-element.26), channel_id=1, source_target_pairs={{1,0},{2,1},{3,2},{4,3},{5,4},{6,5},{7,6},{8,7},{9,8},{10,9},{11,1... | collective-permute-start | bytes 786440 | tf_op jit(solution)/shard_map/ppermute | solution.py:139
  71.9 0.0 collective-permute-done.2.kv3
  71.9 0.0 copy-done.4
  71.9 7.3 %shard_map.77 = (bf16[256,1024]{1,0:T(8,128)(2,1)S(1)}, f32[256,512]{1,0:T(8,128)S(1)}, bf16[256,512]{1,0:T(8,128)(2,1)S(1)}, bf16[256,512]{1,0:T(8,128)(2,1)S(1)}, bf16[256,512]{1,0:T(8,128)(2,1)S(1)}) custom-call(s32[1]{0:T(128)S(6)} %max.3.before_ref, s32[1,256]{1,0:T(1,128)S(1)} %bitcast.7, bf16[256,2048]{1,0:T(8,128)(2,1)S(1)} %copy-done, ...), custom_call_target="tpu_custom_call" | custom-call | tf_op jit(solution)/shard_map/pallas_call | solution.py:93
  79.3 0.0 copy-start.3
  79.3 1.9 %collective-permute-start.6 = (bf16[256,512]{1,0:T(8,128)(2,1)S(1)}, bf16[256,512]{1,0:T(8,128)(2,1)S(1)}, u32[]{:S(2)}, u32[]{:S(2)}) collective-permute-start(bf16[256,512]{1,0:T(8,128)(2,1)S(1)} %get-tuple-element.23), channel_id=1, source_target_pairs={{1,0},{2,1},{3,2},{4,3},{5,4},{6,5},{7,6},{8,7},{9,8},{10,9},{11,1... | collective-permute-start | bytes 786440 | tf_op jit(solution)/shard_map/ppermute | solution.py:139
  81.2 0.0 collective-permute-done.9
  81.2 0.1 add_convert_fusion.1
  81.3 3.7 %collective-permute-start.10 = (bf16[256,512]{1,0:T(8,128)(2,1)S(1)}, bf16[256,512]{1,0:T(8,128)(2,1)S(1)}, u32[]{:S(2)}, u32[]{:S(2)}) collective-permute-start(bf16[256,512]{1,0:T(8,128)(2,1)S(1)} %add_convert_fusion.1), channel_id=1, source_target_pairs={{1,0},{2,1},{3,2},{4,3},{5,4},{6,5},{7,6},{8,7},{9,8},{10,9},{11,1... | collective-permute-start | bytes 786440 | tf_op jit(solution)/shard_map/ppermute | solution.py:139
  85.0 4.7 %collective-permute-done.6 = bf16[256,512]{1,0:T(8,128)(2,1)S(1)} collective-permute-done((bf16[256,512]{1,0:T(8,128)(2,1)S(1)}, bf16[256,512]{1,0:T(8,128)(2,1)S(1)}, u32[]{:S(2)}, u32[]{:S(2)}) %collective-permute-start.6) | collective-permute-done | bytes 262176 | tf_op jit(solution)/shard_map/ppermute | solution.py:139
  89.7 0.1 add_convert_fusion.3
  89.8 5.1 %collective-permute-start.7 = (bf16[256,512]{1,0:T(8,128)(2,1)S(1)}, bf16[256,512]{1,0:T(8,128)(2,1)S(1)}, u32[]{:S(2)}, u32[]{:S(2)}) collective-permute-start(bf16[256,512]{1,0:T(8,128)(2,1)S(1)} %add_convert_fusion.3), channel_id=1, source_target_pairs={{1,0},{2,1},{3,2},{4,3},{5,4},{6,5},{7,6},{8,7},{9,8},{10,9},{11,1... | collective-permute-start | bytes 786440 | tf_op jit(solution)/shard_map/ppermute | solution.py:139
  94.8 0.4 collective-permute-done.10
  95.2 0.1 add_convert_fusion
  95.3 4.5 %collective-permute-start.11 = (bf16[256,512]{1,0:T(8,128)(2,1)S(1)}, bf16[256,512]{1,0:T(8,128)(2,1)S(1)}, u32[]{:S(2)}, u32[]{:S(2)}) collective-permute-start(bf16[256,512]{1,0:T(8,128)(2,1)S(1)} %add_convert_fusion), channel_id=1, source_target_pairs={{1,0},{2,1},{3,2},{4,3},{5,4},{6,5},{7,6},{8,7},{9,8},{10,9},{11,1... | collective-permute-start | bytes 786440 | tf_op jit(solution)/shard_map/ppermute | solution.py:139
  99.8 1.1 collective-permute-done.7
  100.9 0.1 add_convert_fusion.2
  101.0 7.2 %collective-permute-start.8 = (bf16[256,512]{1,0:T(8,128)(2,1)S(1)}, bf16[256,512]{1,0:T(8,128)(2,1)S(1)}, u32[]{:S(2)}, u32[]{:S(2)}) collective-permute-start(bf16[256,512]{1,0:T(8,128)(2,1)S(1)} %add_convert_fusion.2), channel_id=1, source_target_pairs={{1,0},{2,1},{3,2},{4,3},{5,4},{6,5},{7,6},{8,7},{9,8},{10,9},{11,1... | collective-permute-start | bytes 786440 | tf_op jit(solution)/shard_map/ppermute | solution.py:139
  108.2 1.0 pad_maximum_fusion
  109.3 0.0 collective-permute-done.11.refs_3_
  109.3 2.8 %collective-permute-done.8.refs_2_ = bf16[256,512]{1,0:T(8,128)(2,1)S(1)} collective-permute-done((bf16[256,512]{1,0:T(8,128)(2,1)S(1)}, bf16[256,512]{1,0:T(8,128)(2,1)S(1)}, u32[]{:S(2)}, u32[]{:S(2)}) %collective-permute-start.8) | collective-permute-done | bytes 262176 | tf_op jit(solution)/shard_map/ppermute | solution.py:139
  112.1 0.7 copy-done.7
  112.8 2.2 %shard_map.79 = (bf16[256,512]{1,0:T(8,128)(2,1)}, bf16[256,512]{1,0:T(8,128)(2,1)}) custom-call(f32[256,512]{1,0:T(8,128)} %copy-done.3, f32[256,512]{1,0:T(8,128)} %copy-done.2, bf16[256,512]{1,0:T(8,128)(2,1)} %copy-done.7, bf16[256,512]{1,0:T(8,128)(2,1)} %copy-done.6), custom_call_target="tpu_custom_call" | custom-call | tf_op jit(solution)/shard_map/pallas_call | solution.py:130
  (11 shorter events, 0.1 us)
Async XLA Ops:
  2.5 21.4 %collective-permute-start = (bf16[256,512]{1,0:T(8,128)(2,1)}, bf16[256,512]{1,0:T(8,128)(2,1)S(1)}, u32[]{:S(2)}, u32[]{:S(2)}) collective-permute-start(bf16[256,512]{1,0:T(8,128)(2,1)} %get-tuple-element.17.kv0), channel_id=1, source_target_pairs={{0,1},{1,2},{2,3},{3,4},{4,5},{5,6},{6,7},{7,8},{8,9},{9,10},{10,1... | collective-permute-start | bytes 786440 | tf_op jit(solution)/shard_map/ppermute | solution.py:139
  6.4 22.4 %collective-permute-start.3 = (bf16[256,512]{1,0:T(8,128)(2,1)}, bf16[256,512]{1,0:T(8,128)(2,1)S(1)}, u32[]{:S(2)}, u32[]{:S(2)}) collective-permute-start(bf16[256,512]{1,0:T(8,128)(2,1)} %get-tuple-element.19.kv0), channel_id=1, source_target_pairs={{0,1},{1,2},{2,3},{3,4},{4,5},{5,6},{6,7},{7,8},{8,9},{9,10},{10,1... | collective-permute-start | bytes 786440 | tf_op jit(solution)/shard_map/ppermute | solution.py:139
  23.9 21.9 %collective-permute-start.1 = (bf16[256,512]{1,0:T(8,128)(2,1)S(1)}, bf16[256,512]{1,0:T(8,128)(2,1)S(1)}, u32[]{:S(2)}, u32[]{:S(2)}) collective-permute-start(bf16[256,512]{1,0:T(8,128)(2,1)S(1)} %collective-permute-done.kv1), channel_id=1, source_target_pairs={{0,1},{1,2},{2,3},{3,4},{4,5},{5,6},{6,7},{7,8},{8,9},{9,10},{10,1... | collective-permute-start | bytes 786440 | tf_op jit(solution)/shard_map/ppermute | solution.py:139
  28.8 14.9 %collective-permute-start.4 = (bf16[256,512]{1,0:T(8,128)(2,1)S(1)}, bf16[256,512]{1,0:T(8,128)(2,1)S(1)}, u32[]{:S(2)}, u32[]{:S(2)}) collective-permute-start(bf16[256,512]{1,0:T(8,128)(2,1)S(1)} %collective-permute-done.3.kv1), channel_id=1, source_target_pairs={{0,1},{1,2},{2,3},{3,4},{4,5},{5,6},{6,7},{7,8},{8,9},{9,10},{10,1... | collective-permute-start | bytes 786440 | tf_op jit(solution)/shard_map/ppermute | solution.py:139
  43.7 14.7 %collective-permute-start.5 = (bf16[256,512]{1,0:T(8,128)(2,1)S(1)}, bf16[256,512]{1,0:T(8,128)(2,1)S(1)}, u32[]{:S(2)}, u32[]{:S(2)}) collective-permute-start(bf16[256,512]{1,0:T(8,128)(2,1)S(1)} %collective-permute-done.4.kv2), channel_id=1, source_target_pairs={{0,1},{1,2},{2,3},{3,4},{4,5},{5,6},{6,7},{7,8},{8,9},{9,10},{10,1... | collective-permute-start | bytes 786440 | tf_op jit(solution)/shard_map/ppermute | solution.py:139
  45.8 26.2 %collective-permute-start.2 = (bf16[256,512]{1,0:T(8,128)(2,1)S(1)}, bf16[256,512]{1,0:T(8,128)(2,1)S(1)}, u32[]{:S(2)}, u32[]{:S(2)}) collective-permute-start(bf16[256,512]{1,0:T(8,128)(2,1)S(1)} %collective-permute-done.1.kv2), channel_id=1, source_target_pairs={{0,1},{1,2},{2,3},{3,4},{4,5},{5,6},{6,7},{7,8},{8,9},{9,10},{10,1... | collective-permute-start | bytes 786440 | tf_op jit(solution)/shard_map/ppermute | solution.py:139
  58.5 1.2 %copy-start = (bf16[256,2048]{1,0:T(8,128)(2,1)S(1)}, bf16[256,2048]{1,0:T(8,128)(2,1)}, u32[]{:S(2)}) copy-start(bf16[256,2048]{1,0:T(8,128)(2,1)} %q_ref.3) | copy-start | bytes 3145732
  59.7 1.2 %copy-start.1 = (bf16[256,2048]{1,0:T(8,128)(2,1)S(1)}, bf16[256,2048]{1,0:T(8,128)(2,1)}, u32[]{:S(2)}) copy-start(bf16[256,2048]{1,0:T(8,128)(2,1)} %g_ref.3) | copy-start | bytes 3145732
  60.9 0.9 copy-start.5
  61.9 10.1 %copy-start.4 = (bf16[256,512]{1,0:T(8,128)(2,1)S(1)}, bf16[256,512]{1,0:T(8,128)(2,1)}, u32[]{:S(2)}) copy-start(bf16[256,512]{1,0:T(8,128)(2,1)} %get-tuple-element.17.kv0) | copy-start | bytes 786436
  69.2 0.8 copy-start.2
  70.0 11.2 %collective-permute-start.9 = (bf16[256,512]{1,0:T(8,128)(2,1)S(1)}, bf16[256,512]{1,0:T(8,128)(2,1)S(1)}, u32[]{:S(2)}, u32[]{:S(2)}) collective-permute-start(bf16[256,512]{1,0:T(8,128)(2,1)S(1)} %get-tuple-element.26), channel_id=1, source_target_pairs={{1,0},{2,1},{3,2},{4,3},{5,4},{6,5},{7,6},{8,7},{9,8},{10,9},{11,1... | collective-permute-start | bytes 786440 | tf_op jit(solution)/shard_map/ppermute | solution.py:139
  79.3 16.0 %copy-start.3 = (f32[256,512]{1,0:T(8,128)}, f32[256,512]{1,0:T(8,128)S(1)}, u32[]{:S(2)}) copy-start(f32[256,512]{1,0:T(8,128)S(1)} %get-tuple-element.21.refs_0_) | copy-start | bytes 1572868
  79.3 10.4 %collective-permute-start.6 = (bf16[256,512]{1,0:T(8,128)(2,1)S(1)}, bf16[256,512]{1,0:T(8,128)(2,1)S(1)}, u32[]{:S(2)}, u32[]{:S(2)}) collective-permute-start(bf16[256,512]{1,0:T(8,128)(2,1)S(1)} %get-tuple-element.23), channel_id=1, source_target_pairs={{1,0},{2,1},{3,2},{4,3},{5,4},{6,5},{7,6},{8,7},{9,8},{10,9},{11,1... | collective-permute-start | bytes 786440 | tf_op jit(solution)/shard_map/ppermute | solution.py:139
  81.3 13.9 %collective-permute-start.10 = (bf16[256,512]{1,0:T(8,128)(2,1)S(1)}, bf16[256,512]{1,0:T(8,128)(2,1)S(1)}, u32[]{:S(2)}, u32[]{:S(2)}) collective-permute-start(bf16[256,512]{1,0:T(8,128)(2,1)S(1)} %add_convert_fusion.1), channel_id=1, source_target_pairs={{1,0},{2,1},{3,2},{4,3},{5,4},{6,5},{7,6},{8,7},{9,8},{10,9},{11,1... | collective-permute-start | bytes 786440 | tf_op jit(solution)/shard_map/ppermute | solution.py:139
  89.8 11.1 %collective-permute-start.7 = (bf16[256,512]{1,0:T(8,128)(2,1)S(1)}, bf16[256,512]{1,0:T(8,128)(2,1)S(1)}, u32[]{:S(2)}, u32[]{:S(2)}) collective-permute-start(bf16[256,512]{1,0:T(8,128)(2,1)S(1)} %add_convert_fusion.3), channel_id=1, source_target_pairs={{1,0},{2,1},{3,2},{4,3},{5,4},{6,5},{7,6},{8,7},{9,8},{10,9},{11,1... | collective-permute-start | bytes 786440 | tf_op jit(solution)/shard_map/ppermute | solution.py:139
  95.3 14.0 %collective-permute-start.11 = (bf16[256,512]{1,0:T(8,128)(2,1)S(1)}, bf16[256,512]{1,0:T(8,128)(2,1)S(1)}, u32[]{:S(2)}, u32[]{:S(2)}) collective-permute-start(bf16[256,512]{1,0:T(8,128)(2,1)S(1)} %add_convert_fusion), channel_id=1, source_target_pairs={{1,0},{2,1},{3,2},{4,3},{5,4},{6,5},{7,6},{8,7},{9,8},{10,9},{11,1... | collective-permute-start | bytes 786440 | tf_op jit(solution)/shard_map/ppermute | solution.py:139
  101.0 11.1 %collective-permute-start.8 = (bf16[256,512]{1,0:T(8,128)(2,1)S(1)}, bf16[256,512]{1,0:T(8,128)(2,1)S(1)}, u32[]{:S(2)}, u32[]{:S(2)}) collective-permute-start(bf16[256,512]{1,0:T(8,128)(2,1)S(1)} %add_convert_fusion.2), channel_id=1, source_target_pairs={{1,0},{2,1},{3,2},{4,3},{5,4},{6,5},{7,6},{8,7},{9,8},{10,9},{11,1... | collective-permute-start | bytes 786440 | tf_op jit(solution)/shard_map/ppermute | solution.py:139
  109.3 2.8 %copy-start.6 = (bf16[256,512]{1,0:T(8,128)(2,1)}, bf16[256,512]{1,0:T(8,128)(2,1)S(1)}, u32[]{:S(2)}) copy-start(bf16[256,512]{1,0:T(8,128)(2,1)S(1)} %collective-permute-done.11.refs_3_) | copy-start | bytes 786436
  112.1 0.7 copy-start.7

commit v2 on v0

v2 whole, which is shorter than its diff:
```python
import functools

import jax
import jax.numpy as jnp
from jax import lax
from jax.experimental import pallas as pl
from jax.experimental.pallas import tpu as pltpu
from jax.sharding import PartitionSpec as P

HEAD_DIM = 128
REACH = 3
TOK = 256
HALF = 128
GROUP = 4
KV_HEADS = 4
LANES = GROUP * HALF
WIDE = 2 * LANES
SCALE = HEAD_DIM**-0.5
LOG2E = 1.4426950408889634
NEG = -1e30
F32 = jnp.float32
BF = jnp.bfloat16
VMEM_LIMIT = 16 * 2**20


def nt(a, b):
    return lax.dot_general(a, b, (((1,), (1,)), ((), ())), preferred_element_type=F32)


def nn(a, b):
    return lax.dot_general(a, b, (((1,), (0,)), ((), ())), preferred_element_type=F32)


def fold(x, op):
    total = x[:8]
    for i in range(1, x.shape[0] // 8):
        total = op(total, x[i * 8 : (i + 1) * 8])
    return total


def lanes(half):
    return slice(half * LANES, (half + 1) * LANES)


def rows_of(distance, half):
    if distance == 0 and half == 0:
        return 0, HALF
    if distance == REACH and half == 1:
        return HALF, TOK
    return 0, TOK


def regroup(dst, src):
    for half in range(2):
        for h in range(GROUP):
            at = half * LANES + h * HALF
            dst[at : at + HALF, :] = src[half * HALF : (half + 1) * HALF, h * 128 : (h + 1) * 128]


def masked_scores(distance, half, k, q4, start_ref):
    a, b = rows_of(distance, half)
    s = nt(k[a:b], q4[lanes(half), :])
    start = start_ref[:, half * HALF : (half + 1) * HALF]
    at = lax.broadcasted_iota(jnp.int32, (b - a, HALF), 0) + (a - distance * TOK)
    ok = at >= start
    if distance == 0:
        ok = ok & (at <= lax.broadcasted_iota(jnp.int32, (b - a, HALF), 1) + half * HALF)
    return jnp.concatenate(
        [jnp.where(ok, s[:, h * HALF : (h + 1) * HALF], NEG) for h in range(GROUP)], axis=1
    )


def local_probs(distance, k, q4, start_ref, p_ref, stat_ref):
    for half in range(2):
        a, b = rows_of(distance, half)
        ln = lanes(half)
        s = masked_scores(distance, half, k, q4, start_ref)
        top = jnp.max(fold(s, jnp.maximum), axis=0, keepdims=True)
        p = jnp.exp2((s - top) * (SCALE * LOG2E))
        p_ref[a:b, ln] = p.astype(BF)
        stat_ref[0:1, ln] = top
        stat_ref[1:2, ln] = jnp.sum(fold(p, jnp.add), axis=0, keepdims=True)


def local_dprobs(distance, v, g4, p_ref, dp_ref, sum_ref):
    for half in range(2):
        a, b = rows_of(distance, half)
        ln = lanes(half)
        dp = nt(v[a:b], g4[ln, :])
        dp_ref[a:b, ln] = dp
        sum_ref[0:1, ln] = jnp.sum(fold(p_ref[a:b, ln].astype(F32) * dp, jnp.add), axis=0, keepdims=True)


def joined(distance, halves):
    blank = jnp.zeros((HALF, HEAD_DIM), F32)
    full = []
    for half, x in enumerate(halves):
        a, b = rows_of(distance, half)
        x = jnp.concatenate([blank, x], 0) if a else x
        full.append(jnp.concatenate([x, blank], 0) if b < TOK else x)
    return full[0] + full[1]


def value_grad(distance, g4, p_ref, factor):
    halves = []
    for half in range(2):
        a, b = rows_of(distance, half)
        ln = lanes(half)
        probs = p_ref[a:b, ln].astype(F32) * factor[:, ln]
        halves.append(nn(probs.astype(BF), g4[ln, :]))
    return joined(distance, halves)


def key_query_grad(distance, k, q4, p_ref, dp_ref, factor, delta):
    dk, dq = [], []
    for half in range(2):
        a, b = rows_of(distance, half)
        ln = lanes(half)
        probs = p_ref[a:b, ln].astype(F32) * factor[:, ln]
        ds = (probs * (dp_ref[a:b, ln] - delta[:, ln])).astype(BF)
        dk.append(nn(ds, q4[ln, :]) * SCALE)
        dq.append(nn(k[a:b].astype(F32).T.astype(BF), ds))
    return joined(distance, dk), dq


def near(before_ref, distance):
    return before_ref[0] > (distance - 1) * TOK


def gated(distance, before_ref, work, other):
    if distance == 0:
        work()
    else:
        pl.when(near(before_ref, distance))(work)
        pl.when(jnp.logical_not(near(before_ref, distance)))(other)


def no_probs(stat_ref):
    stat_ref[0:1, :] = jnp.full((1, WIDE), NEG, F32)
    stat_ref[1:2, :] = jnp.zeros((1, WIDE), F32)


def probs_kernel(distance, before_ref, start_ref, q_ref, k_ref, *outs):
    i = pl.program_id(0)
    if distance == 0:
        q4_ref, p_ref, stat_ref = outs
        q4 = q4_ref.at[i]
        regroup(q4, q_ref)
    else:
        p_ref, stat_ref = outs
        q4 = q_ref.at[i]
    gated(
        distance,
        before_ref,
        lambda: local_probs(distance, k_ref[...], q4, start_ref, p_ref.at[i], stat_ref.at[i]),
        lambda: no_probs(stat_ref.at[i]),
    )


def dprobs_kernel(distance, before_ref, g_ref, v_ref, p_ref, *outs):
    i = pl.program_id(0)
    if distance == 0:
        g4_ref, dp_ref, sum_ref = outs
        g4 = g4_ref.at[i]
        regroup(g4, g_ref)
    else:
        dp_ref, sum_ref = outs
        g4 = g_ref.at[i]

    def other():
        sum_ref[i, 0:1, :] = jnp.zeros((1, WIDE), F32)

    gated(
        distance,
        before_ref,
        lambda: local_dprobs(distance, v_ref[...], g4, p_ref.at[i], dp_ref.at[i], sum_ref.at[i]),
        other,
    )


def far_value_kernel(before_ref, start_ref, q4_ref, g4_ref, k_ref, s0, s1, s2, part_ref, p_ref, row_ref, stat_ref):
    i = pl.program_id(0)
    row = row_ref.at[i]
    gated(
        REACH,
        before_ref,
        lambda: local_probs(REACH, k_ref[...], q4_ref.at[i], start_ref, p_ref.at[i], stat_ref),
        lambda: no_probs(stat_ref),
    )
    stats = (s0.at[i], s1.at[i], s2.at[i], stat_ref)
    top = functools.reduce(jnp.maximum, [s[0:1, :] for s in stats])
    weight = [jnp.exp2((s[0:1, :] - top) * (SCALE * LOG2E)) for s in stats]
    total = sum(w * s[1:2, :] for w, s in zip(weight, stats))
    for d in range(REACH + 1):
        row[d : d + 1, :] = weight[d] / total

    def work():
        part_ref[...] = value_grad(REACH, g4_ref.at[i], p_ref.at[i], row[REACH : REACH + 1, :]).astype(BF)

    def other():
        part_ref[...] = jnp.zeros_like(part_ref)

    gated(REACH, before_ref, work, other)


def far_key_kernel(before_ref, q4_ref, g4_ref, k_ref, v_ref, p_ref, row_ref, e0, e1, e2, part_ref, dq_ref, delta_ref, dp_ref, sum_ref):
    i = pl.program_id(0)
    row, dq_out = row_ref.at[i], dq_ref.at[i]

    def none():
        sum_ref[0:1, :] = jnp.zeros((1, WIDE), F32)

    gated(
        REACH,
        before_ref,
        lambda: local_dprobs(REACH, v_ref[...], g4_ref.at[i], p_ref.at[i], dp_ref, sum_ref),
        none,
    )
    sums = (e0.at[i], e1.at[i], e2.at[i], sum_ref)
    delta = sum(row[d : d + 1, :] * sums[d][0:1, :] for d in range(REACH + 1))
    delta_ref[i, 0:1, :] = delta

    def work():
        dk, dq = key_query_grad(
            REACH, k_ref[...], q4_ref.at[i], p_ref.at[i], dp_ref, row[REACH : REACH + 1, :], delta
        )
        part_ref[...] = dk.astype(BF)
        for half in range(2):
            dq_out[:, lanes(half)] = dq[half]

    def other():
        part_ref[...] = jnp.zeros_like(part_ref)
        dq_out[...] = jnp.zeros_like(dq_out)

    gated(REACH, before_ref, work, other)


def value_kernel(distance, before_ref, g4_ref, p_ref, row_ref, part_ref):
    i = pl.program_id(0)

    def work():
        factor = row_ref[i, distance : distance + 1, :]
        part_ref[...] = value_grad(distance, g4_ref.at[i], p_ref.at[i], factor).astype(part_ref.dtype)

    def other():
        part_ref[...] = jnp.zeros_like(part_ref)

    gated(distance, before_ref, work, other)


def key_kernel(distance, before_ref, q4_ref, k_ref, p_ref, dp_ref, row_ref, delta_ref, dq_in, part_ref, dq_ref):
    i = pl.program_id(0)
    dq_old = dq_in.at[i]

    def work():
        dk, dq = key_query_grad(
            distance,
            k_ref[...],
            q4_ref.at[i],
            p_ref.at[i],
            dp_ref.at[i],
            row_ref[i, distance : distance + 1, :],
            delta_ref[i, 0:1, :],
        )
        part_ref[...] = dk.astype(part_ref.dtype)
        for half in range(2):
            total = dq_old[:, lanes(half)] + dq[half]
            if distance:
                dq_ref[i, :, lanes(half)] = total
                continue
            total = total * SCALE
            for h in range(GROUP):
                dq_ref[half * HALF : (half + 1) * HALF, h * 128 : (h + 1) * 128] = (
                    total[:, h * HALF : (h + 1) * HALF].T.astype(BF)
                )

    def other():
        part_ref[...] = jnp.zeros_like(part_ref)
        dq_ref[i] = dq_old[...]

    gated(distance, before_ref, work, other)


SMEM = pl.BlockSpec(memory_space=pltpu.SMEM)
HELD = pl.BlockSpec(memory_space=pltpu.VMEM)
START = pl.BlockSpec((1, TOK), lambda i: (0, 0))
QUERY = pl.BlockSpec((TOK, GROUP * HEAD_DIM), lambda i: (0, i))
KEY = pl.BlockSpec((TOK, HEAD_DIM), lambda i: (0, i))


def held(rows, width, dtype):
    return HELD, pltpu.VMEM((KV_HEADS, rows, width), dtype)


GROUPED = held(WIDE, HEAD_DIM, BF)
PROBS = held(TOK, WIDE, BF)
DPROBS = held(TOK, WIDE, F32)
STATS = held(8, WIDE, F32)
QUERY_GRAD = held(HEAD_DIM, WIDE, F32)
PART = KEY, jax.ShapeDtypeStruct((TOK, KV_HEADS * HEAD_DIM), BF)
OWN = KEY, jax.ShapeDtypeStruct((TOK, KV_HEADS * HEAD_DIM), F32)
QUERY_OUT = QUERY, jax.ShapeDtypeStruct((TOK, KV_HEADS * GROUP * HEAD_DIM), BF)


def call(kernel, in_specs, outs, matmuls, args, scratch=()):
    return pl.pallas_call(
        kernel,
        grid=(KV_HEADS,),
        in_specs=in_specs,
        out_specs=[spec for spec, _ in outs],
        out_shape=[shape for _, shape in outs],
        scratch_shapes=scratch,
        compiler_params=pltpu.CompilerParams(vmem_limit_bytes=VMEM_LIMIT),
        cost_estimate=pl.CostEstimate(
            flops=matmuls * KV_HEADS * 2 * TOK * WIDE * HEAD_DIM, bytes_accessed=2**20, transcendentals=0
        ),
    )(*args)


def probs_of(distance, before, start, q, k):
    own = distance == 0
    return call(
        functools.partial(probs_kernel, distance),
        [SMEM, START, QUERY if own else HELD, KEY],
        [GROUPED] * own + [PROBS, STATS],
        1,
        (before, start, q, k),
    )


def dprobs_of(distance, before, g, v, p):
    own = distance == 0
    return call(
        functools.partial(dprobs_kernel, distance),
        [SMEM, QUERY if own else HELD, KEY, HELD],
        [GROUPED] * own + [DPROBS, STATS],
        1,
        (before, g, v, p),
    )


def far_value(before, start, q4, g4, k, *stats):
    return call(
        far_value_kernel,
        [SMEM, START, HELD, HELD, KEY, HELD, HELD, HELD],
        [PART, PROBS, STATS],
        2,
        (before, start, q4, g4, k, *stats),
        [pltpu.VMEM((8, WIDE), F32)],
    )


def far_key(before, q4, g4, k, v, p, row, *sums):
    return call(
        far_key_kernel,
        [SMEM, HELD, HELD, KEY, KEY] + [HELD] * 5,
        [PART, QUERY_GRAD, STATS],
        3,
        (before, q4, g4, k, v, p, row, *sums),
        [pltpu.VMEM((TOK, WIDE), F32), pltpu.VMEM((8, WIDE), F32)],
    )


def value_part(distance, before, g4, p, row):
    return call(
        functools.partial(value_kernel, distance),
        [SMEM, HELD, HELD, HELD],
        [PART if distance else OWN],
        1,
        (before, g4, p, row),
    )[0]


def key_part(distance, before, q4, k, p, dp, row, delta, dq):
    return call(
        functools.partial(key_kernel, distance),
        [SMEM, HELD, KEY] + [HELD] * 5,
        [PART, QUERY_GRAD] if distance else [OWN, QUERY_OUT],
        2,
        (before, q4, k, p, dp, row, delta, dq),
    )


def shift(x, distance):
    devices = range(lax.axis_size(("dp", "ctx")))
    route = [(i - distance, i) for i in devices if i - distance in devices]
    return lax.ppermute(x, ("dp", "ctx"), route)


def add(a, b):
    return (a.astype(F32) + b.astype(F32)).astype(BF)


def after(x, *others):
    return lax.optimization_barrier((x, *others))[0]


def in_hbm(x):
    return pltpu.with_memory_space_constraint(x, pltpu.HBM)


def on_device(queries, keys, values, grad_out, doc_lengths):
    first = lax.axis_index(("dp", "ctx")) * TOK
    ends = jnp.cumsum(doc_lengths)
    pos = first + jnp.arange(TOK, dtype=jnp.int32)
    start = jnp.max(jnp.where(ends[:, None] <= pos[None, :], ends[:, None], 0), axis=0) - first
    before = jnp.maximum(-start[:1], 0)
    start = start[None]
    k, v = [keys], [values]
    k.append(shift(k[0], 1))
    v.append(shift(after(values, start), 1))
    q4, p0, stat0 = probs_of(0, before, start, in_hbm(queries), in_hbm(keys))
    p, dp, stat, total = [p0], [], [stat0], []
    done = stat0
    for d in (1, 2):
        k[d] = after(k[d], done)
        k.append(shift(k[d], 1))
        x, y = probs_of(d, before, start, q4, k[d])
        p.append(x)
        stat.append(y)
        v[d] = after(v[d], y)
        v.append(shift(v[d], 1))
        if d == 1:
            late = after(grad_out, v[d])
            g4, dp0, sum0 = dprobs_of(0, before, in_hbm(late), in_hbm(values), p0)
            dp.append(dp0)
            total.append(sum0)
        x, y = dprobs_of(d, before, g4, v[d], p[d])
        dp.append(x)
        total.append(y)
        done = y
    k[3] = after(k[3], done)
    part, p3, row = far_value(before, start, q4, g4, k[3], *stat)
    gv = shift(part, -1)
    v[3] = after(v[3], part)
    part, dq, delta = far_key(before, q4, g4, k[3], v[3], p3, row, *total)
    gk = shift(part, -1)
    done = part
    for d in (2, 1):
        part = value_part(d, before, g4, p[d], after(row, done))
        gv = add(after(gv, part), part)
        done = gv
        gv = shift(gv, -1)
        part, dq = key_part(d, before, q4, k[d], p[d], dp[d], after(row, done), delta, dq)
        gk = add(after(gk, part), part)
        done = gk
        gk = shift(gk, -1)
    own_v = value_part(0, before, g4, p0, after(row, done))
    own_k, grad_queries = key_part(0, before, q4, keys, p0, dp0, after(row, own_v), delta, dq)
    gv = after(gv, own_k)
    return grad_queries, add(own_k, gk), add(own_v, gv)


def solution(mesh):
    spec = P(("dp", "ctx"), None)
    return jax.shard_map(
        on_device,
        mesh=mesh,
        in_specs=(spec, spec, spec, spec, P()),
        out_specs=(spec, spec, spec),
        check_vma=False,
    )
```

time: 323 us -> 98.2 us (0.30)
  waiting for transfers between devices: 183 us -> 23.2 us
  matrix products: 62 us -> 0 us
  other arithmetic: 24.6 us -> 2.38 us
  starting transfers between devices: 28.9 us -> 50.5 us
  local copies, waits for them, and re-layouts: 20.6 us -> 1.4 us
  Pallas kernels: 0 us -> 18.7 us
    ppermute x6 -> x12, waiting for transfers between devices: 183 us -> 23.2 us  [shift(): return lax.ppermute(x, ('dp', 'ctx'), route)]
    dot_general x20 -> x0, matrix products: 42.5 us -> none  [the longest x4 12.1 us: group_terms(): jnp.einsum('tgd,kd->gtk', g_group, v_group, preferred_element_type=jnp.fl...]
    ppermute x6 -> x12, starting transfers between devices: 28.9 us -> 50.5 us  [shift(): return lax.ppermute(x, ('dp', 'ctx'), route)]
    sub x4 -> x0, matrix products: 19.5 us -> none  [group_terms(): expo = jnp.where(allowed[None], jnp.exp(masked - top), 0.0)]
    pallas_call x0 -> x14, Pallas kernels: none -> 18.7 us  [call(): pl.pallas_call(kernel, grid=(KV_HEADS,), in_specs=in_specs, out_specs=[sp...]
    convert_element_type x4 -> x6, other arithmetic: 10.1 us -> 1.82 us  [add(): return (a.astype(F32) + b.astype(F32)).astype(BF)]
    unnamed x15 -> x2, local copies, waits for them, and re-layouts: 7.91 us -> 0.01 us
    concatenate x2 -> x0, other arithmetic: 7.79 us -> none  [the longest x1 7.76 us: on_device(): window = jnp.concatenate(pieces + [packed], axis=0)]
  transfers between devices with their start and end apart: 6 -> 12, of which waited for: 6 -> 5; matrix products, arithmetic and copies ran while one was open for 2% -> 3% of each run, Pallas kernels for 0% -> 19%
where the time goes in v2:
time: 98.2 us; the launch traced here: 97.7 us
  starting transfers between devices  50.5 us (51%)
  waiting for transfers between devices  23.2 us (24%)
  Pallas kernels  18.7 us (19%)
  other arithmetic  2.38 us (2%)
  between operations  1.58 us (2%)
  local copies, waits for them, and re-layouts  1.4 us (1%)
    ppermute x12, starting transfers between devices, shift(): return lax.ppermute(x, ('dp', 'ctx'), route)  50.5 us
    ppermute x12, waiting for transfers between devices, shift(): return lax.ppermute(x, ('dp', 'ctx'), route)  23.2 us
    pallas_call x14, Pallas kernels, call(): pl.pallas_call(kernel, grid=(KV_HEADS,), in_specs=in_specs, out_specs=[sp...  18.7 us
  transfers between devices with their start and end apart: 12, of which 5 were waited for; matrix products, arithmetic and copies ran while one was open for 3% of the time, Pallas kernels for 19%

profile of v2, /device:TPU:6, one launch (start us, length us, event | category | flops | bytes accessed | tf_op | source)
XLA Modules:
  0.0 97.7 jit_solution(10739211543104740644)
XLA Ops:
  0.6 3.8 %collective-permute-start.1 = (bf16[256,512]{1,0:T(8,128)(2,1)}, bf16[256,512]{1,0:T(8,128)(2,1)S(1)}, u32[]{:S(2)}, u32[]{:S(2)}) collective-permute-start(bf16[256,512]{1,0:T(8,128)(2,1)} %k_ref.3), channel_id=1, source_target_pairs={{0,1},{1,2},{2,3},{3,4},{4,5},{5,6},{6,7},{7,8},{8,9},{9,10},{10,1... | collective-permute-start | bytes 786440 | tf_op jit(solution)/shard_map/ppermute | solution.py:387
  4.5 0.7 pad_bitcast_fusion
  5.2 0.3 reduce-window.9
  5.5 0.1 slice.13
  5.6 0.1 slice_reduce_fusion
  5.7 0.1 add_bitcast_fusion
  5.8 0.1 select_reduce_fusion
  5.9 3.8 %collective-permute-start = (bf16[256,512]{1,0:T(8,128)(2,1)}, bf16[256,512]{1,0:T(8,128)(2,1)S(1)}, u32[]{:S(2)}, u32[]{:S(2)}) collective-permute-start(bf16[256,512]{1,0:T(8,128)(2,1)} %v_ref.1), channel_id=1, source_target_pairs={{0,1},{1,2},{2,3},{3,4},{4,5},{5,6},{6,7},{7,8},{8,9},{9,10},{10,1... | collective-permute-start | bytes 786440 | tf_op jit(solution)/shard_map/ppermute | solution.py:387
  9.8 0.5 slice.16
  10.9 3.3 %shard_map.76 = (bf16[4,1024,128]{2,1,0:T(8,128)(2,1)S(1)}, bf16[4,256,1024]{2,1,0:T(8,128)(2,1)S(1)}, f32[4,8,1024]{2,1,0:T(8,128)S(1)}) custom-call(s32[1]{0:T(128)S(6)} %max.3.before_ref, s32[1,256]{1,0:T(1,128)S(1)} %bitcast.6, bf16[256,2048]{1,0:T(8,128)(2,1)} %q_ref.1, bf16[256,512]{1,0:T(8,128)(2,1)} %k_ref.3), custom_call_target="tpu_custom_call" | custom-call | flops 268435456 | bytes 1048576 | tf_op jit(solution)/shard_map/pallas_call | solution.py:306
  14.2 7.8 %collective-permute-done.1.k_ref = bf16[256,512]{1,0:T(8,128)(2,1)S(1)} collective-permute-done((bf16[256,512]{1,0:T(8,128)(2,1)}, bf16[256,512]{1,0:T(8,128)(2,1)S(1)}, u32[]{:S(2)}, u32[]{:S(2)}) %collective-permute-start.1) | collective-permute-done | bytes 262176 | tf_op jit(solution)/shard_map/ppermute | solution.py:387
  22.0 1.9 %collective-permute-start.2 = (bf16[256,512]{1,0:T(8,128)(2,1)S(1)}, bf16[256,512]{1,0:T(8,128)(2,1)S(1)}, u32[]{:S(2)}, u32[]{:S(2)}) collective-permute-start(bf16[256,512]{1,0:T(8,128)(2,1)S(1)} %collective-permute-done.1.k_ref), channel_id=1, source_target_pairs={{0,1},{1,2},{2,3},{3,4},{4,5},{5,6},{6,7},{7,8},{8,9},{9,10},{10,1... | collective-permute-start | bytes 786440 | tf_op jit(solution)/shard_map/ppermute | solution.py:387
  23.9 2.2 %shard_map.77 = (bf16[4,256,1024]{2,1,0:T(8,128)(2,1)S(1)}, f32[4,8,1024]{2,1,0:T(8,128)S(1)}) custom-call(s32[1]{0:T(128)S(6)} %max.3.before_ref, s32[1,256]{1,0:T(1,128)S(1)} %bitcast.7, bf16[4,1024,128]{2,1,0:T(8,128)(2,1)S(1)} %get-tuple-element.48.q_ref.q4_ref, bf16[256,512]{1,0:T(8,128)(2,1)S(1)} %collective-permute-done.1.k_ref), custom_call_target="tpu_custom_call" | custom-call | flops 268435456 | bytes 1048576 | tf_op jit(solution)/shard_map/pallas_call | solution.py:306
  26.1 0.8 collective-permute-done.v_ref
  26.9 1.9 %collective-permute-start.4 = (bf16[256,512]{1,0:T(8,128)(2,1)S(1)}, bf16[256,512]{1,0:T(8,128)(2,1)S(1)}, u32[]{:S(2)}, u32[]{:S(2)}) collective-permute-start(bf16[256,512]{1,0:T(8,128)(2,1)S(1)} %collective-permute-done.v_ref), channel_id=1, source_target_pairs={{0,1},{1,2},{2,3},{3,4},{4,5},{5,6},{6,7},{7,8},{8,9},{9,10},{10,1... | collective-permute-start | bytes 786440 | tf_op jit(solution)/shard_map/ppermute | solution.py:387
  28.8 2.9 %shard_map.78 = (bf16[4,1024,128]{2,1,0:T(8,128)(2,1)S(1)}, f32[4,256,1024]{2,1,0:T(8,128)S(1)}, f32[4,8,1024]{2,1,0:T(8,128)S(1)}) custom-call(s32[1]{0:T(128)S(6)} %max.3.before_ref, bf16[256,2048]{1,0:T(8,128)(2,1)} %g_ref, bf16[256,512]{1,0:T(8,128)(2,1)} %v_ref.1, bf16[4,256,1024]{2,1,0:T(8,128)(2,1)S(1)} %get-tuple-element.49.p_ref), custom_call_target="tpu_custom_call" | custom-call | flops 268435456 | bytes 1048576 | tf_op jit(solution)/shard_map/pallas_call | solution.py:306
  31.7 1.4 %shard_map.79 = (f32[4,256,1024]{2,1,0:T(8,128)S(1)}, f32[4,8,1024]{2,1,0:T(8,128)S(1)}) custom-call(s32[1]{0:T(128)S(6)} %max.3.before_ref, bf16[4,1024,128]{2,1,0:T(8,128)(2,1)S(1)} %get-tuple-element.57.g_ref.g4_ref, bf16[256,512]{1,0:T(8,128)(2,1)S(1)} %collective-permute-done.v_ref, bf16[4,256,1024]{2,1,0:T(8,128)(2,1)S(1)} %get-tuple-element.58.p_ref), custom_call_target="tpu_custom_call" | custom-call | flops 268435456 | bytes 1048576 | tf_op jit(solution)/shard_map/pallas_call | solution.py:306
  33.1 4.8 %collective-permute-done.2.k_ref = bf16[256,512]{1,0:T(8,128)(2,1)S(1)} collective-permute-done((bf16[256,512]{1,0:T(8,128)(2,1)S(1)}, bf16[256,512]{1,0:T(8,128)(2,1)S(1)}, u32[]{:S(2)}, u32[]{:S(2)}) %collective-permute-start.2) | collective-permute-done | bytes 262176 | tf_op jit(solution)/shard_map/ppermute | solution.py:387
  37.9 1.9 %collective-permute-start.3 = (bf16[256,512]{1,0:T(8,128)(2,1)S(1)}, bf16[256,512]{1,0:T(8,128)(2,1)S(1)}, u32[]{:S(2)}, u32[]{:S(2)}) collective-permute-start(bf16[256,512]{1,0:T(8,128)(2,1)S(1)} %collective-permute-done.2.k_ref), channel_id=1, source_target_pairs={{0,1},{1,2},{2,3},{3,4},{4,5},{5,6},{6,7},{7,8},{8,9},{9,10},{10,1... | collective-permute-start | bytes 786440 | tf_op jit(solution)/shard_map/ppermute | solution.py:387
  39.8 0.2 shard_map.80
  40.0 2.8 %collective-permute-done.4.v_ref = bf16[256,512]{1,0:T(8,128)(2,1)S(1)} collective-permute-done((bf16[256,512]{1,0:T(8,128)(2,1)S(1)}, bf16[256,512]{1,0:T(8,128)(2,1)S(1)}, u32[]{:S(2)}, u32[]{:S(2)}) %collective-permute-start.4) | collective-permute-done | bytes 262176 | tf_op jit(solution)/shard_map/ppermute | solution.py:387
  42.8 1.9 %collective-permute-start.5 = (bf16[256,512]{1,0:T(8,128)(2,1)S(1)}, bf16[256,512]{1,0:T(8,128)(2,1)S(1)}, u32[]{:S(2)}, u32[]{:S(2)}) collective-permute-start(bf16[256,512]{1,0:T(8,128)(2,1)S(1)} %collective-permute-done.4.v_ref), channel_id=1, source_target_pairs={{0,1},{1,2},{2,3},{3,4},{4,5},{5,6},{6,7},{7,8},{8,9},{9,10},{10,1... | collective-permute-start | bytes 786440 | tf_op jit(solution)/shard_map/ppermute | solution.py:387
  44.7 0.2 shard_map.81
  44.9 7.1 %collective-permute-done.3.k_ref = bf16[256,512]{1,0:T(8,128)(2,1)S(1)} collective-permute-done((bf16[256,512]{1,0:T(8,128)(2,1)S(1)}, bf16[256,512]{1,0:T(8,128)(2,1)S(1)}, u32[]{:S(2)}, u32[]{:S(2)}) %collective-permute-start.3) | collective-permute-done | bytes 262176 | tf_op jit(solution)/shard_map/ppermute | solution.py:387
  52.0 0.4 shard_map.82
  52.4 4.7 %collective-permute-start.7 = (bf16[256,512]{1,0:T(8,128)(2,1)S(1)}, bf16[256,512]{1,0:T(8,128)(2,1)S(1)}, u32[]{:S(2)}, u32[]{:S(2)}) collective-permute-start(bf16[256,512]{1,0:T(8,128)(2,1)S(1)} %get-tuple-element.67), channel_id=1, source_target_pairs={{1,0},{2,1},{3,2},{4,3},{5,4},{6,5},{7,6},{8,7},{9,8},{10,9},{11,1... | collective-permute-start | bytes 786440 | tf_op jit(solution)/shard_map/ppermute | solution.py:387
  57.1 0.5 shard_map.83
  57.6 4.2 %collective-permute-start.6 = (bf16[256,512]{1,0:T(8,128)(2,1)S(1)}, bf16[256,512]{1,0:T(8,128)(2,1)S(1)}, u32[]{:S(2)}, u32[]{:S(2)}) collective-permute-start(bf16[256,512]{1,0:T(8,128)(2,1)S(1)} %get-tuple-element.71), channel_id=1, source_target_pairs={{1,0},{2,1},{3,2},{4,3},{5,4},{6,5},{7,6},{8,7},{9,8},{10,9},{11,1... | collective-permute-start | bytes 786440 | tf_op jit(solution)/shard_map/ppermute | solution.py:387
  61.8 0.2 shard_map.84
  62.0 0.0 collective-permute-done.7
  62.0 0.1 add_convert_fusion.5
  62.1 8.0 %collective-permute-start.9 = (bf16[256,512]{1,0:T(8,128)(2,1)S(1)}, bf16[256,512]{1,0:T(8,128)(2,1)S(1)}, u32[]{:S(2)}, u32[]{:S(2)}) collective-permute-start(bf16[256,512]{1,0:T(8,128)(2,1)S(1)} %add_convert_fusion.5), channel_id=1, source_target_pairs={{1,0},{2,1},{3,2},{4,3},{5,4},{6,5},{7,6},{8,7},{9,8},{10,9},{11,1... | collective-permute-start | bytes 786440 | tf_op jit(solution)/shard_map/ppermute | solution.py:387
  70.0 0.4 shard_map.85
  70.5 0.0 collective-permute-done.6
  70.5 0.1 add_convert_fusion.4
  70.5 5.7 %collective-permute-start.8 = (bf16[256,512]{1,0:T(8,128)(2,1)S(1)}, bf16[256,512]{1,0:T(8,128)(2,1)S(1)}, u32[]{:S(2)}, u32[]{:S(2)}) collective-permute-start(bf16[256,512]{1,0:T(8,128)(2,1)S(1)} %add_convert_fusion.4), channel_id=1, source_target_pairs={{1,0},{2,1},{3,2},{4,3},{5,4},{6,5},{7,6},{8,7},{9,8},{10,9},{11,1... | collective-permute-start | bytes 786440 | tf_op jit(solution)/shard_map/ppermute | solution.py:387
  76.2 1.3 %shard_map.86 = bf16[256,512]{1,0:T(8,128)(2,1)S(1)} custom-call(s32[1]{0:T(128)S(6)} %max.3.before_ref, bf16[4,1024,128]{2,1,0:T(8,128)(2,1)S(1)} %get-tuple-element.57.g_ref.g4_ref, bf16[4,256,1024]{2,1,0:T(8,128)(2,1)S(1)} %get-tuple-element.58.p_ref, f32[4,8,1024]{2,1,0:T(8,128)S(1)} %get-tuple-element.88.row_ref), custom_call_target="tpu_custom_call" | custom-call | flops 268435456 | bytes 1048576 | tf_op jit(solution)/shard_map/pallas_call | solution.py:306
  77.6 0.0 collective-permute-done.9
  77.6 0.1 add_convert_fusion.3
  77.7 4.5 %collective-permute-start.11 = (bf16[256,512]{1,0:T(8,128)(2,1)S(1)}, bf16[256,512]{1,0:T(8,128)(2,1)S(1)}, u32[]{:S(2)}, u32[]{:S(2)}) collective-permute-start(bf16[256,512]{1,0:T(8,128)(2,1)S(1)} %add_convert_fusion.3), channel_id=1, source_target_pairs={{1,0},{2,1},{3,2},{4,3},{5,4},{6,5},{7,6},{8,7},{9,8},{10,9},{11,1... | collective-permute-start | bytes 786440 | tf_op jit(solution)/shard_map/ppermute | solution.py:387
  82.2 1.7 %shard_map.87 = (bf16[256,512]{1,0:T(8,128)(2,1)S(1)}, f32[4,128,1024]{2,1,0:T(8,128)S(1)}) custom-call(s32[1]{0:T(128)S(6)} %max.3.before_ref, bf16[4,1024,128]{2,1,0:T(8,128)(2,1)S(1)} %get-tuple-element.48.q_ref.q4_ref, bf16[256,512]{1,0:T(8,128)(2,1)S(1)} %collective-permute-done.1.k_ref, bf16[4,256,1024]{2,1,0:T(8,128)(2,1)S(1)} %get-tuple-element.58.p_ref, ...), custom_call_target="tpu_custom_call" | custom-call | flops 536870912 | bytes 1048576 | tf_op jit(solution)/shard_map/pallas_call | solution.py:306
  83.9 0.1 add_convert_fusion.2
  84.0 0.0 copy-start
  84.0 8.1 %collective-permute-start.10 = (bf16[256,512]{1,0:T(8,128)(2,1)S(1)}, bf16[256,512]{1,0:T(8,128)(2,1)S(1)}, u32[]{:S(2)}, u32[]{:S(2)}) collective-permute-start(bf16[256,512]{1,0:T(8,128)(2,1)S(1)} %add_convert_fusion.2), channel_id=1, source_target_pairs={{1,0},{2,1},{3,2},{4,3},{5,4},{6,5},{7,6},{8,7},{9,8},{10,9},{11,1... | collective-permute-start | bytes 786440 | tf_op jit(solution)/shard_map/ppermute | solution.py:387
  92.1 1.1 %shard_map.88 = f32[256,512]{1,0:T(8,128)S(1)} custom-call(s32[1]{0:T(128)S(6)} %max.3.before_ref, bf16[4,1024,128]{2,1,0:T(8,128)(2,1)S(1)} %get-tuple-element.57.g_ref.g4_ref, bf16[4,256,1024]{2,1,0:T(8,128)(2,1)S(1)} %get-tuple-element.49.p_ref, f32[4,8,1024]{2,1,0:T(8,128)S(1)} %get-tuple-element.88.row_ref), custom_call_target="tpu_custom_call" | custom-call | flops 268435456 | bytes 1048576 | tf_op jit(solution)/shard_map/pallas_call | solution.py:306
  93.2 2.9 %shard_map.89 = (f32[256,512]{1,0:T(8,128)S(1)}, bf16[256,2048]{1,0:T(8,128)(2,1)}) custom-call(s32[1]{0:T(128)S(6)} %max.3.before_ref, bf16[4,1024,128]{2,1,0:T(8,128)(2,1)S(1)} %get-tuple-element.48.q_ref.q4_ref, bf16[256,512]{1,0:T(8,128)(2,1)S(1)} %copy-done, bf16[4,256,1024]{2,1,0:T(8,128)(2,1)S(1)} %get-tuple-element.49.p_ref, ...), custom_call_target="tpu_custom_call" | custom-call | flops 536870912 | bytes 1048576 | tf_op jit(solution)/shard_map/pallas_call | solution.py:306
  96.1 0.8 add_convert_fusion
  96.9 0.8 add_convert_fusion.1
  (8 shorter events, 0.1 us)
Async XLA Ops:
  0.6 21.4 %collective-permute-start.1 = (bf16[256,512]{1,0:T(8,128)(2,1)}, bf16[256,512]{1,0:T(8,128)(2,1)S(1)}, u32[]{:S(2)}, u32[]{:S(2)}) collective-permute-start(bf16[256,512]{1,0:T(8,128)(2,1)} %k_ref.3), channel_id=1, source_target_pairs={{0,1},{1,2},{2,3},{3,4},{4,5},{5,6},{6,7},{7,8},{8,9},{9,10},{10,1... | collective-permute-start | bytes 786440 | tf_op jit(solution)/shard_map/ppermute | solution.py:387
  5.9 20.9 %collective-permute-start = (bf16[256,512]{1,0:T(8,128)(2,1)}, bf16[256,512]{1,0:T(8,128)(2,1)S(1)}, u32[]{:S(2)}, u32[]{:S(2)}) collective-permute-start(bf16[256,512]{1,0:T(8,128)(2,1)} %v_ref.1), channel_id=1, source_target_pairs={{0,1},{1,2},{2,3},{3,4},{4,5},{5,6},{6,7},{7,8},{8,9},{9,10},{10,1... | collective-permute-start | bytes 786440 | tf_op jit(solution)/shard_map/ppermute | solution.py:387
  22.0 15.9 %collective-permute-start.2 = (bf16[256,512]{1,0:T(8,128)(2,1)S(1)}, bf16[256,512]{1,0:T(8,128)(2,1)S(1)}, u32[]{:S(2)}, u32[]{:S(2)}) collective-permute-start(bf16[256,512]{1,0:T(8,128)(2,1)S(1)} %collective-permute-done.1.k_ref), channel_id=1, source_target_pairs={{0,1},{1,2},{2,3},{3,4},{4,5},{5,6},{6,7},{7,8},{8,9},{9,10},{10,1... | collective-permute-start | bytes 786440 | tf_op jit(solution)/shard_map/ppermute | solution.py:387
  26.9 15.9 %collective-permute-start.4 = (bf16[256,512]{1,0:T(8,128)(2,1)S(1)}, bf16[256,512]{1,0:T(8,128)(2,1)S(1)}, u32[]{:S(2)}, u32[]{:S(2)}) collective-permute-start(bf16[256,512]{1,0:T(8,128)(2,1)S(1)} %collective-permute-done.v_ref), channel_id=1, source_target_pairs={{0,1},{1,2},{2,3},{3,4},{4,5},{5,6},{6,7},{7,8},{8,9},{9,10},{10,1... | collective-permute-start | bytes 786440 | tf_op jit(solution)/shard_map/ppermute | solution.py:387
  37.9 14.1 %collective-permute-start.3 = (bf16[256,512]{1,0:T(8,128)(2,1)S(1)}, bf16[256,512]{1,0:T(8,128)(2,1)S(1)}, u32[]{:S(2)}, u32[]{:S(2)}) collective-permute-start(bf16[256,512]{1,0:T(8,128)(2,1)S(1)} %collective-permute-done.2.k_ref), channel_id=1, source_target_pairs={{0,1},{1,2},{2,3},{3,4},{4,5},{5,6},{6,7},{7,8},{8,9},{9,10},{10,1... | collective-permute-start | bytes 786440 | tf_op jit(solution)/shard_map/ppermute | solution.py:387
  42.8 14.3 %collective-permute-start.5 = (bf16[256,512]{1,0:T(8,128)(2,1)S(1)}, bf16[256,512]{1,0:T(8,128)(2,1)S(1)}, u32[]{:S(2)}, u32[]{:S(2)}) collective-permute-start(bf16[256,512]{1,0:T(8,128)(2,1)S(1)} %collective-permute-done.4.v_ref), channel_id=1, source_target_pairs={{0,1},{1,2},{2,3},{3,4},{4,5},{5,6},{6,7},{7,8},{8,9},{9,10},{10,1... | collective-permute-start | bytes 786440 | tf_op jit(solution)/shard_map/ppermute | solution.py:387
  52.4 9.6 %collective-permute-start.7 = (bf16[256,512]{1,0:T(8,128)(2,1)S(1)}, bf16[256,512]{1,0:T(8,128)(2,1)S(1)}, u32[]{:S(2)}, u32[]{:S(2)}) collective-permute-start(bf16[256,512]{1,0:T(8,128)(2,1)S(1)} %get-tuple-element.67), channel_id=1, source_target_pairs={{1,0},{2,1},{3,2},{4,3},{5,4},{6,5},{7,6},{8,7},{9,8},{10,9},{11,1... | collective-permute-start | bytes 786440 | tf_op jit(solution)/shard_map/ppermute | solution.py:387
  57.6 12.9 %collective-permute-start.6 = (bf16[256,512]{1,0:T(8,128)(2,1)S(1)}, bf16[256,512]{1,0:T(8,128)(2,1)S(1)}, u32[]{:S(2)}, u32[]{:S(2)}) collective-permute-start(bf16[256,512]{1,0:T(8,128)(2,1)S(1)} %get-tuple-element.71), channel_id=1, source_target_pairs={{1,0},{2,1},{3,2},{4,3},{5,4},{6,5},{7,6},{8,7},{9,8},{10,9},{11,1... | collective-permute-start | bytes 786440 | tf_op jit(solution)/shard_map/ppermute | solution.py:387
  62.1 15.5 %collective-permute-start.9 = (bf16[256,512]{1,0:T(8,128)(2,1)S(1)}, bf16[256,512]{1,0:T(8,128)(2,1)S(1)}, u32[]{:S(2)}, u32[]{:S(2)}) collective-permute-start(bf16[256,512]{1,0:T(8,128)(2,1)S(1)} %add_convert_fusion.5), channel_id=1, source_target_pairs={{1,0},{2,1},{3,2},{4,3},{5,4},{6,5},{7,6},{8,7},{9,8},{10,9},{11,1... | collective-permute-start | bytes 786440 | tf_op jit(solution)/shard_map/ppermute | solution.py:387
  70.5 13.3 %collective-permute-start.8 = (bf16[256,512]{1,0:T(8,128)(2,1)S(1)}, bf16[256,512]{1,0:T(8,128)(2,1)S(1)}, u32[]{:S(2)}, u32[]{:S(2)}) collective-permute-start(bf16[256,512]{1,0:T(8,128)(2,1)S(1)} %add_convert_fusion.4), channel_id=1, source_target_pairs={{1,0},{2,1},{3,2},{4,3},{5,4},{6,5},{7,6},{8,7},{9,8},{10,9},{11,1... | collective-permute-start | bytes 786440 | tf_op jit(solution)/shard_map/ppermute | solution.py:387
  77.7 18.5 %collective-permute-start.11 = (bf16[256,512]{1,0:T(8,128)(2,1)S(1)}, bf16[256,512]{1,0:T(8,128)(2,1)S(1)}, u32[]{:S(2)}, u32[]{:S(2)}) collective-permute-start(bf16[256,512]{1,0:T(8,128)(2,1)S(1)} %add_convert_fusion.3), channel_id=1, source_target_pairs={{1,0},{2,1},{3,2},{4,3},{5,4},{6,5},{7,6},{8,7},{9,8},{10,9},{11,1... | collective-permute-start | bytes 786440 | tf_op jit(solution)/shard_map/ppermute | solution.py:387
  84.0 9.3 %copy-start = (bf16[256,512]{1,0:T(8,128)(2,1)S(1)}, bf16[256,512]{1,0:T(8,128)(2,1)}, u32[]{:S(2)}) copy-start(bf16[256,512]{1,0:T(8,128)(2,1)} %k_ref.3) | copy-start | bytes 786436
  84.0 12.9 %collective-permute-start.10 = (bf16[256,512]{1,0:T(8,128)(2,1)S(1)}, bf16[256,512]{1,0:T(8,128)(2,1)S(1)}, u32[]{:S(2)}, u32[]{:S(2)}) collective-permute-start(bf16[256,512]{1,0:T(8,128)(2,1)S(1)} %add_convert_fusion.2), channel_id=1, source_target_pairs={{1,0},{2,1},{3,2},{4,3},{5,4},{6,5},{7,6},{8,7},{9,8},{10,9},{11,1... | collective-permute-start | bytes 786440 | tf_op jit(solution)/shard_map/ppermute | solution.py:387

commit v3 on v2

--- a/solution.py
+++ b/solution.py
@@ -13,6 +13,7 @@
 HALF = 128
 GROUP = 4
 KV_HEADS = 4
+FAR_GROUPS = 2
 LANES = GROUP * HALF
 WIDE = 2 * LANES
 SCALE = HEAD_DIM**-0.5
@@ -20,7 +21,7 @@
 NEG = -1e30
 F32 = jnp.float32
 BF = jnp.bfloat16
-VMEM_LIMIT = 16 * 2**20
+VMEM_LIMIT = 20 * 2**20
 
 
 def nt(a, b):
@@ -42,12 +43,25 @@
     return slice(half * LANES, (half + 1) * LANES)
 
 
-def rows_of(distance, half):
-    if distance == 0 and half == 0:
+OWN_BLOCK, NEAR_BLOCK, LATE, EARLY = "own", "near", "late", "early"
+
+
+def rows_of(case, half):
+    if case == OWN_BLOCK and half == 0:
         return 0, HALF
-    if distance == REACH and half == 1:
+    if case == LATE:
         return HALF, TOK
+    if case == EARLY and half == 1:
+        return 0, 0
     return 0, TOK
+
+
+def halves_of(case):
+    return [half for half in range(2) if rows_of(case, half)[1]]
+
+
+def case_of(distance):
+    return NEAR_BLOCK if distance else OWN_BLOCK
 
 
 def regroup(dst, src):
@@ -57,24 +71,26 @@
             dst[at : at + HALF, :] = src[half * HALF : (half + 1) * HALF, h * 128 : (h + 1) * 128]
 
 
-def masked_scores(distance, half, k, q4, start_ref):
-    a, b = rows_of(distance, half)
+def masked_scores(case, distance, half, k, q4, start_ref):
+    a, b = rows_of(case, half)
     s = nt(k[a:b], q4[lanes(half), :])
     start = start_ref[:, half * HALF : (half + 1) * HALF]
     at = lax.broadcasted_iota(jnp.int32, (b - a, HALF), 0) + (a - distance * TOK)
     ok = at >= start
-    if distance == 0:
+    if case == OWN_BLOCK:
         ok = ok & (at <= lax.broadcasted_iota(jnp.int32, (b - a, HALF), 1) + half * HALF)
     return jnp.concatenate(
         [jnp.where(ok, s[:, h * HALF : (h + 1) * HALF], NEG) for h in range(GROUP)], axis=1
     )
 
 
-def local_probs(distance, k, q4, start_ref, p_ref, stat_ref):
-    for half in range(2):
-        a, b = rows_of(distance, half)
+def local_probs(case, distance, k, q4, start_ref, p_ref, stat_ref):
+    if case == EARLY:
+        no_probs(stat_ref)
+    for half in halves_of(case):
+        a, b = rows_of(case, half)
         ln = lanes(half)
-        s = masked_scores(distance, half, k, q4, start_ref)
+        s = masked_scores(case, distance, half, k, q4, start_ref)
         top = jnp.max(fold(s, jnp.maximum), axis=0, keepdims=True)
         p = jnp.exp2((s - top) * (SCALE * LOG2E))
         p_ref[a:b, ln] = p.astype(BF)
@@ -82,45 +98,47 @@
         stat_ref[1:2, ln] = jnp.sum(fold(p, jnp.add), axis=0, keepdims=True)
 
 
-def local_dprobs(distance, v, g4, p_ref, dp_ref, sum_ref):
-    for half in range(2):
-        a, b = rows_of(distance, half)
+def local_dprobs(case, v, g4, p_ref, dp_ref, sum_ref):
+    if case == EARLY:
+        sum_ref[0:1, :] = jnp.zeros((1, WIDE), F32)
+    for half in halves_of(case):
+        a, b = rows_of(case, half)
         ln = lanes(half)
         dp = nt(v[a:b], g4[ln, :])
         dp_ref[a:b, ln] = dp
         sum_ref[0:1, ln] = jnp.sum(fold(p_ref[a:b, ln].astype(F32) * dp, jnp.add), axis=0, keepdims=True)
 
 
-def joined(distance, halves):
+def joined(case, parts):
     blank = jnp.zeros((HALF, HEAD_DIM), F32)
     full = []
-    for half, x in enumerate(halves):
-        a, b = rows_of(distance, half)
+    for half, x in zip(halves_of(case), parts):
+        a, b = rows_of(case, half)
         x = jnp.concatenate([blank, x], 0) if a else x
         full.append(jnp.concatenate([x, blank], 0) if b < TOK else x)
-    return full[0] + full[1]
-
-
-def value_grad(distance, g4, p_ref, factor):
-    halves = []
-    for half in range(2):
-        a, b = rows_of(distance, half)
+    return sum(full[1:], full[0])
+
+
+def value_grad(case, g4, p_ref, factor):
+    parts = []
+    for half in halves_of(case):
+        a, b = rows_of(case, half)
         ln = lanes(half)
         probs = p_ref[a:b, ln].astype(F32) * factor[:, ln]
-        halves.append(nn(probs.astype(BF), g4[ln, :]))
-    return joined(distance, halves)
-
-
-def key_query_grad(distance, k, q4, p_ref, dp_ref, factor, delta):
+        parts.append(nn(probs.astype(BF), g4[ln, :]))
+    return joined(case, parts)
+
+
+def key_query_grad(case, k, q4, p_ref, dp_ref, factor, delta):
     dk, dq = [], []
-    for half in range(2):
-        a, b = rows_of(distance, half)
+    for half in halves_of(case):
+        a, b = rows_of(case, half)
         ln = lanes(half)
         probs = p_ref[a:b, ln].astype(F32) * factor[:, ln]
         ds = (probs * (dp_ref[a:b, ln] - delta[:, ln])).astype(BF)
         dk.append(nn(ds, q4[ln, :]) * SCALE)
         dq.append(nn(k[a:b].astype(F32).T.astype(BF), ds))
-    return joined(distance, dk), dq
+    return joined(case, dk), dq
 
 
 def near(before_ref, distance):
@@ -152,7 +170,7 @@
     gated(
         distance,
         before_ref,
-        lambda: local_probs(distance, k_ref[...], q4, start_ref, p_ref.at[i], stat_ref.at[i]),
+        lambda: local_probs(case_of(distance), distance, k_ref[...], q4, start_ref, p_ref.at[i], stat_ref.at[i]),
         lambda: no_probs(stat_ref.at[i]),
     )
 
@@ -173,66 +191,68 @@
     gated(
         distance,
         before_ref,
-        lambda: local_dprobs(distance, v_ref[...], g4, p_ref.at[i], dp_ref.at[i], sum_ref.at[i]),
+        lambda: local_dprobs(case_of(distance), v_ref[...], g4, p_ref.at[i], dp_ref.at[i], sum_ref.at[i]),
         other,
     )
 
 
+def far_cases(before_ref, work):
+    before = before_ref[0]
+    edge = REACH * TOK - HALF
+    pl.when(before > edge)(functools.partial(work, EARLY))
+    pl.when((before > (REACH - 1) * TOK) & (before <= edge))(functools.partial(work, LATE))
+    pl.when(before <= (REACH - 1) * TOK)(functools.partial(work, None))
+
+
 def far_value_kernel(before_ref, start_ref, q4_ref, g4_ref, k_ref, s0, s1, s2, part_ref, p_ref, row_ref, stat_ref):
-    i = pl.program_id(0)
-    row = row_ref.at[i]
-    gated(
-        REACH,
-        before_ref,
-        lambda: local_probs(REACH, k_ref[...], q4_ref.at[i], start_ref, p_ref.at[i], stat_ref),
-        lambda: no_probs(stat_ref),
-    )
-    stats = (s0.at[i], s1.at[i], s2.at[i], stat_ref)
-    top = functools.reduce(jnp.maximum, [s[0:1, :] for s in stats])
-    weight = [jnp.exp2((s[0:1, :] - top) * (SCALE * LOG2E)) for s in stats]
-    total = sum(w * s[1:2, :] for w, s in zip(weight, stats))
-    for d in range(REACH + 1):
-        row[d : d + 1, :] = weight[d] / total
-
-    def work():
-        part_ref[...] = value_grad(REACH, g4_ref.at[i], p_ref.at[i], row[REACH : REACH + 1, :]).astype(BF)
-
-    def other():
-        part_ref[...] = jnp.zeros_like(part_ref)
-
-    gated(REACH, before_ref, work, other)
+    def work(case):
+        for n in range(FAR_GROUPS):
+            i = pl.program_id(0) * FAR_GROUPS + n
+            at = slice(n * HEAD_DIM, (n + 1) * HEAD_DIM)
+            row, stat = row_ref.at[i], stat_ref.at[n]
+            stats = [s0.at[i], s1.at[i], s2.at[i]]
+            if case:
+                local_probs(case, REACH, k_ref[:, at], q4_ref.at[i], start_ref, p_ref.at[i], stat)
+                stats.append(stat)
+            top = functools.reduce(jnp.maximum, [s[0:1, :] for s in stats])
+            weight = [jnp.exp2((s[0:1, :] - top) * (SCALE * LOG2E)) for s in stats]
+            total = sum(w * s[1:2, :] for w, s in zip(weight, stats))
+            for d, w in enumerate(weight):
+                row[d : d + 1, :] = w / total
+            if case:
+                factor = row[REACH : REACH + 1, :]
+                part_ref[:, at] = value_grad(case, g4_ref.at[i], p_ref.at[i], factor).astype(BF)
+            else:
+                part_ref[:, at] = jnp.zeros((TOK, HEAD_DIM), BF)
+
+    far_cases(before_ref, work)
 
 
 def far_key_kernel(before_ref, q4_ref, g4_ref, k_ref, v_ref, p_ref, row_ref, e0, e1, e2, part_ref, dq_ref, delta_ref, dp_ref, sum_ref):
-    i = pl.program_id(0)
-    row, dq_out = row_ref.at[i], dq_ref.at[i]
-
-    def none():
-        sum_ref[0:1, :] = jnp.zeros((1, WIDE), F32)
-
-    gated(
-        REACH,
-        before_ref,
-        lambda: local_dprobs(REACH, v_ref[...], g4_ref.at[i], p_ref.at[i], dp_ref, sum_ref),
-        none,
-    )
-    sums = (e0.at[i], e1.at[i], e2.at[i], sum_ref)
-    delta = sum(row[d : d + 1, :] * sums[d][0:1, :] for d in range(REACH + 1))
-    delta_ref[i, 0:1, :] = delta
-
-    def work():
-        dk, dq = key_query_grad(
-            REACH, k_ref[...], q4_ref.at[i], p_ref.at[i], dp_ref, row[REACH : REACH + 1, :], delta
-        )
-        part_ref[...] = dk.astype(BF)
-        for half in range(2):
-            dq_out[:, lanes(half)] = dq[half]
-
-    def other():
-        part_ref[...] = jnp.zeros_like(part_ref)
-        dq_out[...] = jnp.zeros_like(dq_out)
-
-    gated(REACH, before_ref, work, other)
+    def work(case):
+        for n in range(FAR_GROUPS):
+            i = pl.program_id(0) * FAR_GROUPS + n
+            at = slice(n * HEAD_DIM, (n + 1) * HEAD_DIM)
+            row, dq_out = row_ref.at[i], dq_ref.at[i]
+            sums = [e0.at[i], e1.at[i], e2.at[i]]
+            if case:
+                local_dprobs(case, v_ref[:, at], g4_ref.at[i], p_ref.at[i], dp_ref.at[n], sum_ref.at[n])
+                sums.append(sum_ref.at[n])
+            delta = sum(row[d : d + 1, :] * s[0:1, :] for d, s in enumerate(sums))
+            delta_ref[i, 0:1, :] = delta
+            if not case:
+                part_ref[:, at] = jnp.zeros((TOK, HEAD_DIM), BF)
+                dq_out[...] = jnp.zeros_like(dq_out)
+                continue
+            factor = row[REACH : REACH + 1, :]
+            dk, dq = key_query_grad(case, k_ref[:, at], q4_ref.at[i], p_ref.at[i], dp_ref.at[n], factor, delta)
+            part_ref[:, at] = dk.astype(BF)
+            if case == EARLY:
+                dq_out[:, lanes(1)] = jnp.zeros((HEAD_DIM, LANES), F32)
+            for half, x in zip(halves_of(case), dq):
+                dq_out[:, lanes(half)] = x
+
+    far_cases(before_ref, work)
 
 
 def value_kernel(distance, before_ref, g4_ref, p_ref, row_ref, part_ref):
@@ -240,7 +260,7 @@
 
     def work():
         factor = row_ref[i, distance : distance + 1, :]
-        part_ref[...] = value_grad(distance, g4_ref.at[i], p_ref.at[i], factor).astype(part_ref.dtype)
+        part_ref[...] = value_grad(case_of(distance), g4_ref.at[i], p_ref.at[i], factor).astype(part_ref.dtype)
 
     def other():
         part_ref[...] = jnp.zeros_like(part_ref)
@@ -254,7 +274,7 @@
 
     def work():
         dk, dq = key_query_grad(
-            distance,
+            case_of(distance),
             k_ref[...],
             q4_ref.at[i],
             p_ref.at[i],
@@ -297,15 +317,17 @@
 DPROBS = held(TOK, WIDE, F32)
 STATS = held(8, WIDE, F32)
 QUERY_GRAD = held(HEAD_DIM, WIDE, F32)
+FAR_KEY = pl.BlockSpec((TOK, FAR_GROUPS * HEAD_DIM), lambda i: (0, i))
 PART = KEY, jax.ShapeDtypeStruct((TOK, KV_HEADS * HEAD_DIM), BF)
+FAR_PART = FAR_KEY, PART[1]
 OWN = KEY, jax.ShapeDtypeStruct((TOK, KV_HEADS * HEAD_DIM), F32)
 QUERY_OUT = QUERY, jax.ShapeDtypeStruct((TOK, KV_HEADS * GROUP * HEAD_DIM), BF)
 
 
-def call(kernel, in_specs, outs, matmuls, args, scratch=()):
+def call(kernel, in_specs, outs, matmuls, args, scratch=(), steps=KV_HEADS):
     return pl.pallas_call(
         kernel,
-        grid=(KV_HEADS,),
+        grid=(steps,),
         in_specs=in_specs,
         out_specs=[spec for spec, _ in outs],
         out_shape=[shape for _, shape in outs],
@@ -342,22 +364,24 @@
 def far_value(before, start, q4, g4, k, *stats):
     return call(
         far_value_kernel,
-        [SMEM, START, HELD, HELD, KEY, HELD, HELD, HELD],
-        [PART, PROBS, STATS],
+        [SMEM, START, HELD, HELD, FAR_KEY, HELD, HELD, HELD],
+        [FAR_PART, PROBS, STATS],
         2,
         (before, start, q4, g4, k, *stats),
-        [pltpu.VMEM((8, WIDE), F32)],
+        [pltpu.VMEM((FAR_GROUPS, 8, WIDE), F32)],
+        KV_HEADS // FAR_GROUPS,
     )
 
 
 def far_key(before, q4, g4, k, v, p, row, *sums):
     return call(
         far_key_kernel,
-        [SMEM, HELD, HELD, KEY, KEY] + [HELD] * 5,
-        [PART, QUERY_GRAD, STATS],
+        [SMEM, HELD, HELD, FAR_KEY, FAR_KEY] + [HELD] * 5,
+        [FAR_PART, QUERY_GRAD, STATS],
         3,
         (before, q4, g4, k, v, p, row, *sums),
-        [pltpu.VMEM((TOK, WIDE), F32), pltpu.VMEM((8, WIDE), F32)],
+        [pltpu.VMEM((FAR_GROUPS, TOK, WIDE), F32), pltpu.VMEM((FAR_GROUPS, 8, WIDE), F32)],
+        KV_HEADS // FAR_GROUPS,
     )
 
 

time: 98.2 us -> 96.5 us (0.983)
  starting transfers between devices: 50.5 us -> 39.7 us
  Pallas kernels: 18.7 us -> 27.5 us
    ppermute x12, starting transfers between devices: 50.5 us -> 39.7 us  [shift(): return lax.ppermute(x, ('dp', 'ctx'), route)]
    pallas_call x14, Pallas kernels: 18.7 us -> 27.5 us  [call(): pl.pallas_call(kernel, grid=(steps,), in_specs=in_specs, out_specs=[spec...]
  transfers between devices with their start and end apart: 12 -> 12, of which waited for: 5 -> 6; matrix products, arithmetic and copies ran while one was open for 3% -> 3% of each run, Pallas kernels for 19% -> 29%
where the time goes in v3:
time: 96.5 us; the launch traced here: 95.9 us
  starting transfers between devices  39.7 us (41%)
  Pallas kernels  27.5 us (28%)
  waiting for transfers between devices  23.4 us (24%)
  other arithmetic  2.38 us (2%)
  between operations  1.57 us (2%)
  local copies, waits for them, and re-layouts  1.4 us (1%)
    ppermute x12, starting transfers between devices, shift(): return lax.ppermute(x, ('dp', 'ctx'), route)  39.7 us
    pallas_call x14, Pallas kernels, call(): pl.pallas_call(kernel, grid=(steps,), in_specs=in_specs, out_specs=[spec...  27.5 us
    ppermute x12, waiting for transfers between devices, shift(): return lax.ppermute(x, ('dp', 'ctx'), route)  23.4 us
  transfers between devices with their start and end apart: 12, of which 6 were waited for; matrix products, arithmetic and copies ran while one was open for 3% of the time, Pallas kernels for 29%

profile of v3, /device:TPU:6, one launch (start us, length us, event | category | flops | bytes accessed | tf_op | source)
XLA Modules:
  0.0 95.9 jit_solution(11200213830812990491)
XLA Ops:
  0.6 3.8 %collective-permute-start.1 = (bf16[256,512]{1,0:T(8,128)(2,1)}, bf16[256,512]{1,0:T(8,128)(2,1)S(1)}, u32[]{:S(2)}, u32[]{:S(2)}) collective-permute-start(bf16[256,512]{1,0:T(8,128)(2,1)} %k_ref.3), channel_id=1, source_target_pairs={{0,1},{1,2},{2,3},{3,4},{4,5},{5,6},{6,7},{7,8},{8,9},{9,10},{10,1... | collective-permute-start | bytes 786440 | tf_op jit(solution)/shard_map/ppermute | solution.py:411
  4.5 0.7 pad_bitcast_fusion
  5.2 0.3 reduce-window.9
  5.5 0.1 slice.13
  5.6 0.1 slice_reduce_fusion
  5.7 0.1 add_bitcast_fusion
  5.8 0.1 select_reduce_fusion
  5.9 3.8 %collective-permute-start = (bf16[256,512]{1,0:T(8,128)(2,1)}, bf16[256,512]{1,0:T(8,128)(2,1)S(1)}, u32[]{:S(2)}, u32[]{:S(2)}) collective-permute-start(bf16[256,512]{1,0:T(8,128)(2,1)} %v_ref.1), channel_id=1, source_target_pairs={{0,1},{1,2},{2,3},{3,4},{4,5},{5,6},{6,7},{7,8},{8,9},{9,10},{10,1... | collective-permute-start | bytes 786440 | tf_op jit(solution)/shard_map/ppermute | solution.py:411
  9.8 0.5 slice.16
  10.9 3.3 %shard_map.76 = (bf16[4,1024,128]{2,1,0:T(8,128)(2,1)S(1)}, bf16[4,256,1024]{2,1,0:T(8,128)(2,1)S(1)}, f32[4,8,1024]{2,1,0:T(8,128)S(1)}) custom-call(s32[1]{0:T(128)S(6)} %max.3.before_ref, s32[1,256]{1,0:T(1,128)S(1)} %bitcast.6, bf16[256,2048]{1,0:T(8,128)(2,1)} %q_ref.1, bf16[256,512]{1,0:T(8,128)(2,1)} %k_ref.3), custom_call_target="tpu_custom_call" | custom-call | flops 268435456 | bytes 1048576 | tf_op jit(solution)/shard_map/pallas_call | solution.py:328
  14.2 7.8 %collective-permute-done.1.k_ref = bf16[256,512]{1,0:T(8,128)(2,1)S(1)} collective-permute-done((bf16[256,512]{1,0:T(8,128)(2,1)}, bf16[256,512]{1,0:T(8,128)(2,1)S(1)}, u32[]{:S(2)}, u32[]{:S(2)}) %collective-permute-start.1) | collective-permute-done | bytes 262176 | tf_op jit(solution)/shard_map/ppermute | solution.py:411
  22.0 1.9 %collective-permute-start.2 = (bf16[256,512]{1,0:T(8,128)(2,1)S(1)}, bf16[256,512]{1,0:T(8,128)(2,1)S(1)}, u32[]{:S(2)}, u32[]{:S(2)}) collective-permute-start(bf16[256,512]{1,0:T(8,128)(2,1)S(1)} %collective-permute-done.1.k_ref), channel_id=1, source_target_pairs={{0,1},{1,2},{2,3},{3,4},{4,5},{5,6},{6,7},{7,8},{8,9},{9,10},{10,1... | collective-permute-start | bytes 786440 | tf_op jit(solution)/shard_map/ppermute | solution.py:411
  23.9 2.2 %shard_map.77 = (bf16[4,256,1024]{2,1,0:T(8,128)(2,1)S(1)}, f32[4,8,1024]{2,1,0:T(8,128)S(1)}) custom-call(s32[1]{0:T(128)S(6)} %max.3.before_ref, s32[1,256]{1,0:T(1,128)S(1)} %bitcast.7, bf16[4,1024,128]{2,1,0:T(8,128)(2,1)S(1)} %get-tuple-element.48.q_ref.q4_ref, bf16[256,512]{1,0:T(8,128)(2,1)S(1)} %collective-permute-done.1.k_ref), custom_call_target="tpu_custom_call" | custom-call | flops 268435456 | bytes 1048576 | tf_op jit(solution)/shard_map/pallas_call | solution.py:328
  26.1 0.8 collective-permute-done.v_ref
  26.9 1.9 %collective-permute-start.4 = (bf16[256,512]{1,0:T(8,128)(2,1)S(1)}, bf16[256,512]{1,0:T(8,128)(2,1)S(1)}, u32[]{:S(2)}, u32[]{:S(2)}) collective-permute-start(bf16[256,512]{1,0:T(8,128)(2,1)S(1)} %collective-permute-done.v_ref), channel_id=1, source_target_pairs={{0,1},{1,2},{2,3},{3,4},{4,5},{5,6},{6,7},{7,8},{8,9},{9,10},{10,1... | collective-permute-start | bytes 786440 | tf_op jit(solution)/shard_map/ppermute | solution.py:411
  28.8 2.9 %shard_map.78 = (bf16[4,1024,128]{2,1,0:T(8,128)(2,1)S(1)}, f32[4,256,1024]{2,1,0:T(8,128)S(1)}, f32[4,8,1024]{2,1,0:T(8,128)S(1)}) custom-call(s32[1]{0:T(128)S(6)} %max.3.before_ref, bf16[256,2048]{1,0:T(8,128)(2,1)} %g_ref, bf16[256,512]{1,0:T(8,128)(2,1)} %v_ref.1, bf16[4,256,1024]{2,1,0:T(8,128)(2,1)S(1)} %get-tuple-element.49.p_ref), custom_call_target="tpu_custom_call" | custom-call | flops 268435456 | bytes 1048576 | tf_op jit(solution)/shard_map/pallas_call | solution.py:328
  31.7 1.4 %shard_map.79 = (f32[4,256,1024]{2,1,0:T(8,128)S(1)}, f32[4,8,1024]{2,1,0:T(8,128)S(1)}) custom-call(s32[1]{0:T(128)S(6)} %max.3.before_ref, bf16[4,1024,128]{2,1,0:T(8,128)(2,1)S(1)} %get-tuple-element.57.g_ref.g4_ref, bf16[256,512]{1,0:T(8,128)(2,1)S(1)} %collective-permute-done.v_ref, bf16[4,256,1024]{2,1,0:T(8,128)(2,1)S(1)} %get-tuple-element.58.p_ref), custom_call_target="tpu_custom_call" | custom-call | flops 268435456 | bytes 1048576 | tf_op jit(solution)/shard_map/pallas_call | solution.py:328
  33.1 4.8 %collective-permute-done.2.k_ref = bf16[256,512]{1,0:T(8,128)(2,1)S(1)} collective-permute-done((bf16[256,512]{1,0:T(8,128)(2,1)S(1)}, bf16[256,512]{1,0:T(8,128)(2,1)S(1)}, u32[]{:S(2)}, u32[]{:S(2)}) %collective-permute-start.2) | collective-permute-done | bytes 262176 | tf_op jit(solution)/shard_map/ppermute | solution.py:411
  37.9 1.9 %collective-permute-start.3 = (bf16[256,512]{1,0:T(8,128)(2,1)S(1)}, bf16[256,512]{1,0:T(8,128)(2,1)S(1)}, u32[]{:S(2)}, u32[]{:S(2)}) collective-permute-start(bf16[256,512]{1,0:T(8,128)(2,1)S(1)} %collective-permute-done.2.k_ref), channel_id=1, source_target_pairs={{0,1},{1,2},{2,3},{3,4},{4,5},{5,6},{6,7},{7,8},{8,9},{9,10},{10,1... | collective-permute-start | bytes 786440 | tf_op jit(solution)/shard_map/ppermute | solution.py:411
  39.8 2.2 %shard_map.80 = (bf16[4,256,1024]{2,1,0:T(8,128)(2,1)S(1)}, f32[4,8,1024]{2,1,0:T(8,128)S(1)}) custom-call(s32[1]{0:T(128)S(6)} %max.3.before_ref, s32[1,256]{1,0:T(1,128)S(1)} %bitcast.8, bf16[4,1024,128]{2,1,0:T(8,128)(2,1)S(1)} %get-tuple-element.48.q_ref.q4_ref, bf16[256,512]{1,0:T(8,128)(2,1)S(1)} %collective-permute-done.2.k_ref), custom_call_target="tpu_custom_call" | custom-call | flops 268435456 | bytes 1048576 | tf_op jit(solution)/shard_map/pallas_call | solution.py:328
  42.0 0.8 collective-permute-done.4.v_ref
  42.8 1.9 %collective-permute-start.5 = (bf16[256,512]{1,0:T(8,128)(2,1)S(1)}, bf16[256,512]{1,0:T(8,128)(2,1)S(1)}, u32[]{:S(2)}, u32[]{:S(2)}) collective-permute-start(bf16[256,512]{1,0:T(8,128)(2,1)S(1)} %collective-permute-done.4.v_ref), channel_id=1, source_target_pairs={{0,1},{1,2},{2,3},{3,4},{4,5},{5,6},{6,7},{7,8},{8,9},{9,10},{10,1... | collective-permute-start | bytes 786440 | tf_op jit(solution)/shard_map/ppermute | solution.py:411
  44.7 1.4 %shard_map.81 = (f32[4,256,1024]{2,1,0:T(8,128)S(1)}, f32[4,8,1024]{2,1,0:T(8,128)S(1)}) custom-call(s32[1]{0:T(128)S(6)} %max.3.before_ref, bf16[4,1024,128]{2,1,0:T(8,128)(2,1)S(1)} %get-tuple-element.57.g_ref.g4_ref, bf16[256,512]{1,0:T(8,128)(2,1)S(1)} %collective-permute-done.4.v_ref, bf16[4,256,1024]{2,1,0:T(8,128)(2,1)S(1)} %get-tuple-element.63.p_ref), custom_call_target="tpu_custom_call" | custom-call | flops 268435456 | bytes 1048576 | tf_op jit(solution)/shard_map/pallas_call | solution.py:328
  46.1 5.9 %collective-permute-done.3.k_ref = bf16[256,512]{1,0:T(8,128)(2,1)S(1)} collective-permute-done((bf16[256,512]{1,0:T(8,128)(2,1)S(1)}, bf16[256,512]{1,0:T(8,128)(2,1)S(1)}, u32[]{:S(2)}, u32[]{:S(2)}) %collective-permute-start.3) | collective-permute-done | bytes 262176 | tf_op jit(solution)/shard_map/ppermute | solution.py:411
  52.0 2.1 %shard_map.82 = (bf16[256,512]{1,0:T(8,128)(2,1)S(1)}, bf16[4,256,1024]{2,1,0:T(8,128)(2,1)S(1)}, f32[4,8,1024]{2,1,0:T(8,128)S(1)}) custom-call(s32[1]{0:T(128)S(6)} %max.3.before_ref, s32[1,256]{1,0:T(1,128)S(1)} %bitcast.9, bf16[4,1024,128]{2,1,0:T(8,128)(2,1)S(1)} %get-tuple-element.48.q_ref.q4_ref, ...), custom_call_target="tpu_custom_call" | custom-call | flops 536870912 | bytes 1048576 | tf_op jit(solution)/shard_map/pallas_call | solution.py:328
  54.1 1.9 %collective-permute-start.7 = (bf16[256,512]{1,0:T(8,128)(2,1)S(1)}, bf16[256,512]{1,0:T(8,128)(2,1)S(1)}, u32[]{:S(2)}, u32[]{:S(2)}) collective-permute-start(bf16[256,512]{1,0:T(8,128)(2,1)S(1)} %get-tuple-element.67), channel_id=1, source_target_pairs={{1,0},{2,1},{3,2},{4,3},{5,4},{6,5},{7,6},{8,7},{9,8},{10,9},{11,1... | collective-permute-start | bytes 786440 | tf_op jit(solution)/shard_map/ppermute | solution.py:411
  56.0 0.0 collective-permute-done.5.v_ref
  56.0 2.0 %shard_map.83 = (bf16[256,512]{1,0:T(8,128)(2,1)S(1)}, f32[4,128,1024]{2,1,0:T(8,128)S(1)}, f32[4,8,1024]{2,1,0:T(8,128)S(1)}) custom-call(s32[1]{0:T(128)S(6)} %max.3.before_ref, bf16[4,1024,128]{2,1,0:T(8,128)(2,1)S(1)} %get-tuple-element.48.q_ref.q4_ref, bf16[4,1024,128]{2,1,0:T(8,128)(2,1)S(1)} %get-tuple-element.57.g_ref.g4_ref, ...), custom_call_target="tpu_custom_call" | custom-call | flops 805306368 | bytes 1048576 | tf_op jit(solution)/shard_map/pallas_call | solution.py:328
  58.0 1.9 %collective-permute-start.6 = (bf16[256,512]{1,0:T(8,128)(2,1)S(1)}, bf16[256,512]{1,0:T(8,128)(2,1)S(1)}, u32[]{:S(2)}, u32[]{:S(2)}) collective-permute-start(bf16[256,512]{1,0:T(8,128)(2,1)S(1)} %get-tuple-element.71), channel_id=1, source_target_pairs={{1,0},{2,1},{3,2},{4,3},{5,4},{6,5},{7,6},{8,7},{9,8},{10,9},{11,1... | collective-permute-start | bytes 786440 | tf_op jit(solution)/shard_map/ppermute | solution.py:411
  59.9 1.3 %shard_map.84 = bf16[256,512]{1,0:T(8,128)(2,1)S(1)} custom-call(s32[1]{0:T(128)S(6)} %max.3.before_ref, bf16[4,1024,128]{2,1,0:T(8,128)(2,1)S(1)} %get-tuple-element.57.g_ref.g4_ref, bf16[4,256,1024]{2,1,0:T(8,128)(2,1)S(1)} %get-tuple-element.63.p_ref, f32[4,8,1024]{2,1,0:T(8,128)S(1)} %get-tuple-element.88.row_ref), custom_call_target="tpu_custom_call" | custom-call | flops 268435456 | bytes 1048576 | tf_op jit(solution)/shard_map/pallas_call | solution.py:328
  61.3 3.4 %collective-permute-done.7 = bf16[256,512]{1,0:T(8,128)(2,1)S(1)} collective-permute-done((bf16[256,512]{1,0:T(8,128)(2,1)S(1)}, bf16[256,512]{1,0:T(8,128)(2,1)S(1)}, u32[]{:S(2)}, u32[]{:S(2)}) %collective-permute-start.7) | collective-permute-done | bytes 262176 | tf_op jit(solution)/shard_map/ppermute | solution.py:411
  64.7 0.1 add_convert_fusion.5
  64.8 5.0 %collective-permute-start.9 = (bf16[256,512]{1,0:T(8,128)(2,1)S(1)}, bf16[256,512]{1,0:T(8,128)(2,1)S(1)}, u32[]{:S(2)}, u32[]{:S(2)}) collective-permute-start(bf16[256,512]{1,0:T(8,128)(2,1)S(1)} %add_convert_fusion.5), channel_id=1, source_target_pairs={{1,0},{2,1},{3,2},{4,3},{5,4},{6,5},{7,6},{8,7},{9,8},{10,9},{11,1... | collective-permute-start | bytes 786440 | tf_op jit(solution)/shard_map/ppermute | solution.py:411
  69.8 1.7 %shard_map.85 = (bf16[256,512]{1,0:T(8,128)(2,1)S(1)}, f32[4,128,1024]{2,1,0:T(8,128)S(1)}) custom-call(s32[1]{0:T(128)S(6)} %max.3.before_ref, bf16[4,1024,128]{2,1,0:T(8,128)(2,1)S(1)} %get-tuple-element.48.q_ref.q4_ref, bf16[256,512]{1,0:T(8,128)(2,1)S(1)} %collective-permute-done.2.k_ref, bf16[4,256,1024]{2,1,0:T(8,128)(2,1)S(1)} %get-tuple-element.63.p_ref, ...), custom_call_target="tpu_custom_call" | custom-call | flops 536870912 | bytes 1048576 | tf_op jit(solution)/shard_map/pallas_call | solution.py:328
  71.5 0.0 collective-permute-done.6
  71.5 0.1 add_convert_fusion.4
  71.6 3.8 %collective-permute-start.8 = (bf16[256,512]{1,0:T(8,128)(2,1)S(1)}, bf16[256,512]{1,0:T(8,128)(2,1)S(1)}, u32[]{:S(2)}, u32[]{:S(2)}) collective-permute-start(bf16[256,512]{1,0:T(8,128)(2,1)S(1)} %add_convert_fusion.4), channel_id=1, source_target_pairs={{1,0},{2,1},{3,2},{4,3},{5,4},{6,5},{7,6},{8,7},{9,8},{10,9},{11,1... | collective-permute-start | bytes 786440 | tf_op jit(solution)/shard_map/ppermute | solution.py:411
  75.4 1.3 %shard_map.86 = bf16[256,512]{1,0:T(8,128)(2,1)S(1)} custom-call(s32[1]{0:T(128)S(6)} %max.3.before_ref, bf16[4,1024,128]{2,1,0:T(8,128)(2,1)S(1)} %get-tuple-element.57.g_ref.g4_ref, bf16[4,256,1024]{2,1,0:T(8,128)(2,1)S(1)} %get-tuple-element.58.p_ref, f32[4,8,1024]{2,1,0:T(8,128)S(1)} %get-tuple-element.88.row_ref), custom_call_target="tpu_custom_call" | custom-call | flops 268435456 | bytes 1048576 | tf_op jit(solution)/shard_map/pallas_call | solution.py:328
  76.7 0.1 add_convert_fusion.3
  76.8 6.3 %collective-permute-start.11 = (bf16[256,512]{1,0:T(8,128)(2,1)S(1)}, bf16[256,512]{1,0:T(8,128)(2,1)S(1)}, u32[]{:S(2)}, u32[]{:S(2)}) collective-permute-start(bf16[256,512]{1,0:T(8,128)(2,1)S(1)} %add_convert_fusion.3), channel_id=1, source_target_pairs={{1,0},{2,1},{3,2},{4,3},{5,4},{6,5},{7,6},{8,7},{9,8},{10,9},{11,1... | collective-permute-start | bytes 786440 | tf_op jit(solution)/shard_map/ppermute | solution.py:411
  83.1 1.7 %shard_map.87 = (bf16[256,512]{1,0:T(8,128)(2,1)S(1)}, f32[4,128,1024]{2,1,0:T(8,128)S(1)}) custom-call(s32[1]{0:T(128)S(6)} %max.3.before_ref, bf16[4,1024,128]{2,1,0:T(8,128)(2,1)S(1)} %get-tuple-element.48.q_ref.q4_ref, bf16[256,512]{1,0:T(8,128)(2,1)S(1)} %collective-permute-done.1.k_ref, bf16[4,256,1024]{2,1,0:T(8,128)(2,1)S(1)} %get-tuple-element.58.p_ref, ...), custom_call_target="tpu_custom_call" | custom-call | flops 536870912 | bytes 1048576 | tf_op jit(solution)/shard_map/pallas_call | solution.py:328
  84.9 0.1 add_convert_fusion.2
  84.9 0.0 copy-start
  84.9 5.4 %collective-permute-start.10 = (bf16[256,512]{1,0:T(8,128)(2,1)S(1)}, bf16[256,512]{1,0:T(8,128)(2,1)S(1)}, u32[]{:S(2)}, u32[]{:S(2)}) collective-permute-start(bf16[256,512]{1,0:T(8,128)(2,1)S(1)} %add_convert_fusion.2), channel_id=1, source_target_pairs={{1,0},{2,1},{3,2},{4,3},{5,4},{6,5},{7,6},{8,7},{9,8},{10,9},{11,1... | collective-permute-start | bytes 786440 | tf_op jit(solution)/shard_map/ppermute | solution.py:411
  90.4 1.1 %shard_map.88 = f32[256,512]{1,0:T(8,128)S(1)} custom-call(s32[1]{0:T(128)S(6)} %max.3.before_ref, bf16[4,1024,128]{2,1,0:T(8,128)(2,1)S(1)} %get-tuple-element.57.g_ref.g4_ref, bf16[4,256,1024]{2,1,0:T(8,128)(2,1)S(1)} %get-tuple-element.49.p_ref, f32[4,8,1024]{2,1,0:T(8,128)S(1)} %get-tuple-element.88.row_ref), custom_call_target="tpu_custom_call" | custom-call | flops 268435456 | bytes 1048576 | tf_op jit(solution)/shard_map/pallas_call | solution.py:328
  91.5 2.9 %shard_map.89 = (f32[256,512]{1,0:T(8,128)S(1)}, bf16[256,2048]{1,0:T(8,128)(2,1)}) custom-call(s32[1]{0:T(128)S(6)} %max.3.before_ref, bf16[4,1024,128]{2,1,0:T(8,128)(2,1)S(1)} %get-tuple-element.48.q_ref.q4_ref, bf16[256,512]{1,0:T(8,128)(2,1)S(1)} %copy-done, bf16[4,256,1024]{2,1,0:T(8,128)(2,1)S(1)} %get-tuple-element.49.p_ref, ...), custom_call_target="tpu_custom_call" | custom-call | flops 536870912 | bytes 1048576 | tf_op jit(solution)/shard_map/pallas_call | solution.py:328
  94.4 0.8 add_convert_fusion
  95.2 0.8 add_convert_fusion.1
  (8 shorter events, 0.1 us)
Async XLA Ops:
  0.6 21.4 %collective-permute-start.1 = (bf16[256,512]{1,0:T(8,128)(2,1)}, bf16[256,512]{1,0:T(8,128)(2,1)S(1)}, u32[]{:S(2)}, u32[]{:S(2)}) collective-permute-start(bf16[256,512]{1,0:T(8,128)(2,1)} %k_ref.3), channel_id=1, source_target_pairs={{0,1},{1,2},{2,3},{3,4},{4,5},{5,6},{6,7},{7,8},{8,9},{9,10},{10,1... | collective-permute-start | bytes 786440 | tf_op jit(solution)/shard_map/ppermute | solution.py:411
  5.9 20.9 %collective-permute-start = (bf16[256,512]{1,0:T(8,128)(2,1)}, bf16[256,512]{1,0:T(8,128)(2,1)S(1)}, u32[]{:S(2)}, u32[]{:S(2)}) collective-permute-start(bf16[256,512]{1,0:T(8,128)(2,1)} %v_ref.1), channel_id=1, source_target_pairs={{0,1},{1,2},{2,3},{3,4},{4,5},{5,6},{6,7},{7,8},{8,9},{9,10},{10,1... | collective-permute-start | bytes 786440 | tf_op jit(solution)/shard_map/ppermute | solution.py:411
  22.0 15.9 %collective-permute-start.2 = (bf16[256,512]{1,0:T(8,128)(2,1)S(1)}, bf16[256,512]{1,0:T(8,128)(2,1)S(1)}, u32[]{:S(2)}, u32[]{:S(2)}) collective-permute-start(bf16[256,512]{1,0:T(8,128)(2,1)S(1)} %collective-permute-done.1.k_ref), channel_id=1, source_target_pairs={{0,1},{1,2},{2,3},{3,4},{4,5},{5,6},{6,7},{7,8},{8,9},{9,10},{10,1... | collective-permute-start | bytes 786440 | tf_op jit(solution)/shard_map/ppermute | solution.py:411
  26.9 15.9 %collective-permute-start.4 = (bf16[256,512]{1,0:T(8,128)(2,1)S(1)}, bf16[256,512]{1,0:T(8,128)(2,1)S(1)}, u32[]{:S(2)}, u32[]{:S(2)}) collective-permute-start(bf16[256,512]{1,0:T(8,128)(2,1)S(1)} %collective-permute-done.v_ref), channel_id=1, source_target_pairs={{0,1},{1,2},{2,3},{3,4},{4,5},{5,6},{6,7},{7,8},{8,9},{9,10},{10,1... | collective-permute-start | bytes 786440 | tf_op jit(solution)/shard_map/ppermute | solution.py:411
  37.9 14.1 %collective-permute-start.3 = (bf16[256,512]{1,0:T(8,128)(2,1)S(1)}, bf16[256,512]{1,0:T(8,128)(2,1)S(1)}, u32[]{:S(2)}, u32[]{:S(2)}) collective-permute-start(bf16[256,512]{1,0:T(8,128)(2,1)S(1)} %collective-permute-done.2.k_ref), channel_id=1, source_target_pairs={{0,1},{1,2},{2,3},{3,4},{4,5},{5,6},{6,7},{7,8},{8,9},{9,10},{10,1... | collective-permute-start | bytes 786440 | tf_op jit(solution)/shard_map/ppermute | solution.py:411
  42.8 13.2 %collective-permute-start.5 = (bf16[256,512]{1,0:T(8,128)(2,1)S(1)}, bf16[256,512]{1,0:T(8,128)(2,1)S(1)}, u32[]{:S(2)}, u32[]{:S(2)}) collective-permute-start(bf16[256,512]{1,0:T(8,128)(2,1)S(1)} %collective-permute-done.4.v_ref), channel_id=1, source_target_pairs={{0,1},{1,2},{2,3},{3,4},{4,5},{5,6},{6,7},{7,8},{8,9},{9,10},{10,1... | collective-permute-start | bytes 786440 | tf_op jit(solution)/shard_map/ppermute | solution.py:411
  54.1 10.6 %collective-permute-start.7 = (bf16[256,512]{1,0:T(8,128)(2,1)S(1)}, bf16[256,512]{1,0:T(8,128)(2,1)S(1)}, u32[]{:S(2)}, u32[]{:S(2)}) collective-permute-start(bf16[256,512]{1,0:T(8,128)(2,1)S(1)} %get-tuple-element.67), channel_id=1, source_target_pairs={{1,0},{2,1},{3,2},{4,3},{5,4},{6,5},{7,6},{8,7},{9,8},{10,9},{11,1... | collective-permute-start | bytes 786440 | tf_op jit(solution)/shard_map/ppermute | solution.py:411
  58.0 13.5 %collective-permute-start.6 = (bf16[256,512]{1,0:T(8,128)(2,1)S(1)}, bf16[256,512]{1,0:T(8,128)(2,1)S(1)}, u32[]{:S(2)}, u32[]{:S(2)}) collective-permute-start(bf16[256,512]{1,0:T(8,128)(2,1)S(1)} %get-tuple-element.71), channel_id=1, source_target_pairs={{1,0},{2,1},{3,2},{4,3},{5,4},{6,5},{7,6},{8,7},{9,8},{10,9},{11,1... | collective-permute-start | bytes 786440 | tf_op jit(solution)/shard_map/ppermute | solution.py:411
  64.8 12.0 %collective-permute-start.9 = (bf16[256,512]{1,0:T(8,128)(2,1)S(1)}, bf16[256,512]{1,0:T(8,128)(2,1)S(1)}, u32[]{:S(2)}, u32[]{:S(2)}) collective-permute-start(bf16[256,512]{1,0:T(8,128)(2,1)S(1)} %add_convert_fusion.5), channel_id=1, source_target_pairs={{1,0},{2,1},{3,2},{4,3},{5,4},{6,5},{7,6},{8,7},{9,8},{10,9},{11,1... | collective-permute-start | bytes 786440 | tf_op jit(solution)/shard_map/ppermute | solution.py:411
  71.6 13.3 %collective-permute-start.8 = (bf16[256,512]{1,0:T(8,128)(2,1)S(1)}, bf16[256,512]{1,0:T(8,128)(2,1)S(1)}, u32[]{:S(2)}, u32[]{:S(2)}) collective-permute-start(bf16[256,512]{1,0:T(8,128)(2,1)S(1)} %add_convert_fusion.4), channel_id=1, source_target_pairs={{1,0},{2,1},{3,2},{4,3},{5,4},{6,5},{7,6},{8,7},{9,8},{10,9},{11,1... | collective-permute-start | bytes 786440 | tf_op jit(solution)/shard_map/ppermute | solution.py:411
  76.8 17.6 %collective-permute-start.11 = (bf16[256,512]{1,0:T(8,128)(2,1)S(1)}, bf16[256,512]{1,0:T(8,128)(2,1)S(1)}, u32[]{:S(2)}, u32[]{:S(2)}) collective-permute-start(bf16[256,512]{1,0:T(8,128)(2,1)S(1)} %add_convert_fusion.3), channel_id=1, source_target_pairs={{1,0},{2,1},{3,2},{4,3},{5,4},{6,5},{7,6},{8,7},{9,8},{10,9},{11,1... | collective-permute-start | bytes 786440 | tf_op jit(solution)/shard_map/ppermute | solution.py:411
  84.9 6.6 %copy-start = (bf16[256,512]{1,0:T(8,128)(2,1)S(1)}, bf16[256,512]{1,0:T(8,128)(2,1)}, u32[]{:S(2)}) copy-start(bf16[256,512]{1,0:T(8,128)(2,1)} %k_ref.3) | copy-start | bytes 786436
  84.9 10.2 %collective-permute-start.10 = (bf16[256,512]{1,0:T(8,128)(2,1)S(1)}, bf16[256,512]{1,0:T(8,128)(2,1)S(1)}, u32[]{:S(2)}, u32[]{:S(2)}) collective-permute-start(bf16[256,512]{1,0:T(8,128)(2,1)S(1)} %add_convert_fusion.2), channel_id=1, source_target_pairs={{1,0},{2,1},{3,2},{4,3},{5,4},{6,5},{7,6},{8,7},{9,8},{10,9},{11,1... | collective-permute-start | bytes 786440 | tf_op jit(solution)/shard_map/ppermute | solution.py:411

commit v4 on v3

--- a/solution.py
+++ b/solution.py
@@ -13,7 +13,7 @@
 HALF = 128
 GROUP = 4
 KV_HEADS = 4
-FAR_GROUPS = 2
+FAR_GROUPS = 4
 LANES = GROUP * HALF
 WIDE = 2 * LANES
 SCALE = HEAD_DIM**-0.5

time: 96.5 us -> 95.5 us (0.990)
  Pallas kernels: 27.5 us -> 23.6 us
  waiting for transfers between devices: 23.4 us -> 25.7 us
    pallas_call x14, Pallas kernels: 27.5 us -> 23.6 us  [call(): pl.pallas_call(kernel, grid=(steps,), in_specs=in_specs, out_specs=[spec...]
    ppermute x12, waiting for transfers between devices: 23.4 us -> 25.7 us  [shift(): return lax.ppermute(x, ('dp', 'ctx'), route)]
  transfers between devices with their start and end apart: 12 -> 12, of which waited for: 6 -> 7; matrix products, arithmetic and copies ran while one was open for 3% -> 3% of each run, Pallas kernels for 29% -> 25%
where the time goes in v4:
time: 95.5 us; the launch traced here: 94.4 us
  starting transfers between devices  39.7 us (42%)
  waiting for transfers between devices  25.7 us (27%)
  Pallas kernels  23.6 us (25%)
  other arithmetic  2.38 us (2%)
  between operations  1.56 us (2%)
  local copies, waits for them, and re-layouts  1.4 us (1%)
    ppermute x12, starting transfers between devices, shift(): return lax.ppermute(x, ('dp', 'ctx'), route)  39.7 us
    ppermute x12, waiting for transfers between devices, shift(): return lax.ppermute(x, ('dp', 'ctx'), route)  25.7 us
    pallas_call x14, Pallas kernels, call(): pl.pallas_call(kernel, grid=(steps,), in_specs=in_specs, out_specs=[spec...  23.6 us
  transfers between devices with their start and end apart: 12, of which 7 were waited for; matrix products, arithmetic and copies ran while one was open for 3% of the time, Pallas kernels for 25%

profile of v4, /device:TPU:6, one launch (start us, length us, event | category | flops | bytes accessed | tf_op | source)
XLA Modules:
  0.0 94.4 jit_solution(7882384712726561604)
XLA Ops:
  0.6 3.8 %collective-permute-start.1 = (bf16[256,512]{1,0:T(8,128)(2,1)}, bf16[256,512]{1,0:T(8,128)(2,1)S(1)}, u32[]{:S(2)}, u32[]{:S(2)}) collective-permute-start(bf16[256,512]{1,0:T(8,128)(2,1)} %k_ref.3), channel_id=1, source_target_pairs={{0,1},{1,2},{2,3},{3,4},{4,5},{5,6},{6,7},{7,8},{8,9},{9,10},{10,1... | collective-permute-start | bytes 786440 | tf_op jit(solution)/shard_map/ppermute | solution.py:411
  4.5 0.7 pad_bitcast_fusion
  5.2 0.3 reduce-window.9
  5.5 0.1 slice.13
  5.6 0.1 slice_reduce_fusion
  5.7 0.1 add_bitcast_fusion
  5.8 0.1 select_reduce_fusion
  5.9 3.8 %collective-permute-start = (bf16[256,512]{1,0:T(8,128)(2,1)}, bf16[256,512]{1,0:T(8,128)(2,1)S(1)}, u32[]{:S(2)}, u32[]{:S(2)}) collective-permute-start(bf16[256,512]{1,0:T(8,128)(2,1)} %v_ref.1), channel_id=1, source_target_pairs={{0,1},{1,2},{2,3},{3,4},{4,5},{5,6},{6,7},{7,8},{8,9},{9,10},{10,1... | collective-permute-start | bytes 786440 | tf_op jit(solution)/shard_map/ppermute | solution.py:411
  9.8 0.5 slice.16
  10.9 3.3 %shard_map.76 = (bf16[4,1024,128]{2,1,0:T(8,128)(2,1)S(1)}, bf16[4,256,1024]{2,1,0:T(8,128)(2,1)S(1)}, f32[4,8,1024]{2,1,0:T(8,128)S(1)}) custom-call(s32[1]{0:T(128)S(6)} %max.3.before_ref, s32[1,256]{1,0:T(1,128)S(1)} %bitcast.6, bf16[256,2048]{1,0:T(8,128)(2,1)} %q_ref.1, bf16[256,512]{1,0:T(8,128)(2,1)} %k_ref.3), custom_call_target="tpu_custom_call" | custom-call | flops 268435456 | bytes 1048576 | tf_op jit(solution)/shard_map/pallas_call | solution.py:328
  14.2 7.8 %collective-permute-done.1.k_ref = bf16[256,512]{1,0:T(8,128)(2,1)S(1)} collective-permute-done((bf16[256,512]{1,0:T(8,128)(2,1)}, bf16[256,512]{1,0:T(8,128)(2,1)S(1)}, u32[]{:S(2)}, u32[]{:S(2)}) %collective-permute-start.1) | collective-permute-done | bytes 262176 | tf_op jit(solution)/shard_map/ppermute | solution.py:411
  22.0 1.9 %collective-permute-start.2 = (bf16[256,512]{1,0:T(8,128)(2,1)S(1)}, bf16[256,512]{1,0:T(8,128)(2,1)S(1)}, u32[]{:S(2)}, u32[]{:S(2)}) collective-permute-start(bf16[256,512]{1,0:T(8,128)(2,1)S(1)} %collective-permute-done.1.k_ref), channel_id=1, source_target_pairs={{0,1},{1,2},{2,3},{3,4},{4,5},{5,6},{6,7},{7,8},{8,9},{9,10},{10,1... | collective-permute-start | bytes 786440 | tf_op jit(solution)/shard_map/ppermute | solution.py:411
  23.9 2.2 %shard_map.77 = (bf16[4,256,1024]{2,1,0:T(8,128)(2,1)S(1)}, f32[4,8,1024]{2,1,0:T(8,128)S(1)}) custom-call(s32[1]{0:T(128)S(6)} %max.3.before_ref, s32[1,256]{1,0:T(1,128)S(1)} %bitcast.7, bf16[4,1024,128]{2,1,0:T(8,128)(2,1)S(1)} %get-tuple-element.48.q_ref.q4_ref, bf16[256,512]{1,0:T(8,128)(2,1)S(1)} %collective-permute-done.1.k_ref), custom_call_target="tpu_custom_call" | custom-call | flops 268435456 | bytes 1048576 | tf_op jit(solution)/shard_map/pallas_call | solution.py:328
  26.1 0.8 collective-permute-done.v_ref
  26.9 1.9 %collective-permute-start.4 = (bf16[256,512]{1,0:T(8,128)(2,1)S(1)}, bf16[256,512]{1,0:T(8,128)(2,1)S(1)}, u32[]{:S(2)}, u32[]{:S(2)}) collective-permute-start(bf16[256,512]{1,0:T(8,128)(2,1)S(1)} %collective-permute-done.v_ref), channel_id=1, source_target_pairs={{0,1},{1,2},{2,3},{3,4},{4,5},{5,6},{6,7},{7,8},{8,9},{9,10},{10,1... | collective-permute-start | bytes 786440 | tf_op jit(solution)/shard_map/ppermute | solution.py:411
  28.8 2.9 %shard_map.78 = (bf16[4,1024,128]{2,1,0:T(8,128)(2,1)S(1)}, f32[4,256,1024]{2,1,0:T(8,128)S(1)}, f32[4,8,1024]{2,1,0:T(8,128)S(1)}) custom-call(s32[1]{0:T(128)S(6)} %max.3.before_ref, bf16[256,2048]{1,0:T(8,128)(2,1)} %g_ref, bf16[256,512]{1,0:T(8,128)(2,1)} %v_ref.1, bf16[4,256,1024]{2,1,0:T(8,128)(2,1)S(1)} %get-tuple-element.49.p_ref), custom_call_target="tpu_custom_call" | custom-call | flops 268435456 | bytes 1048576 | tf_op jit(solution)/shard_map/pallas_call | solution.py:328
  31.7 1.4 %shard_map.79 = (f32[4,256,1024]{2,1,0:T(8,128)S(1)}, f32[4,8,1024]{2,1,0:T(8,128)S(1)}) custom-call(s32[1]{0:T(128)S(6)} %max.3.before_ref, bf16[4,1024,128]{2,1,0:T(8,128)(2,1)S(1)} %get-tuple-element.57.g_ref.g4_ref, bf16[256,512]{1,0:T(8,128)(2,1)S(1)} %collective-permute-done.v_ref, bf16[4,256,1024]{2,1,0:T(8,128)(2,1)S(1)} %get-tuple-element.58.p_ref), custom_call_target="tpu_custom_call" | custom-call | flops 268435456 | bytes 1048576 | tf_op jit(solution)/shard_map/pallas_call | solution.py:328
  33.1 4.8 %collective-permute-done.2.k_ref = bf16[256,512]{1,0:T(8,128)(2,1)S(1)} collective-permute-done((bf16[256,512]{1,0:T(8,128)(2,1)S(1)}, bf16[256,512]{1,0:T(8,128)(2,1)S(1)}, u32[]{:S(2)}, u32[]{:S(2)}) %collective-permute-start.2) | collective-permute-done | bytes 262176 | tf_op jit(solution)/shard_map/ppermute | solution.py:411
  37.9 1.9 %collective-permute-start.3 = (bf16[256,512]{1,0:T(8,128)(2,1)S(1)}, bf16[256,512]{1,0:T(8,128)(2,1)S(1)}, u32[]{:S(2)}, u32[]{:S(2)}) collective-permute-start(bf16[256,512]{1,0:T(8,128)(2,1)S(1)} %collective-permute-done.2.k_ref), channel_id=1, source_target_pairs={{0,1},{1,2},{2,3},{3,4},{4,5},{5,6},{6,7},{7,8},{8,9},{9,10},{10,1... | collective-permute-start | bytes 786440 | tf_op jit(solution)/shard_map/ppermute | solution.py:411
  39.8 2.2 %shard_map.80 = (bf16[4,256,1024]{2,1,0:T(8,128)(2,1)S(1)}, f32[4,8,1024]{2,1,0:T(8,128)S(1)}) custom-call(s32[1]{0:T(128)S(6)} %max.3.before_ref, s32[1,256]{1,0:T(1,128)S(1)} %bitcast.8, bf16[4,1024,128]{2,1,0:T(8,128)(2,1)S(1)} %get-tuple-element.48.q_ref.q4_ref, bf16[256,512]{1,0:T(8,128)(2,1)S(1)} %collective-permute-done.2.k_ref), custom_call_target="tpu_custom_call" | custom-call | flops 268435456 | bytes 1048576 | tf_op jit(solution)/shard_map/pallas_call | solution.py:328
  42.0 0.8 collective-permute-done.4.v_ref
  42.8 1.9 %collective-permute-start.5 = (bf16[256,512]{1,0:T(8,128)(2,1)S(1)}, bf16[256,512]{1,0:T(8,128)(2,1)S(1)}, u32[]{:S(2)}, u32[]{:S(2)}) collective-permute-start(bf16[256,512]{1,0:T(8,128)(2,1)S(1)} %collective-permute-done.4.v_ref), channel_id=1, source_target_pairs={{0,1},{1,2},{2,3},{3,4},{4,5},{5,6},{6,7},{7,8},{8,9},{9,10},{10,1... | collective-permute-start | bytes 786440 | tf_op jit(solution)/shard_map/ppermute | solution.py:411
  44.7 1.4 %shard_map.81 = (f32[4,256,1024]{2,1,0:T(8,128)S(1)}, f32[4,8,1024]{2,1,0:T(8,128)S(1)}) custom-call(s32[1]{0:T(128)S(6)} %max.3.before_ref, bf16[4,1024,128]{2,1,0:T(8,128)(2,1)S(1)} %get-tuple-element.57.g_ref.g4_ref, bf16[256,512]{1,0:T(8,128)(2,1)S(1)} %collective-permute-done.4.v_ref, bf16[4,256,1024]{2,1,0:T(8,128)(2,1)S(1)} %get-tuple-element.63.p_ref), custom_call_target="tpu_custom_call" | custom-call | flops 268435456 | bytes 1048576 | tf_op jit(solution)/shard_map/pallas_call | solution.py:328
  46.1 5.9 %collective-permute-done.3.k_ref = bf16[256,512]{1,0:T(8,128)(2,1)S(1)} collective-permute-done((bf16[256,512]{1,0:T(8,128)(2,1)S(1)}, bf16[256,512]{1,0:T(8,128)(2,1)S(1)}, u32[]{:S(2)}, u32[]{:S(2)}) %collective-permute-start.3) | collective-permute-done | bytes 262176 | tf_op jit(solution)/shard_map/ppermute | solution.py:411
  52.0 0.1 shard_map.82
  52.0 1.9 %collective-permute-start.7 = (bf16[256,512]{1,0:T(8,128)(2,1)S(1)}, bf16[256,512]{1,0:T(8,128)(2,1)S(1)}, u32[]{:S(2)}, u32[]{:S(2)}) collective-permute-start(bf16[256,512]{1,0:T(8,128)(2,1)S(1)} %get-tuple-element.67), channel_id=1, source_target_pairs={{1,0},{2,1},{3,2},{4,3},{5,4},{6,5},{7,6},{8,7},{9,8},{10,9},{11,1... | collective-permute-start | bytes 786440 | tf_op jit(solution)/shard_map/ppermute | solution.py:411
  54.0 1.7 %collective-permute-done.5.v_ref = bf16[256,512]{1,0:T(8,128)(2,1)S(1)} collective-permute-done((bf16[256,512]{1,0:T(8,128)(2,1)S(1)}, bf16[256,512]{1,0:T(8,128)(2,1)S(1)}, u32[]{:S(2)}, u32[]{:S(2)}) %collective-permute-start.5) | collective-permute-done | bytes 262176 | tf_op jit(solution)/shard_map/ppermute | solution.py:411
  55.6 0.2 shard_map.83
  55.8 1.9 %collective-permute-start.6 = (bf16[256,512]{1,0:T(8,128)(2,1)S(1)}, bf16[256,512]{1,0:T(8,128)(2,1)S(1)}, u32[]{:S(2)}, u32[]{:S(2)}) collective-permute-start(bf16[256,512]{1,0:T(8,128)(2,1)S(1)} %get-tuple-element.71), channel_id=1, source_target_pairs={{1,0},{2,1},{3,2},{4,3},{5,4},{6,5},{7,6},{8,7},{9,8},{10,9},{11,1... | collective-permute-start | bytes 786440 | tf_op jit(solution)/shard_map/ppermute | solution.py:411
  57.7 1.3 %shard_map.84 = bf16[256,512]{1,0:T(8,128)(2,1)S(1)} custom-call(s32[1]{0:T(128)S(6)} %max.3.before_ref, bf16[4,1024,128]{2,1,0:T(8,128)(2,1)S(1)} %get-tuple-element.57.g_ref.g4_ref, bf16[4,256,1024]{2,1,0:T(8,128)(2,1)S(1)} %get-tuple-element.63.p_ref, f32[4,8,1024]{2,1,0:T(8,128)S(1)} %get-tuple-element.88.row_ref), custom_call_target="tpu_custom_call" | custom-call | flops 268435456 | bytes 1048576 | tf_op jit(solution)/shard_map/pallas_call | solution.py:328
  59.1 4.1 %collective-permute-done.7 = bf16[256,512]{1,0:T(8,128)(2,1)S(1)} collective-permute-done((bf16[256,512]{1,0:T(8,128)(2,1)S(1)}, bf16[256,512]{1,0:T(8,128)(2,1)S(1)}, u32[]{:S(2)}, u32[]{:S(2)}) %collective-permute-start.7) | collective-permute-done | bytes 262176 | tf_op jit(solution)/shard_map/ppermute | solution.py:411
  63.2 0.1 add_convert_fusion.5
  63.2 5.9 %collective-permute-start.9 = (bf16[256,512]{1,0:T(8,128)(2,1)S(1)}, bf16[256,512]{1,0:T(8,128)(2,1)S(1)}, u32[]{:S(2)}, u32[]{:S(2)}) collective-permute-start(bf16[256,512]{1,0:T(8,128)(2,1)S(1)} %add_convert_fusion.5), channel_id=1, source_target_pairs={{1,0},{2,1},{3,2},{4,3},{5,4},{6,5},{7,6},{8,7},{9,8},{10,9},{11,1... | collective-permute-start | bytes 786440 | tf_op jit(solution)/shard_map/ppermute | solution.py:411
  69.2 1.7 %shard_map.85 = (bf16[256,512]{1,0:T(8,128)(2,1)S(1)}, f32[4,128,1024]{2,1,0:T(8,128)S(1)}) custom-call(s32[1]{0:T(128)S(6)} %max.3.before_ref, bf16[4,1024,128]{2,1,0:T(8,128)(2,1)S(1)} %get-tuple-element.48.q_ref.q4_ref, bf16[256,512]{1,0:T(8,128)(2,1)S(1)} %collective-permute-done.2.k_ref, bf16[4,256,1024]{2,1,0:T(8,128)(2,1)S(1)} %get-tuple-element.63.p_ref, ...), custom_call_target="tpu_custom_call" | custom-call | flops 536870912 | bytes 1048576 | tf_op jit(solution)/shard_map/pallas_call | solution.py:328
  70.9 0.1 add_convert_fusion.4
  71.0 3.0 %collective-permute-start.8 = (bf16[256,512]{1,0:T(8,128)(2,1)S(1)}, bf16[256,512]{1,0:T(8,128)(2,1)S(1)}, u32[]{:S(2)}, u32[]{:S(2)}) collective-permute-start(bf16[256,512]{1,0:T(8,128)(2,1)S(1)} %add_convert_fusion.4), channel_id=1, source_target_pairs={{1,0},{2,1},{3,2},{4,3},{5,4},{6,5},{7,6},{8,7},{9,8},{10,9},{11,1... | collective-permute-start | bytes 786440 | tf_op jit(solution)/shard_map/ppermute | solution.py:411
  74.0 1.3 %shard_map.86 = bf16[256,512]{1,0:T(8,128)(2,1)S(1)} custom-call(s32[1]{0:T(128)S(6)} %max.3.before_ref, bf16[4,1024,128]{2,1,0:T(8,128)(2,1)S(1)} %get-tuple-element.57.g_ref.g4_ref, bf16[4,256,1024]{2,1,0:T(8,128)(2,1)S(1)} %get-tuple-element.58.p_ref, f32[4,8,1024]{2,1,0:T(8,128)S(1)} %get-tuple-element.88.row_ref), custom_call_target="tpu_custom_call" | custom-call | flops 268435456 | bytes 1048576 | tf_op jit(solution)/shard_map/pallas_call | solution.py:328
  75.3 0.0 collective-permute-done.9
  75.3 0.1 add_convert_fusion.3
  75.4 7.6 %collective-permute-start.11 = (bf16[256,512]{1,0:T(8,128)(2,1)S(1)}, bf16[256,512]{1,0:T(8,128)(2,1)S(1)}, u32[]{:S(2)}, u32[]{:S(2)}) collective-permute-start(bf16[256,512]{1,0:T(8,128)(2,1)S(1)} %add_convert_fusion.3), channel_id=1, source_target_pairs={{1,0},{2,1},{3,2},{4,3},{5,4},{6,5},{7,6},{8,7},{9,8},{10,9},{11,1... | collective-permute-start | bytes 786440 | tf_op jit(solution)/shard_map/ppermute | solution.py:411
  83.0 1.7 %shard_map.87 = (bf16[256,512]{1,0:T(8,128)(2,1)S(1)}, f32[4,128,1024]{2,1,0:T(8,128)S(1)}) custom-call(s32[1]{0:T(128)S(6)} %max.3.before_ref, bf16[4,1024,128]{2,1,0:T(8,128)(2,1)S(1)} %get-tuple-element.48.q_ref.q4_ref, bf16[256,512]{1,0:T(8,128)(2,1)S(1)} %collective-permute-done.1.k_ref, bf16[4,256,1024]{2,1,0:T(8,128)(2,1)S(1)} %get-tuple-element.58.p_ref, ...), custom_call_target="tpu_custom_call" | custom-call | flops 536870912 | bytes 1048576 | tf_op jit(solution)/shard_map/pallas_call | solution.py:328
  84.7 0.1 add_convert_fusion.2
  84.8 0.0 copy-start
  84.8 4.0 %collective-permute-start.10 = (bf16[256,512]{1,0:T(8,128)(2,1)S(1)}, bf16[256,512]{1,0:T(8,128)(2,1)S(1)}, u32[]{:S(2)}, u32[]{:S(2)}) collective-permute-start(bf16[256,512]{1,0:T(8,128)(2,1)S(1)} %add_convert_fusion.2), channel_id=1, source_target_pairs={{1,0},{2,1},{3,2},{4,3},{5,4},{6,5},{7,6},{8,7},{9,8},{10,9},{11,1... | collective-permute-start | bytes 786440 | tf_op jit(solution)/shard_map/ppermute | solution.py:411
  88.8 1.1 %shard_map.88 = f32[256,512]{1,0:T(8,128)S(1)} custom-call(s32[1]{0:T(128)S(6)} %max.3.before_ref, bf16[4,1024,128]{2,1,0:T(8,128)(2,1)S(1)} %get-tuple-element.57.g_ref.g4_ref, bf16[4,256,1024]{2,1,0:T(8,128)(2,1)S(1)} %get-tuple-element.49.p_ref, f32[4,8,1024]{2,1,0:T(8,128)S(1)} %get-tuple-element.88.row_ref), custom_call_target="tpu_custom_call" | custom-call | flops 268435456 | bytes 1048576 | tf_op jit(solution)/shard_map/pallas_call | solution.py:328
  90.0 2.9 %shard_map.89 = (f32[256,512]{1,0:T(8,128)S(1)}, bf16[256,2048]{1,0:T(8,128)(2,1)}) custom-call(s32[1]{0:T(128)S(6)} %max.3.before_ref, bf16[4,1024,128]{2,1,0:T(8,128)(2,1)S(1)} %get-tuple-element.48.q_ref.q4_ref, bf16[256,512]{1,0:T(8,128)(2,1)S(1)} %copy-done, bf16[4,256,1024]{2,1,0:T(8,128)(2,1)S(1)} %get-tuple-element.49.p_ref, ...), custom_call_target="tpu_custom_call" | custom-call | flops 536870912 | bytes 1048576 | tf_op jit(solution)/shard_map/pallas_call | solution.py:328
  92.8 0.8 add_convert_fusion
  93.6 0.8 add_convert_fusion.1
  (8 shorter events, 0.1 us)
Async XLA Ops:
  0.6 21.4 %collective-permute-start.1 = (bf16[256,512]{1,0:T(8,128)(2,1)}, bf16[256,512]{1,0:T(8,128)(2,1)S(1)}, u32[]{:S(2)}, u32[]{:S(2)}) collective-permute-start(bf16[256,512]{1,0:T(8,128)(2,1)} %k_ref.3), channel_id=1, source_target_pairs={{0,1},{1,2},{2,3},{3,4},{4,5},{5,6},{6,7},{7,8},{8,9},{9,10},{10,1... | collective-permute-start | bytes 786440 | tf_op jit(solution)/shard_map/ppermute | solution.py:411
  5.9 20.9 %collective-permute-start = (bf16[256,512]{1,0:T(8,128)(2,1)}, bf16[256,512]{1,0:T(8,128)(2,1)S(1)}, u32[]{:S(2)}, u32[]{:S(2)}) collective-permute-start(bf16[256,512]{1,0:T(8,128)(2,1)} %v_ref.1), channel_id=1, source_target_pairs={{0,1},{1,2},{2,3},{3,4},{4,5},{5,6},{6,7},{7,8},{8,9},{9,10},{10,1... | collective-permute-start | bytes 786440 | tf_op jit(solution)/shard_map/ppermute | solution.py:411
  22.0 15.9 %collective-permute-start.2 = (bf16[256,512]{1,0:T(8,128)(2,1)S(1)}, bf16[256,512]{1,0:T(8,128)(2,1)S(1)}, u32[]{:S(2)}, u32[]{:S(2)}) collective-permute-start(bf16[256,512]{1,0:T(8,128)(2,1)S(1)} %collective-permute-done.1.k_ref), channel_id=1, source_target_pairs={{0,1},{1,2},{2,3},{3,4},{4,5},{5,6},{6,7},{7,8},{8,9},{9,10},{10,1... | collective-permute-start | bytes 786440 | tf_op jit(solution)/shard_map/ppermute | solution.py:411
  26.9 15.9 %collective-permute-start.4 = (bf16[256,512]{1,0:T(8,128)(2,1)S(1)}, bf16[256,512]{1,0:T(8,128)(2,1)S(1)}, u32[]{:S(2)}, u32[]{:S(2)}) collective-permute-start(bf16[256,512]{1,0:T(8,128)(2,1)S(1)} %collective-permute-done.v_ref), channel_id=1, source_target_pairs={{0,1},{1,2},{2,3},{3,4},{4,5},{5,6},{6,7},{7,8},{8,9},{9,10},{10,1... | collective-permute-start | bytes 786440 | tf_op jit(solution)/shard_map/ppermute | solution.py:411
  37.9 14.1 %collective-permute-start.3 = (bf16[256,512]{1,0:T(8,128)(2,1)S(1)}, bf16[256,512]{1,0:T(8,128)(2,1)S(1)}, u32[]{:S(2)}, u32[]{:S(2)}) collective-permute-start(bf16[256,512]{1,0:T(8,128)(2,1)S(1)} %collective-permute-done.2.k_ref), channel_id=1, source_target_pairs={{0,1},{1,2},{2,3},{3,4},{4,5},{5,6},{6,7},{7,8},{8,9},{9,10},{10,1... | collective-permute-start | bytes 786440 | tf_op jit(solution)/shard_map/ppermute | solution.py:411
  42.8 12.9 %collective-permute-start.5 = (bf16[256,512]{1,0:T(8,128)(2,1)S(1)}, bf16[256,512]{1,0:T(8,128)(2,1)S(1)}, u32[]{:S(2)}, u32[]{:S(2)}) collective-permute-start(bf16[256,512]{1,0:T(8,128)(2,1)S(1)} %collective-permute-done.4.v_ref), channel_id=1, source_target_pairs={{0,1},{1,2},{2,3},{3,4},{4,5},{5,6},{6,7},{7,8},{8,9},{9,10},{10,1... | collective-permute-start | bytes 786440 | tf_op jit(solution)/shard_map/ppermute | solution.py:411
  52.0 11.1 %collective-permute-start.7 = (bf16[256,512]{1,0:T(8,128)(2,1)S(1)}, bf16[256,512]{1,0:T(8,128)(2,1)S(1)}, u32[]{:S(2)}, u32[]{:S(2)}) collective-permute-start(bf16[256,512]{1,0:T(8,128)(2,1)S(1)} %get-tuple-element.67), channel_id=1, source_target_pairs={{1,0},{2,1},{3,2},{4,3},{5,4},{6,5},{7,6},{8,7},{9,8},{10,9},{11,1... | collective-permute-start | bytes 786440 | tf_op jit(solution)/shard_map/ppermute | solution.py:411
  55.8 15.1 %collective-permute-start.6 = (bf16[256,512]{1,0:T(8,128)(2,1)S(1)}, bf16[256,512]{1,0:T(8,128)(2,1)S(1)}, u32[]{:S(2)}, u32[]{:S(2)}) collective-permute-start(bf16[256,512]{1,0:T(8,128)(2,1)S(1)} %get-tuple-element.71), channel_id=1, source_target_pairs={{1,0},{2,1},{3,2},{4,3},{5,4},{6,5},{7,6},{8,7},{9,8},{10,9},{11,1... | collective-permute-start | bytes 786440 | tf_op jit(solution)/shard_map/ppermute | solution.py:411
  63.2 12.1 %collective-permute-start.9 = (bf16[256,512]{1,0:T(8,128)(2,1)S(1)}, bf16[256,512]{1,0:T(8,128)(2,1)S(1)}, u32[]{:S(2)}, u32[]{:S(2)}) collective-permute-start(bf16[256,512]{1,0:T(8,128)(2,1)S(1)} %add_convert_fusion.5), channel_id=1, source_target_pairs={{1,0},{2,1},{3,2},{4,3},{5,4},{6,5},{7,6},{8,7},{9,8},{10,9},{11,1... | collective-permute-start | bytes 786440 | tf_op jit(solution)/shard_map/ppermute | solution.py:411
  71.0 13.7 %collective-permute-start.8 = (bf16[256,512]{1,0:T(8,128)(2,1)S(1)}, bf16[256,512]{1,0:T(8,128)(2,1)S(1)}, u32[]{:S(2)}, u32[]{:S(2)}) collective-permute-start(bf16[256,512]{1,0:T(8,128)(2,1)S(1)} %add_convert_fusion.4), channel_id=1, source_target_pairs={{1,0},{2,1},{3,2},{4,3},{5,4},{6,5},{7,6},{8,7},{9,8},{10,9},{11,1... | collective-permute-start | bytes 786440 | tf_op jit(solution)/shard_map/ppermute | solution.py:411
  75.4 17.4 %collective-permute-start.11 = (bf16[256,512]{1,0:T(8,128)(2,1)S(1)}, bf16[256,512]{1,0:T(8,128)(2,1)S(1)}, u32[]{:S(2)}, u32[]{:S(2)}) collective-permute-start(bf16[256,512]{1,0:T(8,128)(2,1)S(1)} %add_convert_fusion.3), channel_id=1, source_target_pairs={{1,0},{2,1},{3,2},{4,3},{5,4},{6,5},{7,6},{8,7},{9,8},{10,9},{11,1... | collective-permute-start | bytes 786440 | tf_op jit(solution)/shard_map/ppermute | solution.py:411
  84.8 5.2 %copy-start = (bf16[256,512]{1,0:T(8,128)(2,1)S(1)}, bf16[256,512]{1,0:T(8,128)(2,1)}, u32[]{:S(2)}) copy-start(bf16[256,512]{1,0:T(8,128)(2,1)} %k_ref.3) | copy-start | bytes 786436
  84.8 8.8 %collective-permute-start.10 = (bf16[256,512]{1,0:T(8,128)(2,1)S(1)}, bf16[256,512]{1,0:T(8,128)(2,1)S(1)}, u32[]{:S(2)}, u32[]{:S(2)}) collective-permute-start(bf16[256,512]{1,0:T(8,128)(2,1)S(1)} %add_convert_fusion.2), channel_id=1, source_target_pairs={{1,0},{2,1},{3,2},{4,3},{5,4},{6,5},{7,6},{8,7},{9,8},{10,9},{11,1... | collective-permute-start | bytes 786440 | tf_op jit(solution)/shard_map/ppermute | solution.py:411

commit v5 on v4

--- a/solution.py
+++ b/solution.py
@@ -434,8 +434,9 @@
     k.append(shift(k[0], 1))
     v.append(shift(after(values, start), 1))
     q4, p0, stat0 = probs_of(0, before, start, in_hbm(queries), in_hbm(keys))
-    p, dp, stat, total = [p0], [], [stat0], []
-    done = stat0
+    g4, dp0, sum0 = dprobs_of(0, before, in_hbm(grad_out), in_hbm(values), p0)
+    p, dp, stat, total = [p0], [dp0], [stat0], [sum0]
+    done = sum0
     for d in (1, 2):
         k[d] = after(k[d], done)
         k.append(shift(k[d], 1))
@@ -444,11 +445,6 @@
         stat.append(y)
         v[d] = after(v[d], y)
         v.append(shift(v[d], 1))
-        if d == 1:
-            late = after(grad_out, v[d])
-            g4, dp0, sum0 = dprobs_of(0, before, in_hbm(late), in_hbm(values), p0)
-            dp.append(dp0)
-            total.append(sum0)
         x, y = dprobs_of(d, before, g4, v[d], p[d])
         dp.append(x)
         total.append(y)

time: 95.5 us -> 95.8 us (level)
  the two profiles are of different devices: /device:TPU:6 before, /device:TPU:2 now
where the time goes in v5:
time: 95.8 us; the launch traced here: 95.1 us
  starting transfers between devices  49.7 us (52%)
  waiting for transfers between devices  22 us (23%)
  Pallas kernels  18 us (19%)
  other arithmetic  2.38 us (2%)
  between operations  1.56 us (2%)
  local copies, waits for them, and re-layouts  1.4 us (1%)
    ppermute x12, starting transfers between devices, shift(): return lax.ppermute(x, ('dp', 'ctx'), route)  49.7 us
    ppermute x12, waiting for transfers between devices, shift(): return lax.ppermute(x, ('dp', 'ctx'), route)  22 us
    pallas_call x14, Pallas kernels, call(): pl.pallas_call(kernel, grid=(steps,), in_specs=in_specs, out_specs=[spec...  18 us
  transfers between devices with their start and end apart: 12, of which 7 were waited for; matrix products, arithmetic and copies ran while one was open for 3% of the time, Pallas kernels for 19%

profile of v5, /device:TPU:2, one launch (start us, length us, event | category | flops | bytes accessed | tf_op | source)
XLA Modules:
  0.0 95.1 jit_solution(12279311673976647608)
XLA Ops:
  0.6 3.8 %collective-permute-start = (bf16[256,512]{1,0:T(8,128)(2,1)}, bf16[256,512]{1,0:T(8,128)(2,1)S(1)}, u32[]{:S(2)}, u32[]{:S(2)}) collective-permute-start(bf16[256,512]{1,0:T(8,128)(2,1)} %k_ref.3), channel_id=1, source_target_pairs={{0,1},{1,2},{2,3},{3,4},{4,5},{5,6},{6,7},{7,8},{8,9},{9,10},{10,1... | collective-permute-start | bytes 786440 | tf_op jit(solution)/shard_map/ppermute | solution.py:411
  4.5 0.7 pad_bitcast_fusion
  5.2 0.3 reduce-window.9
  5.5 0.1 slice.13
  5.6 0.1 slice_reduce_fusion
  5.7 0.1 add_bitcast_fusion
  5.8 0.1 select_reduce_fusion
  5.9 3.8 %collective-permute-start.2 = (bf16[256,512]{1,0:T(8,128)(2,1)}, bf16[256,512]{1,0:T(8,128)(2,1)S(1)}, u32[]{:S(2)}, u32[]{:S(2)}) collective-permute-start(bf16[256,512]{1,0:T(8,128)(2,1)} %v_ref.1), channel_id=1, source_target_pairs={{0,1},{1,2},{2,3},{3,4},{4,5},{5,6},{6,7},{7,8},{8,9},{9,10},{10,1... | collective-permute-start | bytes 786440 | tf_op jit(solution)/shard_map/ppermute | solution.py:411
  9.8 0.5 slice.16
  10.9 3.3 %shard_map.76 = (bf16[4,1024,128]{2,1,0:T(8,128)(2,1)S(1)}, bf16[4,256,1024]{2,1,0:T(8,128)(2,1)S(1)}, f32[4,8,1024]{2,1,0:T(8,128)S(1)}) custom-call(s32[1]{0:T(128)S(6)} %max.3.before_ref, s32[1,256]{1,0:T(1,128)S(1)} %bitcast.6, bf16[256,2048]{1,0:T(8,128)(2,1)} %q_ref.1, bf16[256,512]{1,0:T(8,128)(2,1)} %k_ref.3), custom_call_target="tpu_custom_call" | custom-call | flops 268435456 | bytes 1048576 | tf_op jit(solution)/shard_map/pallas_call | solution.py:328
  14.2 2.9 %shard_map.77 = (bf16[4,1024,128]{2,1,0:T(8,128)(2,1)S(1)}, f32[4,256,1024]{2,1,0:T(8,128)S(1)}, f32[4,8,1024]{2,1,0:T(8,128)S(1)}) custom-call(s32[1]{0:T(128)S(6)} %max.3.before_ref, bf16[256,2048]{1,0:T(8,128)(2,1)} %g_ref.1, bf16[256,512]{1,0:T(8,128)(2,1)} %v_ref.1, bf16[4,256,1024]{2,1,0:T(8,128)(2,1)S(1)} %get-tuple-element.48.p_ref), custom_call_target="tpu_custom_call" | custom-call | flops 268435456 | bytes 1048576 | tf_op jit(solution)/shard_map/pallas_call | solution.py:328
  17.1 3.0 %collective-permute-done.k_ref = bf16[256,512]{1,0:T(8,128)(2,1)S(1)} collective-permute-done((bf16[256,512]{1,0:T(8,128)(2,1)}, bf16[256,512]{1,0:T(8,128)(2,1)S(1)}, u32[]{:S(2)}, u32[]{:S(2)}) %collective-permute-start) | collective-permute-done | bytes 262176 | tf_op jit(solution)/shard_map/ppermute | solution.py:411
  20.1 1.9 %collective-permute-start.1 = (bf16[256,512]{1,0:T(8,128)(2,1)S(1)}, bf16[256,512]{1,0:T(8,128)(2,1)S(1)}, u32[]{:S(2)}, u32[]{:S(2)}) collective-permute-start(bf16[256,512]{1,0:T(8,128)(2,1)S(1)} %collective-permute-done.k_ref), channel_id=1, source_target_pairs={{0,1},{1,2},{2,3},{3,4},{4,5},{5,6},{6,7},{7,8},{8,9},{9,10},{10,1... | collective-permute-start | bytes 786440 | tf_op jit(solution)/shard_map/ppermute | solution.py:411
  22.1 2.2 %shard_map.78 = (bf16[4,256,1024]{2,1,0:T(8,128)(2,1)S(1)}, f32[4,8,1024]{2,1,0:T(8,128)S(1)}) custom-call(s32[1]{0:T(128)S(6)} %max.3.before_ref, s32[1,256]{1,0:T(1,128)S(1)} %bitcast.7, bf16[4,1024,128]{2,1,0:T(8,128)(2,1)S(1)} %get-tuple-element.47.q_ref.q4_ref, bf16[256,512]{1,0:T(8,128)(2,1)S(1)} %collective-permute-done.k_ref), custom_call_target="tpu_custom_call" | custom-call | flops 268435456 | bytes 1048576 | tf_op jit(solution)/shard_map/pallas_call | solution.py:328
  24.3 1.5 %collective-permute-done.2.v_ref = bf16[256,512]{1,0:T(8,128)(2,1)S(1)} collective-permute-done((bf16[256,512]{1,0:T(8,128)(2,1)}, bf16[256,512]{1,0:T(8,128)(2,1)S(1)}, u32[]{:S(2)}, u32[]{:S(2)}) %collective-permute-start.2) | collective-permute-done | bytes 262176 | tf_op jit(solution)/shard_map/ppermute | solution.py:411
  25.8 2.5 %collective-permute-start.4 = (bf16[256,512]{1,0:T(8,128)(2,1)S(1)}, bf16[256,512]{1,0:T(8,128)(2,1)S(1)}, u32[]{:S(2)}, u32[]{:S(2)}) collective-permute-start(bf16[256,512]{1,0:T(8,128)(2,1)S(1)} %collective-permute-done.2.v_ref), channel_id=1, source_target_pairs={{0,1},{1,2},{2,3},{3,4},{4,5},{5,6},{6,7},{7,8},{8,9},{9,10},{10,1... | collective-permute-start | bytes 786440 | tf_op jit(solution)/shard_map/ppermute | solution.py:411
  28.2 1.4 %shard_map.79 = (f32[4,256,1024]{2,1,0:T(8,128)S(1)}, f32[4,8,1024]{2,1,0:T(8,128)S(1)}) custom-call(s32[1]{0:T(128)S(6)} %max.3.before_ref, bf16[4,1024,128]{2,1,0:T(8,128)(2,1)S(1)} %get-tuple-element.50.g_ref.g4_ref, bf16[256,512]{1,0:T(8,128)(2,1)S(1)} %collective-permute-done.2.v_ref, bf16[4,256,1024]{2,1,0:T(8,128)(2,1)S(1)} %get-tuple-element.56.p_ref), custom_call_target="tpu_custom_call" | custom-call | flops 268435456 | bytes 1048576 | tf_op jit(solution)/shard_map/pallas_call | solution.py:328
  29.6 4.6 %collective-permute-done.1.k_ref = bf16[256,512]{1,0:T(8,128)(2,1)S(1)} collective-permute-done((bf16[256,512]{1,0:T(8,128)(2,1)S(1)}, bf16[256,512]{1,0:T(8,128)(2,1)S(1)}, u32[]{:S(2)}, u32[]{:S(2)}) %collective-permute-start.1) | collective-permute-done | bytes 262176 | tf_op jit(solution)/shard_map/ppermute | solution.py:411
  34.3 1.9 %collective-permute-start.3 = (bf16[256,512]{1,0:T(8,128)(2,1)S(1)}, bf16[256,512]{1,0:T(8,128)(2,1)S(1)}, u32[]{:S(2)}, u32[]{:S(2)}) collective-permute-start(bf16[256,512]{1,0:T(8,128)(2,1)S(1)} %collective-permute-done.1.k_ref), channel_id=1, source_target_pairs={{0,1},{1,2},{2,3},{3,4},{4,5},{5,6},{6,7},{7,8},{8,9},{9,10},{10,1... | collective-permute-start | bytes 786440 | tf_op jit(solution)/shard_map/ppermute | solution.py:411
  36.2 0.2 shard_map.80
  36.4 4.3 %collective-permute-done.4.v_ref = bf16[256,512]{1,0:T(8,128)(2,1)S(1)} collective-permute-done((bf16[256,512]{1,0:T(8,128)(2,1)S(1)}, bf16[256,512]{1,0:T(8,128)(2,1)S(1)}, u32[]{:S(2)}, u32[]{:S(2)}) %collective-permute-start.4) | collective-permute-done | bytes 262176 | tf_op jit(solution)/shard_map/ppermute | solution.py:411
  40.6 1.9 %collective-permute-start.5 = (bf16[256,512]{1,0:T(8,128)(2,1)S(1)}, bf16[256,512]{1,0:T(8,128)(2,1)S(1)}, u32[]{:S(2)}, u32[]{:S(2)}) collective-permute-start(bf16[256,512]{1,0:T(8,128)(2,1)S(1)} %collective-permute-done.4.v_ref), channel_id=1, source_target_pairs={{0,1},{1,2},{2,3},{3,4},{4,5},{5,6},{6,7},{7,8},{8,9},{9,10},{10,1... | collective-permute-start | bytes 786440 | tf_op jit(solution)/shard_map/ppermute | solution.py:411
  42.6 0.2 shard_map.81
  42.8 6.1 %collective-permute-done.3.k_ref = bf16[256,512]{1,0:T(8,128)(2,1)S(1)} collective-permute-done((bf16[256,512]{1,0:T(8,128)(2,1)S(1)}, bf16[256,512]{1,0:T(8,128)(2,1)S(1)}, u32[]{:S(2)}, u32[]{:S(2)}) %collective-permute-start.3) | collective-permute-done | bytes 262176 | tf_op jit(solution)/shard_map/ppermute | solution.py:411
  48.8 0.1 shard_map.82
  48.9 4.8 %collective-permute-start.7 = (bf16[256,512]{1,0:T(8,128)(2,1)S(1)}, bf16[256,512]{1,0:T(8,128)(2,1)S(1)}, u32[]{:S(2)}, u32[]{:S(2)}) collective-permute-start(bf16[256,512]{1,0:T(8,128)(2,1)S(1)} %get-tuple-element.66), channel_id=1, source_target_pairs={{1,0},{2,1},{3,2},{4,3},{5,4},{6,5},{7,6},{8,7},{9,8},{10,9},{11,1... | collective-permute-start | bytes 786440 | tf_op jit(solution)/shard_map/ppermute | solution.py:411
  53.7 0.9 collective-permute-done.5.v_ref
  54.6 0.2 shard_map.83
  54.8 3.2 %collective-permute-start.6 = (bf16[256,512]{1,0:T(8,128)(2,1)S(1)}, bf16[256,512]{1,0:T(8,128)(2,1)S(1)}, u32[]{:S(2)}, u32[]{:S(2)}) collective-permute-start(bf16[256,512]{1,0:T(8,128)(2,1)S(1)} %get-tuple-element.69), channel_id=1, source_target_pairs={{1,0},{2,1},{3,2},{4,3},{5,4},{6,5},{7,6},{8,7},{9,8},{10,9},{11,1... | collective-permute-start | bytes 786440 | tf_op jit(solution)/shard_map/ppermute | solution.py:411
  58.1 0.2 shard_map.84
  58.3 1.6 %collective-permute-done.7 = bf16[256,512]{1,0:T(8,128)(2,1)S(1)} collective-permute-done((bf16[256,512]{1,0:T(8,128)(2,1)S(1)}, bf16[256,512]{1,0:T(8,128)(2,1)S(1)}, u32[]{:S(2)}, u32[]{:S(2)}) %collective-permute-start.7) | collective-permute-done | bytes 262176 | tf_op jit(solution)/shard_map/ppermute | solution.py:411
  59.9 0.1 add_convert_fusion.5
  60.0 9.0 %collective-permute-start.9 = (bf16[256,512]{1,0:T(8,128)(2,1)S(1)}, bf16[256,512]{1,0:T(8,128)(2,1)S(1)}, u32[]{:S(2)}, u32[]{:S(2)}) collective-permute-start(bf16[256,512]{1,0:T(8,128)(2,1)S(1)} %add_convert_fusion.5), channel_id=1, source_target_pairs={{1,0},{2,1},{3,2},{4,3},{5,4},{6,5},{7,6},{8,7},{9,8},{10,9},{11,1... | collective-permute-start | bytes 786440 | tf_op jit(solution)/shard_map/ppermute | solution.py:411
  69.0 0.4 shard_map.85
  69.4 0.0 collective-permute-done.6
  69.4 0.1 add_convert_fusion.4
  69.5 4.9 %collective-permute-start.8 = (bf16[256,512]{1,0:T(8,128)(2,1)S(1)}, bf16[256,512]{1,0:T(8,128)(2,1)S(1)}, u32[]{:S(2)}, u32[]{:S(2)}) collective-permute-start(bf16[256,512]{1,0:T(8,128)(2,1)S(1)} %add_convert_fusion.4), channel_id=1, source_target_pairs={{1,0},{2,1},{3,2},{4,3},{5,4},{6,5},{7,6},{8,7},{9,8},{10,9},{11,1... | collective-permute-start | bytes 786440 | tf_op jit(solution)/shard_map/ppermute | solution.py:411
  74.4 1.3 %shard_map.86 = bf16[256,512]{1,0:T(8,128)(2,1)S(1)} custom-call(s32[1]{0:T(128)S(6)} %max.3.before_ref, bf16[4,1024,128]{2,1,0:T(8,128)(2,1)S(1)} %get-tuple-element.50.g_ref.g4_ref, bf16[4,256,1024]{2,1,0:T(8,128)(2,1)S(1)} %get-tuple-element.56.p_ref, f32[4,8,1024]{2,1,0:T(8,128)S(1)} %get-tuple-element.86.row_ref), custom_call_target="tpu_custom_call" | custom-call | flops 268435456 | bytes 1048576 | tf_op jit(solution)/shard_map/pallas_call | solution.py:328
  75.7 0.1 add_convert_fusion.3
  75.8 8.0 %collective-permute-start.11 = (bf16[256,512]{1,0:T(8,128)(2,1)S(1)}, bf16[256,512]{1,0:T(8,128)(2,1)S(1)}, u32[]{:S(2)}, u32[]{:S(2)}) collective-permute-start(bf16[256,512]{1,0:T(8,128)(2,1)S(1)} %add_convert_fusion.3), channel_id=1, source_target_pairs={{1,0},{2,1},{3,2},{4,3},{5,4},{6,5},{7,6},{8,7},{9,8},{10,9},{11,1... | collective-permute-start | bytes 786440 | tf_op jit(solution)/shard_map/ppermute | solution.py:411
  83.8 1.7 %shard_map.87 = (bf16[256,512]{1,0:T(8,128)(2,1)S(1)}, f32[4,128,1024]{2,1,0:T(8,128)S(1)}) custom-call(s32[1]{0:T(128)S(6)} %max.3.before_ref, bf16[4,1024,128]{2,1,0:T(8,128)(2,1)S(1)} %get-tuple-element.47.q_ref.q4_ref, bf16[256,512]{1,0:T(8,128)(2,1)S(1)} %collective-permute-done.k_ref, bf16[4,256,1024]{2,1,0:T(8,128)(2,1)S(1)} %get-tuple-element.56.p_ref, ...), custom_call_target="tpu_custom_call" | custom-call | flops 536870912 | bytes 1048576 | tf_op jit(solution)/shard_map/pallas_call | solution.py:328
  85.5 0.1 add_convert_fusion.2
  85.5 0.0 copy-start
  85.6 4.0 %collective-permute-start.10 = (bf16[256,512]{1,0:T(8,128)(2,1)S(1)}, bf16[256,512]{1,0:T(8,128)(2,1)S(1)}, u32[]{:S(2)}, u32[]{:S(2)}) collective-permute-start(bf16[256,512]{1,0:T(8,128)(2,1)S(1)} %add_convert_fusion.2), channel_id=1, source_target_pairs={{1,0},{2,1},{3,2},{4,3},{5,4},{6,5},{7,6},{8,7},{9,8},{10,9},{11,1... | collective-permute-start | bytes 786440 | tf_op jit(solution)/shard_map/ppermute | solution.py:411
  89.6 1.1 %shard_map.88 = f32[256,512]{1,0:T(8,128)S(1)} custom-call(s32[1]{0:T(128)S(6)} %max.3.before_ref, bf16[4,1024,128]{2,1,0:T(8,128)(2,1)S(1)} %get-tuple-element.50.g_ref.g4_ref, bf16[4,256,1024]{2,1,0:T(8,128)(2,1)S(1)} %get-tuple-element.48.p_ref, f32[4,8,1024]{2,1,0:T(8,128)S(1)} %get-tuple-element.86.row_ref), custom_call_target="tpu_custom_call" | custom-call | flops 268435456 | bytes 1048576 | tf_op jit(solution)/shard_map/pallas_call | solution.py:328
  90.7 2.9 %shard_map.89 = (f32[256,512]{1,0:T(8,128)S(1)}, bf16[256,2048]{1,0:T(8,128)(2,1)}) custom-call(s32[1]{0:T(128)S(6)} %max.3.before_ref, bf16[4,1024,128]{2,1,0:T(8,128)(2,1)S(1)} %get-tuple-element.47.q_ref.q4_ref, bf16[256,512]{1,0:T(8,128)(2,1)S(1)} %copy-done, bf16[4,256,1024]{2,1,0:T(8,128)(2,1)S(1)} %get-tuple-element.48.p_ref, ...), custom_call_target="tpu_custom_call" | custom-call | flops 536870912 | bytes 1048576 | tf_op jit(solution)/shard_map/pallas_call | solution.py:328
  93.6 0.8 add_convert_fusion
  94.3 0.8 add_convert_fusion.1
  (8 shorter events, 0.1 us)
Async XLA Ops:
  0.6 19.5 %collective-permute-start = (bf16[256,512]{1,0:T(8,128)(2,1)}, bf16[256,512]{1,0:T(8,128)(2,1)S(1)}, u32[]{:S(2)}, u32[]{:S(2)}) collective-permute-start(bf16[256,512]{1,0:T(8,128)(2,1)} %k_ref.3), channel_id=1, source_target_pairs={{0,1},{1,2},{2,3},{3,4},{4,5},{5,6},{6,7},{7,8},{8,9},{9,10},{10,1... | collective-permute-start | bytes 786440 | tf_op jit(solution)/shard_map/ppermute | solution.py:411
  5.9 19.8 %collective-permute-start.2 = (bf16[256,512]{1,0:T(8,128)(2,1)}, bf16[256,512]{1,0:T(8,128)(2,1)S(1)}, u32[]{:S(2)}, u32[]{:S(2)}) collective-permute-start(bf16[256,512]{1,0:T(8,128)(2,1)} %v_ref.1), channel_id=1, source_target_pairs={{0,1},{1,2},{2,3},{3,4},{4,5},{5,6},{6,7},{7,8},{8,9},{9,10},{10,1... | collective-permute-start | bytes 786440 | tf_op jit(solution)/shard_map/ppermute | solution.py:411
  20.1 14.1 %collective-permute-start.1 = (bf16[256,512]{1,0:T(8,128)(2,1)S(1)}, bf16[256,512]{1,0:T(8,128)(2,1)S(1)}, u32[]{:S(2)}, u32[]{:S(2)}) collective-permute-start(bf16[256,512]{1,0:T(8,128)(2,1)S(1)} %collective-permute-done.k_ref), channel_id=1, source_target_pairs={{0,1},{1,2},{2,3},{3,4},{4,5},{5,6},{6,7},{7,8},{8,9},{9,10},{10,1... | collective-permute-start | bytes 786440 | tf_op jit(solution)/shard_map/ppermute | solution.py:411
  25.8 14.9 %collective-permute-start.4 = (bf16[256,512]{1,0:T(8,128)(2,1)S(1)}, bf16[256,512]{1,0:T(8,128)(2,1)S(1)}, u32[]{:S(2)}, u32[]{:S(2)}) collective-permute-start(bf16[256,512]{1,0:T(8,128)(2,1)S(1)} %collective-permute-done.2.v_ref), channel_id=1, source_target_pairs={{0,1},{1,2},{2,3},{3,4},{4,5},{5,6},{6,7},{7,8},{8,9},{9,10},{10,1... | collective-permute-start | bytes 786440 | tf_op jit(solution)/shard_map/ppermute | solution.py:411
  34.3 14.5 %collective-permute-start.3 = (bf16[256,512]{1,0:T(8,128)(2,1)S(1)}, bf16[256,512]{1,0:T(8,128)(2,1)S(1)}, u32[]{:S(2)}, u32[]{:S(2)}) collective-permute-start(bf16[256,512]{1,0:T(8,128)(2,1)S(1)} %collective-permute-done.1.k_ref), channel_id=1, source_target_pairs={{0,1},{1,2},{2,3},{3,4},{4,5},{5,6},{6,7},{7,8},{8,9},{9,10},{10,1... | collective-permute-start | bytes 786440 | tf_op jit(solution)/shard_map/ppermute | solution.py:411
  40.6 14.0 %collective-permute-start.5 = (bf16[256,512]{1,0:T(8,128)(2,1)S(1)}, bf16[256,512]{1,0:T(8,128)(2,1)S(1)}, u32[]{:S(2)}, u32[]{:S(2)}) collective-permute-start(bf16[256,512]{1,0:T(8,128)(2,1)S(1)} %collective-permute-done.4.v_ref), channel_id=1, source_target_pairs={{0,1},{1,2},{2,3},{3,4},{4,5},{5,6},{6,7},{7,8},{8,9},{9,10},{10,1... | collective-permute-start | bytes 786440 | tf_op jit(solution)/shard_map/ppermute | solution.py:411
  48.9 11.0 %collective-permute-start.7 = (bf16[256,512]{1,0:T(8,128)(2,1)S(1)}, bf16[256,512]{1,0:T(8,128)(2,1)S(1)}, u32[]{:S(2)}, u32[]{:S(2)}) collective-permute-start(bf16[256,512]{1,0:T(8,128)(2,1)S(1)} %get-tuple-element.66), channel_id=1, source_target_pairs={{1,0},{2,1},{3,2},{4,3},{5,4},{6,5},{7,6},{8,7},{9,8},{10,9},{11,1... | collective-permute-start | bytes 786440 | tf_op jit(solution)/shard_map/ppermute | solution.py:411
  54.8 14.6 %collective-permute-start.6 = (bf16[256,512]{1,0:T(8,128)(2,1)S(1)}, bf16[256,512]{1,0:T(8,128)(2,1)S(1)}, u32[]{:S(2)}, u32[]{:S(2)}) collective-permute-start(bf16[256,512]{1,0:T(8,128)(2,1)S(1)} %get-tuple-element.69), channel_id=1, source_target_pairs={{1,0},{2,1},{3,2},{4,3},{5,4},{6,5},{7,6},{8,7},{9,8},{10,9},{11,1... | collective-permute-start | bytes 786440 | tf_op jit(solution)/shard_map/ppermute | solution.py:411
  60.0 15.7 %collective-permute-start.9 = (bf16[256,512]{1,0:T(8,128)(2,1)S(1)}, bf16[256,512]{1,0:T(8,128)(2,1)S(1)}, u32[]{:S(2)}, u32[]{:S(2)}) collective-permute-start(bf16[256,512]{1,0:T(8,128)(2,1)S(1)} %add_convert_fusion.5), channel_id=1, source_target_pairs={{1,0},{2,1},{3,2},{4,3},{5,4},{6,5},{7,6},{8,7},{9,8},{10,9},{11,1... | collective-permute-start | bytes 786440 | tf_op jit(solution)/shard_map/ppermute | solution.py:411
  69.5 16.0 %collective-permute-start.8 = (bf16[256,512]{1,0:T(8,128)(2,1)S(1)}, bf16[256,512]{1,0:T(8,128)(2,1)S(1)}, u32[]{:S(2)}, u32[]{:S(2)}) collective-permute-start(bf16[256,512]{1,0:T(8,128)(2,1)S(1)} %add_convert_fusion.4), channel_id=1, source_target_pairs={{1,0},{2,1},{3,2},{4,3},{5,4},{6,5},{7,6},{8,7},{9,8},{10,9},{11,1... | collective-permute-start | bytes 786440 | tf_op jit(solution)/shard_map/ppermute | solution.py:411
  75.8 17.8 %collective-permute-start.11 = (bf16[256,512]{1,0:T(8,128)(2,1)S(1)}, bf16[256,512]{1,0:T(8,128)(2,1)S(1)}, u32[]{:S(2)}, u32[]{:S(2)}) collective-permute-start(bf16[256,512]{1,0:T(8,128)(2,1)S(1)} %add_convert_fusion.3), channel_id=1, source_target_pairs={{1,0},{2,1},{3,2},{4,3},{5,4},{6,5},{7,6},{8,7},{9,8},{10,9},{11,1... | collective-permute-start | bytes 786440 | tf_op jit(solution)/shard_map/ppermute | solution.py:411
  85.5 5.1 %copy-start = (bf16[256,512]{1,0:T(8,128)(2,1)S(1)}, bf16[256,512]{1,0:T(8,128)(2,1)}, u32[]{:S(2)}) copy-start(bf16[256,512]{1,0:T(8,128)(2,1)} %k_ref.3) | copy-start | bytes 786436
  85.6 8.8 %collective-permute-start.10 = (bf16[256,512]{1,0:T(8,128)(2,1)S(1)}, bf16[256,512]{1,0:T(8,128)(2,1)S(1)}, u32[]{:S(2)}, u32[]{:S(2)}) collective-permute-start(bf16[256,512]{1,0:T(8,128)(2,1)S(1)} %add_convert_fusion.2), channel_id=1, source_target_pairs={{1,0},{2,1},{3,2},{4,3},{5,4},{6,5},{7,6},{8,7},{9,8},{10,9},{11,1... | collective-permute-start | bytes 786440 | tf_op jit(solution)/shard_map/ppermute | solution.py:411
